TPU v7x, 32 devices: a whole 2x2x4 slice. The times are simulated.
32 devices in a mesh: ctx: 8 (over z, x), tp: 4 (over y, core).
Axes of the slice: x: 2, y: 2, z: 4, core: 2. Of those that a mesh axis runs over, the one named last changes fastest.
Arguments:
- tokens: bfloat16 [1024, 4096], P('ctx', 'tp'), may hold values from -6 to 6
- routes: int32 [1024, 8], P('ctx'), may hold values from 0 to 127, all different within a row
- gates: float32 [1024, 8], P('ctx'), may hold values from 0.1 to 1
- w_gate: bfloat16 [8, 4096, 1536], P('ctx', None, 'tp'), may hold values from -0.09375 to 0.09375
- w_up: bfloat16 [8, 4096, 1536], P('ctx', None, 'tp'), may hold values from -0.09375 to 0.09375
- w_down: bfloat16 [8, 1536, 4096], P('ctx', 'tp'), may hold values from -0.15625 to 0.15625
- d_out: bfloat16 [1024, 4096], P('ctx', 'tp'), may hold values from -6 to 6
Outputs:
- mixed: bfloat16 [1024, 4096], P('ctx', 'tp')
- d_tokens: bfloat16 [1024, 4096], P('ctx', 'tp')
- d_gates: float32 [1024, 8], P('ctx')
- d_w_gate: bfloat16 [8, 4096, 1536], P('ctx', None, 'tp')
- d_w_up: bfloat16 [8, 4096, 1536], P('ctx', None, 'tp')
- d_w_down: bfloat16 [8, 1536, 4096], P('ctx', 'tp')
Inputs may be any that keep to these rules, and one draw needn't show every extreme that they name: `routes`: each row names 8 different experts of 128; pairs naming an expert of 8 or above are outside this window.
All inputs are finite; a program needn't handle non-finite values.
Results may differ from a plain program's by a relative error of at most 0.0063.
Values may be sent and summed in bfloat16 or wider, within the bound.
No kernel may reach another device: no remote copies, remote signals or barrier semaphores. Data moves between devices by JAX's collectives and lax.ppermute only.
A program may use at most 128 MiB of HBM per device.

v0:
```python
import jax
import jax.numpy as jnp
from jax import lax
from jax.sharding import PartitionSpec as P

CAP = 16


def expert_forward(xfull, wg, wu):
    act = jnp.dot(xfull, wg, preferred_element_type=jnp.float32)
    lin = jnp.dot(xfull, wu, preferred_element_type=jnp.float32)
    sig = jax.nn.sigmoid(act)
    hidden = (act * sig * lin).astype(jnp.bfloat16)
    return (act, lin, sig, hidden)


def expert_backward(xfull, dfull, act, lin, sig, hidden, wd):
    dhid = jnp.dot(dfull, wd.T, preferred_element_type=jnp.float32)
    grad_down = jnp.dot(hidden.T, dfull, preferred_element_type=jnp.float32).astype(jnp.bfloat16)
    dlin = (dhid * act * sig).astype(jnp.bfloat16)
    dact = (dhid * lin * sig * (1.0 + act * (1.0 - sig))).astype(jnp.bfloat16)
    grad_gate = jnp.dot(xfull.T, dact, preferred_element_type=jnp.float32).astype(jnp.bfloat16)
    grad_up = jnp.dot(xfull.T, dlin, preferred_element_type=jnp.float32).astype(jnp.bfloat16)
    return (grad_gate, grad_up, grad_down, dact, dlin)


def partial_inputs(dact, dlin, wg, wu):
    return jnp.dot(dact, wg.T, preferred_element_type=jnp.float32) + jnp.dot(
        dlin, wu.T, preferred_element_type=jnp.float32
    )


def on_device(tokens, routes, gates, w_gate, w_up, w_down, d_out):
    tok_rows, quarter = tokens.shape
    topk = routes.shape[1]
    sources = lax.axis_size("ctx")
    experts = sources * w_gate.shape[0]
    slots = experts * CAP
    flat = routes.reshape(-1)
    onehot = (flat[:, None] == jnp.arange(experts, dtype=jnp.int32)[None, :]).astype(jnp.int32)
    before = jnp.sum((jnp.cumsum(onehot, axis=0) - onehot) * onehot, axis=-1)
    keep = (flat < experts) & (before < CAP)
    target = flat * CAP + before
    placed = (
        (target[:, None] == jnp.arange(slots, dtype=jnp.int32)[None, :]) & keep[:, None]
    ).astype(jnp.float32)
    select = jnp.sum(placed.reshape(tok_rows, topk, slots), axis=1)
    weighted = jnp.sum((placed * gates.reshape(-1)[:, None]).reshape(tok_rows, topk, slots), axis=1)
    select_bf = select.astype(jnp.bfloat16)
    xslots = jnp.dot(select_bf.T, tokens, preferred_element_type=jnp.float32).astype(jnp.bfloat16)
    dslots = jnp.dot(weighted.T, d_out.astype(jnp.float32), precision=lax.Precision.HIGHEST).astype(
        jnp.bfloat16
    )
    xslots = xslots.reshape(experts, CAP, quarter)
    dslots = dslots.reshape(experts, CAP, quarter)
    wg = w_gate[0]
    wu = w_up[0]
    wd = w_down[0]
    rows = sources * CAP
    xrecv = lax.all_to_all(xslots, "ctx", split_axis=0, concat_axis=0, tiled=True)
    xfull = lax.all_gather(xrecv, "tp", axis=2, tiled=True).reshape(rows, -1)
    act, lin, sig, hidden = expert_forward(xfull, wg, wu)
    partial_out = jnp.dot(hidden, wd, preferred_element_type=jnp.float32)
    out_sum = lax.psum_scatter(partial_out, "tp", scatter_dimension=1, tiled=True)
    out_rows = out_sum.astype(jnp.bfloat16).reshape(sources, CAP, quarter)
    back_out = lax.all_to_all(out_rows, "ctx", split_axis=0, concat_axis=0, tiled=True)
    drecv = lax.all_to_all(dslots, "ctx", split_axis=0, concat_axis=0, tiled=True)
    dfull = lax.all_gather(drecv, "tp", axis=2, tiled=True).reshape(rows, -1)
    grad_gate, grad_up, grad_down, dact, dlin = expert_backward(
        xfull, dfull, act, lin, sig, hidden, wd
    )
    partial_dx = partial_inputs(dact, dlin, wg, wu)
    dx_sum = lax.psum_scatter(partial_dx, "tp", scatter_dimension=1, tiled=True)
    dx_rows = dx_sum.astype(jnp.bfloat16).reshape(sources, CAP, quarter)
    back_dx = lax.all_to_all(dx_rows, "ctx", split_axis=0, concat_axis=0, tiled=True)
    back_out = back_out.reshape(slots, quarter)
    back_dx = back_dx.reshape(slots, quarter)
    mixed = jnp.dot(weighted, back_out.astype(jnp.float32), precision=lax.Precision.HIGHEST).astype(
        jnp.bfloat16
    )
    d_tokens = jnp.dot(select_bf, back_dx, preferred_element_type=jnp.float32).astype(jnp.bfloat16)
    plain_dy = jnp.dot(select_bf.T, d_out, preferred_element_type=jnp.float32)
    slot_dots = jnp.sum(plain_dy * back_out.astype(jnp.float32), axis=1)
    pair_dots = jnp.dot(placed, slot_dots, precision=lax.Precision.HIGHEST)
    d_gates = lax.psum(pair_dots, "tp").reshape(tok_rows, topk)
    return (mixed, d_tokens, d_gates, grad_gate[None], grad_up[None], grad_down[None])


def solution(mesh):
    placed = (
        P("ctx", "tp"),
        P("ctx", None),
        P("ctx", None),
        P("ctx", None, "tp"),
        P("ctx", None, "tp"),
        P("ctx", "tp", None),
        P("ctx", "tp"),
    )
    return jax.shard_map(
        on_device,
        mesh=mesh,
        in_specs=placed,
        out_specs=(
            P("ctx", "tp"),
            P("ctx", "tp"),
            P("ctx", None),
            P("ctx", None, "tp"),
            P("ctx", None, "tp"),
            P("ctx", "tp", None),
        ),
        check_vma=False,
    )
```

profile of v0, /device:TPU:0, one launch (start us, length us, event | category | flops | bytes accessed | tf_op | source)
XLA Modules:
  0.0 174.5 jit_solution(5491479167264273635)
XLA Ops:
  8.4 2.3 %reduce-window.6 = s32[8,8,128]{2,1,0:T(8,128)S(1)} reduce-window(s32[8,8,128]{2,1,0:T(8,128)S(1)} %fusion.24, s32[]{:T(128)} %constant.4.clone.1), window={size=1x1x128 pad=0_0x0_0x127_0}, to_apply=%region_0.0 | reduce-window | flops 1040384 | bytes 65540 | tf_op jit(solution)/shard_map/reduce-window
  15.8 16.1 %all_to_all.20 = bf16[8,16,1024]{2,1,0:T(8,128)(2,1)} all-to-all(bf16[8,16,1024]{2,1,0:T(8,128)(2,1)S(1)} %bitcast.84), channel_id=1, replica_groups=mesh['ctx'=8,'tp'=4] {'ctx'}, dimensions={0} | all-to-all | bytes 524288 | tf_op jit(solution)/shard_map/all_to_all | solution.py:60
  31.9 1.4 convolution_convert_fusion.4
  33.3 12.1 %all_to_all.21 = bf16[8,16,1024]{2,1,0:T(8,128)(2,1)} all-to-all(bf16[8,16,1024]{2,1,0:T(8,128)(2,1)S(1)} %bitcast.85), channel_id=1, replica_groups=mesh['ctx'=8,'tp'=4] {'ctx'}, dimensions={0} | all-to-all | bytes 524288 | tf_op jit(solution)/shard_map/all_to_all | solution.py:67
  45.4 2.4 %all-gather.3.cloned.1.call-done = bf16[8,16,4096]{2,1,0:T(8,128)(2,1)} async-done(((bf16[8,16,1024]{2,1,0:T(8,128)(2,1)}), bf16[8,16,4096]{2,1,0:T(8,128)(2,1)}) %all-gather.3.cloned.1.call-update) | async-done | bytes 1048592 | tf_op jit(solution)/shard_map/all_gather | solution.py:61
  47.8 3.7 %fusion.8 = f32[128,384]{1,0:T(8,128)} fusion(bf16[128,4096]{1,0:T(8,128)(2,1)} %bitcast.76, bf16[1,4096,384]{2,1,0:T(8,128)(2,1)} %param.11), kind=kOutput, calls=%fused_computation.12 | convolution fusion | flops 402653184 | bytes 4390912 | tf_op jit(solution)/shard_map/dot_general | solution.py:11
  51.5 1.4 fusion.12
  52.9 13.2 %all-gather.5.cloned.1.call-done = bf16[8,16,4096]{2,1,0:T(8,128)(2,1)} async-done(((bf16[8,16,1024]{2,1,0:T(8,128)(2,1)}), bf16[8,16,4096]{2,1,0:T(8,128)(2,1)}) %all-gather.5.cloned.1.call-update) | async-done | bytes 1048592 | tf_op jit(solution)/shard_map/all_gather | solution.py:68
  66.1 2.4 %multiply_convert_fusion = (bf16[128,384]{1,0:T(8,128)(2,1)S(1)}, bf16[128,384]{1,0:T(8,128)(2,1)S(1)}, bf16[128,384]{1,0:T(8,128)(2,1)S(1)}) fusion(f32[128,384]{1,0:T(8,128)} %fusion.12, f32[128,384]{1,0:T(8,128)} %fusion.8, bf16[128,4096]{1,0:T(8,128)(2,1)} %bitcast.86, bf16[1,384,4096]{2,1,0:T(8,128)(2,1)S(1)} %copy-done), kind=kOutput, calls=%fused_computation.33 | convolution fusion | flops 403439616 | bytes 4882432 | tf_op jit(solution)/shard_map/dot_general | solution.py:18
  69.2 2.1 %fusion.5 = f32[128,4096]{1,0:T(8,128)} fusion(bf16[128,384]{1,0:T(8,128)(2,1)S(1)} %get-tuple-element.28, bf16[1,384,4096]{2,1,0:T(8,128)(2,1)S(1)} %copy-done), kind=kOutput, calls=%fused_computation.9 | convolution fusion | flops 402653184 | bytes 5341184 | tf_op jit(solution)/shard_map/dot_general | solution.py:63
  71.3 3.1 %fusion.10 = f32[128,4096]{1,0:T(8,128)S(1)} fusion(bf16[128,384]{1,0:T(8,128)(2,1)S(1)} %get-tuple-element.27, bf16[1,4096,384]{2,1,0:T(8,128)(2,1)} %param.10), kind=kOutput, calls=%fused_computation.14 | convolution fusion | flops 402653184 | bytes 5341184 | tf_op jit(solution)/shard_map/dot_general | solution.py:28
  74.5 2.4 %convolution_add_fusion = f32[128,4096]{1,0:T(8,128)} fusion(f32[128,4096]{1,0:T(8,128)S(1)} %fusion.10, bf16[128,384]{1,0:T(8,128)(2,1)S(1)} %get-tuple-element.26, bf16[1,4096,384]{2,1,0:T(8,128)(2,1)S(1)} %copy-done.3), kind=kOutput, calls=%fused_computation.6 | convolution fusion | flops 403177472 | bytes 7438336 | tf_op jit(solution)/shard_map/dot_general | solution.py:28
  77.0 25.9 %reduce-scatter.3.cloned.1.call-done = f32[128,1024]{1,0:T(8,128)} async-done(((f32[128,4096]{1,0:T(8,128)}), f32[128,1024]{1,0:T(8,128)}) %reduce-scatter.3.cloned.1.call-update) | async-done | bytes 524304 | tf_op jit(solution)/shard_map/reduce_scatter | solution.py:64
  102.9 1.8 %convert_element_type.61 = bf16[128,1024]{1,0:T(8,128)(2,1)} convert(f32[128,1024]{1,0:T(8,128)} %reduce-scatter.3.cloned.1.call-done) | non-fusion elementwise | flops 131072 | bytes 786432 | tf_op jit(solution)/shard_map/convert_element_type | solution.py:65
  104.6 5.5 %all-to-all-start.1 = ((bf16[8,16,1024]{2,1,0:T(8,128)(2,1)}), bf16[8,16,1024]{2,1,0:T(8,128)(2,1)S(1)}, u32[]{:S(2)}, u32[]{:S(2)}) async-start(bf16[8,16,1024]{2,1,0:T(8,128)(2,1)} %bitcast.82), calls=%async_computation.2 | async-start | bytes 524288 | tf_op jit(solution)/shard_map/all_to_all | solution.py:66
  110.2 4.2 %fusion.2 = bf16[1,384,4096]{2,1,0:T(8,128)(2,1)} fusion(bf16[128,384]{1,0:T(8,128)(2,1)} %copy-done.6, bf16[128,4096]{1,0:T(8,128)(2,1)} %bitcast.87), kind=kOutput, calls=%fused_computation.5 | convolution fusion | flops 404226048 | bytes 4292608 | tf_op jit(solution)/shard_map/dot_general | solution.py:19
  114.4 2.7 %fusion.1 = bf16[1,4096,384]{2,1,0:T(8,128)(2,1)} fusion(bf16[128,4096]{1,0:T(8,128)(2,1)S(1)} %bitcast.79, bf16[128,384]{1,0:T(8,128)(2,1)S(1)} %copy-done.8), kind=kOutput, calls=%fused_computation.4 | convolution fusion | flops 404226048 | bytes 4292608 | tf_op jit(solution)/shard_map/dot_general | solution.py:23
  117.1 20.3 %reduce-scatter.5.cloned.1.call-done = f32[128,1024]{1,0:T(8,128)} async-done(((f32[128,4096]{1,0:T(8,128)}), f32[128,1024]{1,0:T(8,128)}) %reduce-scatter.5.cloned.1.call-update) | async-done | bytes 524304 | tf_op jit(solution)/shard_map/reduce_scatter | solution.py:73
  137.4 1.8 %convert_element_type.66 = bf16[128,1024]{1,0:T(8,128)(2,1)} convert(f32[128,1024]{1,0:T(8,128)} %reduce-scatter.5.cloned.1.call-done) | non-fusion elementwise | flops 131072 | bytes 786432 | tf_op jit(solution)/shard_map/convert_element_type | solution.py:74
  139.2 5.5 %all-to-all-start.3 = ((bf16[8,16,1024]{2,1,0:T(8,128)(2,1)}), bf16[8,16,1024]{2,1,0:T(8,128)(2,1)}, u32[]{:S(2)}, u32[]{:S(2)}) async-start(bf16[8,16,1024]{2,1,0:T(8,128)(2,1)} %bitcast.83), calls=%async_computation.5 | async-start | bytes 524288 | tf_op jit(solution)/shard_map/all_to_all | solution.py:75
  144.7 3.9 %fusion = bf16[1,4096,384]{2,1,0:T(8,128)(2,1)} fusion(bf16[128,4096]{1,0:T(8,128)(2,1)} %bitcast.77, bf16[128,384]{1,0:T(8,128)(2,1)} %copy-done.9), kind=kOutput, calls=%fused_computation.3 | convolution fusion | flops 404226048 | bytes 4292608 | tf_op jit(solution)/shard_map/dot_general | solution.py:22
  150.1 3.7 %all-to-all-done.3 = bf16[8,16,1024]{2,1,0:T(8,128)(2,1)} async-done(((bf16[8,16,1024]{2,1,0:T(8,128)(2,1)}), bf16[8,16,1024]{2,1,0:T(8,128)(2,1)}, u32[]{:S(2)}, u32[]{:S(2)}) %all-to-all-start.3) | async-done | bytes 262176 | tf_op jit(solution)/shard_map/all_to_all | solution.py:75
  153.8 1.9 %convolution_convert_fusion.3 = bf16[128,1024]{1,0:T(8,128)(2,1)} fusion(bf16[128,1024]{1,0:T(8,128)(2,1)} %bitcast.11, bf16[128,128]{1,0:T(8,128)(2,1)S(1)} %get-tuple-element.24), kind=kOutput, calls=%fused_computation.19 | convolution fusion | flops 33685504 | bytes 557056 | tf_op jit(solution)/shard_map/dot_general | solution.py:81
  156.3 11.0 %psum.7 = f32[128,8]{1,0:T(8,128)S(1)} all-reduce(f32[128,8]{1,0:T(8,128)S(1)} %reshape.119), channel_id=1, replica_groups=mesh['ctx'=8,'tp'=4] {'tp'}, use_global_device_ids=true, to_apply=%region_8.9 | all-reduce | flops 1024 | bytes 8192 | tf_op jit(solution)/shard_map/psum | solution.py:85
  (53 shorter events, 9.9 us)
Async XLA Ops:
  7.2 58.9 %copy-start = (bf16[1,384,4096]{2,1,0:T(8,128)(2,1)S(1)}, bf16[1,384,4096]{2,1,0:T(8,128)(2,1)}, u32[]{:S(2)}) copy-start(bf16[1,384,4096]{2,1,0:T(8,128)(2,1)} %param.12) | copy-start | bytes 9437188
  7.2 40.6 %all-gather.3.cloned.1.call-start = ((), (), s32[]{:S(2)}) async-start(), calls=%async_computation.6 | async-start | bytes 1310720 | tf_op jit(solution)/shard_map/all_gather | solution.py:61
  31.9 34.2 %all-gather.5.cloned.1.call-start = ((), (), s32[]{:S(2)}) async-start(), calls=%async_computation.8 | async-start | bytes 1310720 | tf_op jit(solution)/shard_map/all_gather | solution.py:68
  45.4 57.5 %reduce-scatter.3.cloned.1.call-start = ((), (), s32[]{:S(2)}) async-start(), calls=%async_computation.7 | async-start | bytes 2621440 | tf_op jit(solution)/shard_map/reduce_scatter | solution.py:64
  47.8 3.8 %copy-start.1 = (bf16[8,16,4096]{2,1,0:T(8,128)(2,1)S(1)}, bf16[8,16,4096]{2,1,0:T(8,128)(2,1)}, u32[]{:S(2)}) copy-start(bf16[8,16,4096]{2,1,0:T(8,128)(2,1)} %all-gather.3.cloned.1.call-done) | copy-start | bytes 3145732
  47.8 3.8 %copy-start.4 = (bf16[1,4096,384]{2,1,0:T(8,128)(2,1)S(1)}, bf16[1,4096,384]{2,1,0:T(8,128)(2,1)}, u32[]{:S(2)}) copy-start(bf16[1,4096,384]{2,1,0:T(8,128)(2,1)} %param.10) | copy-start | bytes 9437188
  68.5 0.6 copy-start.6
  68.6 2.8 %copy-start.9 = (bf16[128,384]{1,0:T(8,128)(2,1)}, bf16[128,384]{1,0:T(8,128)(2,1)S(1)}, u32[]{:S(2)}) copy-start(bf16[128,384]{1,0:T(8,128)(2,1)S(1)} %get-tuple-element.27) | copy-start | bytes 294916
  68.6 5.9 %copy-start.7 = (bf16[128,384]{1,0:T(8,128)(2,1)}, bf16[128,384]{1,0:T(8,128)(2,1)S(1)}, u32[]{:S(2)}) copy-start(bf16[128,384]{1,0:T(8,128)(2,1)S(1)} %get-tuple-element.26) | copy-start | bytes 294916
  71.3 66.2 %reduce-scatter.5.cloned.1.call-start = ((), (), s32[]{:S(2)}) async-start(), calls=%async_computation.9 | async-start | bytes 2621440 | tf_op jit(solution)/shard_map/reduce_scatter | solution.py:73
  71.3 3.2 %copy-start.3 = (bf16[1,4096,384]{2,1,0:T(8,128)(2,1)S(1)}, bf16[1,4096,384]{2,1,0:T(8,128)(2,1)}, u32[]{:S(2)}) copy-start(bf16[1,4096,384]{2,1,0:T(8,128)(2,1)} %param.11) | copy-start | bytes 9437188
  104.6 34.6 %all-to-all-start.1 = ((bf16[8,16,1024]{2,1,0:T(8,128)(2,1)}), bf16[8,16,1024]{2,1,0:T(8,128)(2,1)S(1)}, u32[]{:S(2)}, u32[]{:S(2)}) async-start(bf16[8,16,1024]{2,1,0:T(8,128)(2,1)} %bitcast.82), calls=%async_computation.2 | async-start | bytes 524288 | tf_op jit(solution)/shard_map/all_to_all | solution.py:66
  110.1 4.3 %copy-start.2 = (bf16[8,16,4096]{2,1,0:T(8,128)(2,1)S(1)}, bf16[8,16,4096]{2,1,0:T(8,128)(2,1)}, u32[]{:S(2)}) copy-start(bf16[8,16,4096]{2,1,0:T(8,128)(2,1)} %all-gather.3.cloned.1.call-done) | copy-start | bytes 3145732
  110.2 4.3 %copy-start.8 = (bf16[128,384]{1,0:T(8,128)(2,1)S(1)}, bf16[128,384]{1,0:T(8,128)(2,1)}, u32[]{:S(2)}) copy-start(bf16[128,384]{1,0:T(8,128)(2,1)} %copy-done.7) | copy-start | bytes 294916
  139.2 14.5 %all-to-all-start.3 = ((bf16[8,16,1024]{2,1,0:T(8,128)(2,1)}), bf16[8,16,1024]{2,1,0:T(8,128)(2,1)}, u32[]{:S(2)}, u32[]{:S(2)}) async-start(bf16[8,16,1024]{2,1,0:T(8,128)(2,1)} %bitcast.83), calls=%async_computation.5 | async-start | bytes 524288 | tf_op jit(solution)/shard_map/all_to_all | solution.py:75
  144.7 4.0 %copy-start.5 = (bf16[128,1024]{1,0:T(8,128)(2,1)S(1)}, bf16[128,1024]{1,0:T(8,128)(2,1)}, u32[]{:S(2)}) copy-start(bf16[128,1024]{1,0:T(8,128)(2,1)} %param.13) | copy-start | bytes 786436
Sparse Core Ops, SparseCore 0:
  32.0 15.7 all-gather.2
  49.3 16.7 all-gather.4
  71.4 31.4 reduce-scatter.2
  106.0 31.4 reduce-scatter.4
where the time goes:
time: 175 us; the launch traced here: 174 us
  waiting for transfers between devices  65.5 us (37%)
  blocking collectives  39.1 us (22%)
  matrix products  32.5 us (19%)
  between operations  13.9 us (8%)
  starting transfers between devices  11.2 us (6%)
  other arithmetic  8.35 us (5%)
  local copies, waits for them, and re-layouts  3.96 us (2%)
    reduce_scatter x1, waiting for transfers between devices, on_device(): lax.psum_scatter(partial_out, 'tp', scatter_dimension=1, tiled=True)  25.9 us
    reduce_scatter x1, waiting for transfers between devices, on_device(): dx_sum = lax.psum_scatter(partial_dx, 'tp', scatter_dimension=1, tiled=True)  20.3 us
    all_to_all x1, blocking collectives, on_device(): lax.all_to_all(xslots, 'ctx', split_axis=0, concat_axis=0, tiled=True)  16.1 us
    all_gather x1, waiting for transfers between devices, on_device(): dfull = lax.all_gather(drecv, 'tp', axis=2, tiled=True).reshape(rows, -1)  13.2 us
    all_to_all x1, blocking collectives, on_device(): lax.all_to_all(dslots, 'ctx', split_axis=0, concat_axis=0, tiled=True)  12.1 us
    psum x1, blocking collectives, on_device(): d_gates = lax.psum(pair_dots, 'tp').reshape(tok_rows, topk)  11 us
    all_to_all x1, starting transfers between devices, on_device(): lax.all_to_all(out_rows, 'ctx', split_axis=0, concat_axis=0, tiled=True)  5.51 us
    all_to_all x1, starting transfers between devices, on_device(): lax.all_to_all(dx_rows, 'ctx', split_axis=0, concat_axis=0, tiled=True)  5.49 us
  transfers between devices with their start and end apart: 6, of which 5 were waited for; matrix products, arithmetic and copies ran while one was open for 16% of the time, Pallas kernels for 0%

commit v1 on v0

v1 whole, which is shorter than its diff:
```python
import jax
import jax.numpy as jnp
from jax import lax
from jax.experimental import pallas as pl
from jax.experimental.pallas import tpu as pltpu
from jax.sharding import PartitionSpec as P

CAP = 16
F32 = jnp.float32
BF16 = jnp.bfloat16
VMEM_BYTES = 40 * 1024 * 1024
NN = (((1,), (0,)), ((), ()))
NT = (((1,), (1,)), ((), ()))
TN = (((0,), (0,)), ((), ()))


def dot(a, b, dims=NN):
    return lax.dot_general(a, b, dims, preferred_element_type=F32)


def params():
    return pltpu.CompilerParams(vmem_limit_bytes=VMEM_BYTES)


def cost(flops, nbytes):
    return pl.CostEstimate(flops=flops, bytes_accessed=nbytes, transcendentals=0)


def vspec():
    return pl.BlockSpec(memory_space=pltpu.VMEM)


def aspec():
    return pl.BlockSpec(memory_space=pl.ANY)


def dispatch_kernel(routes, gates, tokens, d_out, xs, ds, sel, pick, w_hi, w_lo):
    experts, cap, quarter = xs.shape
    topk, tok = routes.shape
    slots = experts * cap
    r = routes[...]
    match = r[None] == lax.broadcasted_iota(jnp.int32, (experts, topk, tok), 0)
    hit = jnp.sum(jnp.where(match, 1.0, 0.0), axis=1)
    gate = jnp.sum(jnp.where(match, gates[...][None], 0.0), axis=1)
    earlier = lax.broadcasted_iota(jnp.int32, (tok, tok), 0) < lax.broadcasted_iota(
        jnp.int32, (tok, tok), 1
    )
    before = dot(hit.astype(BF16), jnp.where(earlier, 1.0, 0.0).astype(BF16))
    place = jnp.where(hit > 0.0, before, -1.0)[:, None, :]
    row = lax.broadcasted_iota(jnp.int32, (experts, cap, tok), 1).astype(F32)
    chosen = jnp.where(place == row, 1.0, 0.0)
    weight = (chosen * gate[:, None, :]).reshape(slots, tok)
    chosen = chosen.reshape(slots, tok)
    select = chosen.astype(BF16)
    xs[...] = dot(select, tokens[...]).astype(BF16).reshape(experts, cap, quarter)
    slot_gate = jnp.sum(weight, axis=1, keepdims=True)
    ds[...] = (slot_gate * dot(select, d_out[...])).astype(BF16).reshape(experts, cap, quarter)
    sel[...] = select
    pick[...] = chosen.T.astype(BF16)
    back = weight.T
    high = back.astype(BF16)
    w_hi[...] = high
    w_lo[...] = (back - high.astype(F32)).astype(BF16)


def dispatch(routes_t, gates_t, tokens, d_out, experts):
    tok, quarter = tokens.shape
    slots = experts * CAP
    return pl.pallas_call(
        dispatch_kernel,
        out_shape=(
            jax.ShapeDtypeStruct((experts, CAP, quarter), BF16),
            jax.ShapeDtypeStruct((experts, CAP, quarter), BF16),
            jax.ShapeDtypeStruct((slots, tok), BF16),
            jax.ShapeDtypeStruct((tok, slots), BF16),
            jax.ShapeDtypeStruct((tok, slots), BF16),
            jax.ShapeDtypeStruct((tok, slots), BF16),
        ),
        in_specs=[vspec()] * 4,
        out_specs=(vspec(),) * 6,
        compiler_params=params(),
        cost_estimate=cost(4 * slots * tok * quarter, 8 * tok * quarter),
        name="dispatch",
    )(routes_t, gates_t, tokens, d_out)


ORDER = (0, 1, 2, 3)


def quarter_of(me, flip, size):
    return pl.ds(pl.multiple_of((me ^ flip) * size, size), size)


def fetch(src, dst, sem, part):
    copy = pltpu.make_async_copy(src.at[part], dst.at[part], sem)
    copy.start()
    return copy


def forward_kernel(
    x0, x1, x2, x3, wg, wu, wd, act, lin, hidden, send, keep, vg, vu, vd, sem
):
    me = lax.axis_index("tp")
    size = x0.shape[1]
    xs = (x0, x1, x2, x3)
    loads = []
    for i in ORDER:
        part = (quarter_of(me, i, size), slice(None))
        loads.append((fetch(wg, vg, sem.at[0, i], part), fetch(wu, vu, sem.at[1, i], part)))
    tail = [
        fetch(wd, vd, sem.at[2, i], (slice(None), quarter_of(me, i, size))) for i in (3, 1, 2, 0)
    ]
    a = b = None
    for i in ORDER:
        part = quarter_of(me, i, size)
        x = xs[i][...]
        loads[i][0].wait()
        pa = dot(x, vg[part, :])
        loads[i][1].wait()
        pb = dot(x, vu[part, :])
        a = pa if a is None else a + pa
        b = pb if b is None else b + pb
    act[...] = a
    lin[...] = b
    h = (a * jax.nn.sigmoid(a) * b).astype(BF16)
    hidden[...] = h
    for n, i in enumerate((3, 1, 2, 0)):
        tail[n].wait()
        p = dot(h, vd[:, quarter_of(me, i, size)])
        if n < 2:
            send[n] = p.astype(BF16)
        else:
            keep[n - 2] = p


def forward(xs, wg, wu, wd):
    rows, size = xs[0].shape
    d, ff = wg.shape
    return pl.pallas_call(
        forward_kernel,
        out_shape=(
            jax.ShapeDtypeStruct((rows, ff), F32),
            jax.ShapeDtypeStruct((rows, ff), F32),
            jax.ShapeDtypeStruct((rows, ff), BF16),
            jax.ShapeDtypeStruct((2, rows, size), BF16),
            jax.ShapeDtypeStruct((2, rows, size), F32),
        ),
        in_specs=[vspec()] * 4 + [aspec()] * 3,
        out_specs=(vspec(),) * 5,
        scratch_shapes=[
            pltpu.VMEM((d, ff), BF16),
            pltpu.VMEM((d, ff), BF16),
            pltpu.VMEM((ff, d), BF16),
            pltpu.SemaphoreType.DMA((3, 4)),
        ],
        compiler_params=params(),
        cost_estimate=cost(6 * rows * d * ff, 6 * d * ff + 6 * rows * d),
        name="forward",
    )(*xs, wg, wu, wd)


def backward_kernel(
    d0, d1, d2, d3, act, lin, wg, wu, wd, dact, dlin, send, keep, vg, vu, vd, sem
):
    me = lax.axis_index("tp")
    size = d0.shape[1]
    ds = (d0, d1, d2, d3)
    head = [
        fetch(wd, vd, sem.at[2, i], (slice(None), quarter_of(me, i, size))) for i in ORDER
    ]
    loads = []
    for i in (3, 1, 2, 0):
        part = (quarter_of(me, i, size), slice(None))
        loads.append((fetch(wg, vg, sem.at[0, i], part), fetch(wu, vu, sem.at[1, i], part)))
    dhid = None
    for i in ORDER:
        head[i].wait()
        p = dot(ds[i][...], vd[:, quarter_of(me, i, size)], NT)
        dhid = p if dhid is None else dhid + p
    a = act[...]
    s = jax.nn.sigmoid(a)
    dl = (dhid * (a * s)).astype(BF16)
    da = (dhid * lin[...] * s * (1.0 + a * (1.0 - s))).astype(BF16)
    dlin[...] = dl
    dact[...] = da
    for n, i in enumerate((3, 1, 2, 0)):
        part = quarter_of(me, i, size)
        loads[n][0].wait()
        loads[n][1].wait()
        p = dot(da, vg[part, :], NT) + dot(dl, vu[part, :], NT)
        if n < 2:
            send[n] = p.astype(BF16)
        else:
            keep[n - 2] = p


def backward(ds, act, lin, wg, wu, wd):
    rows, size = ds[0].shape
    d, ff = wg.shape
    return pl.pallas_call(
        backward_kernel,
        out_shape=(
            jax.ShapeDtypeStruct((rows, ff), BF16),
            jax.ShapeDtypeStruct((rows, ff), BF16),
            jax.ShapeDtypeStruct((2, rows, size), BF16),
            jax.ShapeDtypeStruct((2, rows, size), F32),
        ),
        in_specs=[vspec()] * 6 + [aspec()] * 3,
        out_specs=(vspec(),) * 4,
        scratch_shapes=[
            pltpu.VMEM((d, ff), BF16),
            pltpu.VMEM((d, ff), BF16),
            pltpu.VMEM((ff, d), BF16),
            pltpu.SemaphoreType.DMA((3, 4)),
        ],
        compiler_params=params(),
        cost_estimate=cost(6 * rows * d * ff, 6 * d * ff + 6 * rows * d),
        name="backward",
    )(*ds, act, lin, wg, wu, wd)


def grads_kernel(
    x0, x1, x2, x3, d0, d1, d2, d3, hidden, dact, dlin, gg, gu, gd, vg, vu, vd, sem
):
    me = lax.axis_index("tp")
    size = x0.shape[1]
    xs, ds = (x0, x1, x2, x3), (d0, d1, d2, d3)
    h = hidden[...]
    da = dact[...]
    dl = dlin[...]
    stores = []
    for i in ORDER:
        part = quarter_of(me, i, size)
        rows = (part, slice(None))
        cols = (slice(None), part)
        x = xs[i][...]
        vg[part, :] = dot(x, da, TN).astype(BF16)
        stores.append(fetch(vg, gg, sem.at[0, i], rows))
        vu[part, :] = dot(x, dl, TN).astype(BF16)
        stores.append(fetch(vu, gu, sem.at[1, i], rows))
        vd[:, part] = dot(h, ds[i][...], TN).astype(BF16)
        stores.append(fetch(vd, gd, sem.at[2, i], cols))
    for store in stores:
        store.wait()


def grads(xs, ds, hidden, dact, dlin):
    rows, size = xs[0].shape
    ff = hidden.shape[1]
    d = 4 * size
    return pl.pallas_call(
        grads_kernel,
        out_shape=(
            jax.ShapeDtypeStruct((d, ff), BF16),
            jax.ShapeDtypeStruct((d, ff), BF16),
            jax.ShapeDtypeStruct((ff, d), BF16),
        ),
        in_specs=[vspec()] * 11,
        out_specs=(aspec(),) * 3,
        scratch_shapes=[
            pltpu.VMEM((d, ff), BF16),
            pltpu.VMEM((d, ff), BF16),
            pltpu.VMEM((ff, d), BF16),
            pltpu.SemaphoreType.DMA((3, 4)),
        ],
        compiler_params=params(),
        cost_estimate=cost(6 * rows * d * ff, 6 * d * ff + 4 * rows * d),
        name="grads",
    )(*xs, *ds, hidden, dact, dlin)


def mix_kernel(back, w_hi, w_lo, sel, d_out, routes, mixed, dots):
    slots, tok = sel.shape
    topk = routes.shape[0]
    experts = slots // CAP
    o = back[...]
    mixed[...] = (dot(w_hi[...], o) + dot(w_lo[...], o)).astype(BF16)
    select = sel[...]
    per_slot = jnp.sum(dot(select, d_out[...]) * o.astype(F32), axis=1, keepdims=True)
    spread = select.astype(F32) * per_slot
    per_expert = jnp.sum(spread.reshape(experts, CAP, tok), axis=1)
    match = routes[...][None] == lax.broadcasted_iota(jnp.int32, (experts, topk, tok), 0)
    dots[...] = jnp.sum(jnp.where(match, per_expert[:, None, :], 0.0), axis=0)


def mix(back, w_hi, w_lo, sel, d_out, routes_t):
    slots, quarter = back.shape
    topk, tok = routes_t.shape
    return pl.pallas_call(
        mix_kernel,
        out_shape=(
            jax.ShapeDtypeStruct((tok, quarter), BF16),
            jax.ShapeDtypeStruct((topk, tok), F32),
        ),
        in_specs=[vspec()] * 6,
        out_specs=(vspec(),) * 2,
        compiler_params=params(),
        cost_estimate=cost(6 * slots * tok * quarter, 6 * tok * quarter),
        name="mix",
    )(back, w_hi, w_lo, sel, d_out, routes_t)


def collect_kernel(back, pick, d_tokens):
    d_tokens[...] = dot(pick[...], back[...]).astype(BF16)


def collect(back, pick):
    slots, quarter = back.shape
    tok = pick.shape[0]
    return pl.pallas_call(
        collect_kernel,
        out_shape=jax.ShapeDtypeStruct((tok, quarter), BF16),
        in_specs=[vspec()] * 2,
        out_specs=vspec(),
        compiler_params=params(),
        cost_estimate=cost(2 * slots * tok * quarter, 4 * tok * quarter),
        name="collect",
    )(back, pick)


def swap(x, flip):
    return lax.ppermute(x, "tp", [(i, i ^ flip) for i in range(4)])


def exchange(x):
    return lax.all_to_all(x, "ctx", split_axis=0, concat_axis=0, tiled=True)


def gather(own):
    near = swap(own, 1)
    far = swap(own, 2)
    return (own, near, far, swap(far, 1))


def scatter_sum(send, keep):
    got = swap(send, 1)
    across = swap((keep[0] + got[0].astype(F32)).astype(BF16), 2)
    return (keep[1] + got[1].astype(F32) + across.astype(F32)).astype(BF16)


def on_device(tokens, routes, gates, w_gate, w_up, w_down, d_out):
    tok, quarter = tokens.shape
    sources = lax.axis_size("ctx")
    experts = sources * w_gate.shape[0]
    slots = experts * CAP
    rows = sources * CAP
    wg, wu, wd = w_gate[0], w_up[0], w_down[0]
    routes_t = routes.T
    xs, ds, sel, pick, w_hi, w_lo = dispatch(routes_t, gates.T, tokens, d_out, experts)
    xq = gather(exchange(xs).reshape(rows, quarter))
    dq = gather(exchange(ds).reshape(rows, quarter))
    act, lin, hidden, send_out, keep_out = forward(xq, wg, wu, wd)
    dact, dlin, send_dx, keep_dx = backward(dq, act, lin, wg, wu, wd)
    out_rows = scatter_sum(send_out, keep_out)
    back_out = exchange(out_rows.reshape(sources, CAP, quarter)).reshape(slots, quarter)
    dx_rows = scatter_sum(send_dx, keep_dx)
    back_dx = exchange(dx_rows.reshape(sources, CAP, quarter)).reshape(slots, quarter)
    grad_gate, grad_up, grad_down = grads(xq, dq, hidden, dact, dlin)
    mixed, dots = mix(back_out, w_hi, w_lo, sel, d_out, routes_t)
    dots = dots + swap(dots, 1)
    dots = dots + swap(dots, 2)
    d_tokens = collect(back_dx, pick)
    return (mixed, d_tokens, dots.T, grad_gate[None], grad_up[None], grad_down[None])


def solution(mesh):
    placed = (
        P("ctx", "tp"),
        P("ctx", None),
        P("ctx", None),
        P("ctx", None, "tp"),
        P("ctx", None, "tp"),
        P("ctx", "tp", None),
        P("ctx", "tp"),
    )
    return jax.shard_map(
        on_device,
        mesh=mesh,
        in_specs=placed,
        out_specs=(
            P("ctx", "tp"),
            P("ctx", "tp"),
            P("ctx", None),
            P("ctx", None, "tp"),
            P("ctx", None, "tp"),
            P("ctx", "tp", None),
        ),
        check_vma=False,
    )
```

time: 175 us -> 101 us (0.58)
  waiting for transfers between devices: 65.5 us -> 26.1 us
  matrix products: 32.5 us -> 0 us
  blocking collectives: 39.1 us -> 15.9 us
  Pallas kernels: 0 us -> 17.2 us
  between operations: 13.9 us -> 0.89 us
  local copies, waits for them, and re-layouts: 3.96 us -> 16.7 us
  starting transfers between devices: 11.2 us -> 20.8 us
  other arithmetic: 8.35 us -> 2.3 us
    reduce_scatter x2 -> x0, waiting for transfers between devices: 46.2 us -> none  [the longest x1 25.9 us: on_device(): lax.psum_scatter(partial_out, 'tp', scatter_dimension=1, tiled=True)]
    dot_general x15 -> x0, matrix products: 32.5 us -> none  [the longest x1 4.23 us: expert_backward(): jnp.dot(hidden.T, dfull, preferred_element_type=jnp.float32)]
    pallas_call x0 -> x6, Pallas kernels: none -> 17.2 us  [the longest x1 5.58 us: backward(): pl.pallas_call(backward_kernel, out_shape=(jax.ShapeDtypeStruct((rows, ff...]
    all_gather x2 -> x0, waiting for transfers between devices: 15.5 us -> none  [the longest x1 13.2 us: on_device(): dfull = lax.all_gather(drecv, 'tp', axis=2, tiled=True).reshape(rows, -1)]
    unnamed x23 -> x56, local copies, waits for them, and re-layouts: 3.04 us -> 16.7 us
    all_to_all x2 -> x1, blocking collectives: 28.1 us -> 15.9 us  [exchange(): return lax.all_to_all(x, 'ctx', split_axis=0, concat_axis=0, tiled=True)]
    ppermute x0 -> x12, waiting for transfers between devices: none -> 11.4 us  [swap(): return lax.ppermute(x, 'tp', [(i, i ^ flip) for i in range(4)])]
    all_to_all x2 -> x3, waiting for transfers between devices: 3.67 us -> 14.7 us  [exchange(): return lax.all_to_all(x, 'ctx', split_axis=0, concat_axis=0, tiled=True)]
  transfers between devices with their start and end apart: 6 -> 15, of which waited for: 5 -> 6; matrix products, arithmetic and copies ran while one was open for 16% -> 2% of each run, Pallas kernels for 0% -> 16%
where the time goes in v1:
time: 101 us; the launch traced here: 99.9 us
  waiting for transfers between devices  26.1 us (26%)
  starting transfers between devices  20.8 us (21%)
  Pallas kernels  17.2 us (17%)
  local copies, waits for them, and re-layouts  16.7 us (17%)
  blocking collectives  15.9 us (16%)
  other arithmetic  2.3 us (2%)
    unnamed x56, local copies, waits for them, and re-layouts  16.7 us
    all_to_all x1, blocking collectives, exchange(): return lax.all_to_all(x, 'ctx', split_axis=0, concat_axis=0, tiled=True)  15.9 us
    all_to_all x3, waiting for transfers between devices, exchange(): return lax.all_to_all(x, 'ctx', split_axis=0, concat_axis=0, tiled=True)  14.7 us
    all_to_all x3, starting transfers between devices, exchange(): return lax.all_to_all(x, 'ctx', split_axis=0, concat_axis=0, tiled=True)  11.8 us
    ppermute x12, waiting for transfers between devices, swap(): return lax.ppermute(x, 'tp', [(i, i ^ flip) for i in range(4)])  11.4 us
    ppermute x12, starting transfers between devices, swap(): return lax.ppermute(x, 'tp', [(i, i ^ flip) for i in range(4)])  8.94 us
    pallas_call x1, Pallas kernels, backward(): pl.pallas_call(backward_kernel, out_shape=(jax.ShapeDtypeStruct((rows, ff...  5.58 us
    pallas_call x1, Pallas kernels, forward(): pl.pallas_call(forward_kernel, out_shape=(jax.ShapeDtypeStruct((rows, ff)...  4.31 us
  transfers between devices with their start and end apart: 15, of which 6 were waited for; matrix products, arithmetic and copies ran while one was open for 2% of the time, Pallas kernels for 16%

profile of v1, /device:TPU:0, one launch (start us, length us, event | category | flops | bytes accessed | tf_op | source)
XLA Modules:
  0.0 99.9 jit_solution(17742173954618778936)
XLA Ops:
  1.6 0.9 copy-done.18
  3.9 1.1 %dispatch.1 = (bf16[8,16,1024]{2,1,0:T(8,128)(2,1)S(1)}, bf16[8,16,1024]{2,1,0:T(8,128)(2,1)}, bf16[128,128]{1,0:T(8,128)(2,1)S(1)}, bf16[128,128]{1,0:T(8,128)(...) custom-call(s32[8,128]{1,0:T(8,128)S(1)} %bitcast.44, f32[8,128]{1,0:T(8,128)S(1)} %bitcast.46, ...), custom_call_target="tpu_custom_call" | custom-call | flops 67108864 | bytes 1048576 | tf_op jit(solution)/shard_map/dispatch/pallas_call | solution.py:69
  5.1 15.9 %all_to_all.20 = bf16[8,16,1024]{2,1,0:T(8,128)(2,1)S(1)} all-to-all(bf16[8,16,1024]{2,1,0:T(8,128)(2,1)S(1)} %get-tuple-element.26), channel_id=1, replica_groups=mesh['ctx'=8,'tp'=4] {'ctx'}, dimensions={0} | all-to-all | bytes 524288 | tf_op jit(solution)/shard_map/all_to_all | solution.py:326
  21.0 3.6 %all-to-all-start.2 = ((bf16[8,16,1024]{2,1,0:T(8,128)(2,1)}), bf16[8,16,1024]{2,1,0:T(8,128)(2,1)S(1)}, u32[]{:S(2)}, u32[]{:S(2)}) async-start(bf16[8,16,1024]{2,1,0:T(8,128)(2,1)} %get-tuple-element.33), calls=%async_computation.2 | async-start | bytes 524288 | tf_op jit(solution)/shard_map/all_to_all | solution.py:326
  24.6 1.5 %collective-permute-start.1 = (bf16[128,1024]{1,0:T(8,128)(2,1)S(1)}, bf16[128,1024]{1,0:T(8,128)(2,1)S(1)}, u32[]{:S(2)}, u32[]{:S(2)}) collective-permute-start(bf16[128,1024]{1,0:T(8,128)(2,1)S(1)} %bitcast.34), channel_id=1, source_target_pairs={{0,2},{1,3},{2,0},{3,1},{4,6},{5,7},{6,4},{7,5},{8,10},{9,11},{10,... | collective-permute-start | bytes 786440 | tf_op jit(solution)/shard_map/ppermute | solution.py:322
  26.1 7.0 %all-to-all-done.2 = bf16[8,16,1024]{2,1,0:T(8,128)(2,1)S(1)} async-done(((bf16[8,16,1024]{2,1,0:T(8,128)(2,1)}), bf16[8,16,1024]{2,1,0:T(8,128)(2,1)S(1)}, u32[]{:S(2)}, u32[]{:S(2)}) %all-to-all-start.2) | async-done | bytes 262176 | tf_op jit(solution)/shard_map/all_to_all | solution.py:326
  33.1 1.5 %collective-permute-start.6 = (bf16[128,1024]{1,0:T(8,128)(2,1)S(1)}, bf16[128,1024]{1,0:T(8,128)(2,1)S(1)}, u32[]{:S(2)}, u32[]{:S(2)}) collective-permute-start(bf16[128,1024]{1,0:T(8,128)(2,1)S(1)} %bitcast.38), channel_id=1, source_target_pairs={{0,2},{1,3},{2,0},{3,1},{4,6},{5,7},{6,4},{7,5},{8,10},{9,11},{10,... | collective-permute-start | bytes 786440 | tf_op jit(solution)/shard_map/ppermute | solution.py:322
  35.2 4.3 %collective-permute-done.6.d2 = bf16[128,1024]{1,0:T(8,128)(2,1)S(1)} collective-permute-done((bf16[128,1024]{1,0:T(8,128)(2,1)S(1)}, bf16[128,1024]{1,0:T(8,128)(2,1)S(1)}, u32[]{:S(2)}, u32[]{:S(2)}) %collective-permute-start.6) | collective-permute-done | bytes 262176 | tf_op jit(solution)/shard_map/ppermute | solution.py:322
  39.6 2.1 %copy-done = bf16[1,4096,384]{2,1,0:T(8,128)(2,1)S(1)} copy-done((bf16[1,4096,384]{2,1,0:T(8,128)(2,1)S(1)}, bf16[1,4096,384]{2,1,0:T(8,128)(2,1)}, u32[]{:S(2)}) %copy-start) | copy-done | bytes 3145752
  41.7 1.9 %copy-done.2 = bf16[1,4096,384]{2,1,0:T(8,128)(2,1)S(1)} copy-done((bf16[1,4096,384]{2,1,0:T(8,128)(2,1)S(1)}, bf16[1,4096,384]{2,1,0:T(8,128)(2,1)}, u32[]{:S(2)}) %copy-start.2) | copy-done | bytes 3145752
  43.6 1.9 %copy-done.4 = bf16[1,384,4096]{2,1,0:T(8,128)(2,1)S(1)} copy-done((bf16[1,384,4096]{2,1,0:T(8,128)(2,1)S(1)}, bf16[1,384,4096]{2,1,0:T(8,128)(2,1)}, u32[]{:S(2)}) %copy-start.4) | copy-done | bytes 3145752
  45.5 4.3 %forward.1 = (f32[128,384]{1,0:T(8,128)S(1)}, f32[128,384]{1,0:T(8,128)S(1)}, bf16[128,384]{1,0:T(8,128)(2,1)S(1)}, bf16[2,128,1024]{2,1,0:T(8,128)(2,1)S(1)}, f32[2,128,1024]{2,1,0:T(8,128)S(1)}) custom-call(bf16[128,1024]{1,0:T(8,128)(2,1)S(1)} %bitcast.36, bf16[128,1024]{1,0:T(8,128)(2,1)S(1)} %collective-permute-done.x1, ...), custom_call_target="tpu_custom_call" | custom-call | flops 1207959552 | bytes 12582912 | tf_op jit(solution)/shard_map/forward/pallas_call | solution.py:139
  50.4 5.6 %backward.1 = (bf16[128,384]{1,0:T(8,128)(2,1)S(1)}, bf16[128,384]{1,0:T(8,128)(2,1)S(1)}, bf16[2,128,1024]{2,1,0:T(8,128)(2,1)S(1)}, f32[2,128,1024]{2,1,0:T(8,128)S(1)}) custom-call(bf16[128,1024]{1,0:T(8,128)(2,1)S(1)} %bitcast.40, bf16[128,1024]{1,0:T(8,128)(2,1)S(1)} %collective-permute-done.5.d1, bf16[128,1024]{1,0:T(8,128)(2,1)S(1)} %collective-permute-done.6.d2, ...), custom_call_target="tpu_custom_call" | custom-call | flops 1207959552 | bytes 12582912 | tf_op jit(solution)/shard_map/backward/pallas_call | solution.py:200
  56.3 1.6 %collective-permute-start.4 = (bf16[128,1024]{1,0:T(8,128)(2,1)S(1)}, bf16[128,1024]{1,0:T(8,128)(2,1)S(1)}, u32[]{:S(2)}, u32[]{:S(2)}) collective-permute-start(bf16[128,1024]{1,0:T(8,128)(2,1)S(1)} %fusion.2), channel_id=1, source_target_pairs={{0,2},{1,3},{2,0},{3,1},{4,6},{5,7},{6,4},{7,5},{8,10},{9,11},{10,... | collective-permute-start | bytes 786440 | tf_op jit(solution)/shard_map/ppermute | solution.py:322
  58.1 1.6 %collective-permute-start.9 = (bf16[128,1024]{1,0:T(8,128)(2,1)S(1)}, bf16[128,1024]{1,0:T(8,128)(2,1)S(1)}, u32[]{:S(2)}, u32[]{:S(2)}) collective-permute-start(bf16[128,1024]{1,0:T(8,128)(2,1)S(1)} %fusion.3), channel_id=1, source_target_pairs={{0,2},{1,3},{2,0},{3,1},{4,6},{5,7},{6,4},{7,5},{8,10},{9,11},{10,... | collective-permute-start | bytes 786440 | tf_op jit(solution)/shard_map/ppermute | solution.py:322
  59.7 5.8 %collective-permute-done.4 = bf16[128,1024]{1,0:T(8,128)(2,1)S(1)} collective-permute-done((bf16[128,1024]{1,0:T(8,128)(2,1)S(1)}, bf16[128,1024]{1,0:T(8,128)(2,1)S(1)}, u32[]{:S(2)}, u32[]{:S(2)}) %collective-permute-start.4) | collective-permute-done | bytes 262176 | tf_op jit(solution)/shard_map/ppermute | solution.py:322
  66.3 4.8 %all-to-all-start.1 = ((bf16[8,16,1024]{2,1,0:T(8,128)(2,1)}), bf16[8,16,1024]{2,1,0:T(8,128)(2,1)S(1)}, u32[]{:S(2)}, u32[]{:S(2)}) async-start(bf16[8,16,1024]{2,1,0:T(8,128)(2,1)} %bitcast.8), calls=%async_computation.1 | async-start | bytes 524288 | tf_op jit(solution)/shard_map/all_to_all | solution.py:326
  71.9 7.6 %all-to-all-done.1 = bf16[8,16,1024]{2,1,0:T(8,128)(2,1)S(1)} async-done(((bf16[8,16,1024]{2,1,0:T(8,128)(2,1)}), bf16[8,16,1024]{2,1,0:T(8,128)(2,1)S(1)}, u32[]{:S(2)}, u32[]{:S(2)}) %all-to-all-start.1) | async-done | bytes 262176 | tf_op jit(solution)/shard_map/all_to_all | solution.py:326
  79.5 3.4 %all-to-all-start.3 = ((bf16[8,16,1024]{2,1,0:T(8,128)(2,1)}), bf16[8,16,1024]{2,1,0:T(8,128)(2,1)S(1)}, u32[]{:S(2)}, u32[]{:S(2)}) async-start(bf16[8,16,1024]{2,1,0:T(8,128)(2,1)} %bitcast.13), calls=%async_computation.3 | async-start | bytes 524288 | tf_op jit(solution)/shard_map/all_to_all | solution.py:326
  82.9 1.1 %mix.1 = (bf16[128,1024]{1,0:T(8,128)(2,1)}, f32[8,128]{1,0:T(8,128)S(1)}) custom-call(bf16[128,1024]{1,0:T(8,128)(2,1)S(1)} %bitcast.43, bf16[128,128]{1,0:T(8,128)(2,1)S(1)} %get-tuple-element.29.w_hi, bf16[128,128]{1,0:T(8,128)(2,1)S(1)} %get-tuple-element.30.w_lo, bf16[128,128]{1,0:T(8,128)(2,1)S(1)} %get-tuple-element.31.sel, ...), custom_call_target="tpu_custom_call" | custom-call | flops 100663296 | bytes 786432 | tf_op jit(solution)/shard_map/mix/pallas_call | solution.py:289
  84.0 1.2 %collective-permute-done.10 = f32[8,128]{1,0:T(8,128)S(1)} collective-permute-done((f32[8,128]{1,0:T(8,128)S(1)}, f32[8,128]{1,0:T(8,128)S(1)}, u32[]{:S(2)}, u32[]{:S(2)}) %collective-permute-start.10) | collective-permute-done | bytes 4128 | tf_op jit(solution)/shard_map/ppermute | solution.py:322
  85.1 1.5 %collective-permute-start.11 = (f32[8,128]{1,0:T(8,128)S(1)}, f32[8,128]{1,0:T(8,128)S(1)}, u32[]{:S(2)}, u32[]{:S(2)}) collective-permute-start(f32[8,128]{1,0:T(8,128)S(1)} %add.40), channel_id=1, source_target_pairs={{0,2},{1,3},{2,0},{3,1},{4,6},{5,7},{6,4},{7,5},{8,10},{9,11},{10,... | collective-permute-start | bytes 12296 | tf_op jit(solution)/shard_map/ppermute | solution.py:322
  86.7 0.9 copy-done.9
  94.1 4.2 %grads.1 = (bf16[4096,384]{1,0:T(8,128)(2,1)}, bf16[4096,384]{1,0:T(8,128)(2,1)}, bf16[384,4096]{1,0:T(8,128)(2,1)}) custom-call(bf16[128,1024]{1,0:T(8,128)(2,1)S(1)} %bitcast.37, bf16[128,1024]{1,0:T(8,128)(2,1)S(1)} %copy-done.11, bf16[128,1024]{1,0:T(8,128)(2,1)S(1)} %collective-permute-done.1.x2, bf16[128,1024]{1,0:T(8,128)(2,1)S(1)} %copy-done.13, ...), custom_call_target="tpu_custom_call" | custom-call | flops 1207959552 | bytes 11534336 | tf_op jit(solution)/shard_map/grads/pallas_call | solution.py:251
  (75 shorter events, 13.4 us)
Async XLA Ops:
  21.0 12.2 %all-to-all-start.2 = ((bf16[8,16,1024]{2,1,0:T(8,128)(2,1)}), bf16[8,16,1024]{2,1,0:T(8,128)(2,1)S(1)}, u32[]{:S(2)}, u32[]{:S(2)}) async-start(bf16[8,16,1024]{2,1,0:T(8,128)(2,1)} %get-tuple-element.33), calls=%async_computation.2 | async-start | bytes 524288 | tf_op jit(solution)/shard_map/all_to_all | solution.py:326
  24.6 10.1 %collective-permute-start.1 = (bf16[128,1024]{1,0:T(8,128)(2,1)S(1)}, bf16[128,1024]{1,0:T(8,128)(2,1)S(1)}, u32[]{:S(2)}, u32[]{:S(2)}) collective-permute-start(bf16[128,1024]{1,0:T(8,128)(2,1)S(1)} %bitcast.34), channel_id=1, source_target_pairs={{0,2},{1,3},{2,0},{3,1},{4,6},{5,7},{6,4},{7,5},{8,10},{9,11},{10,... | collective-permute-start | bytes 786440 | tf_op jit(solution)/shard_map/ppermute | solution.py:322
  33.1 6.4 %collective-permute-start.6 = (bf16[128,1024]{1,0:T(8,128)(2,1)S(1)}, bf16[128,1024]{1,0:T(8,128)(2,1)S(1)}, u32[]{:S(2)}, u32[]{:S(2)}) collective-permute-start(bf16[128,1024]{1,0:T(8,128)(2,1)S(1)} %bitcast.38), channel_id=1, source_target_pairs={{0,2},{1,3},{2,0},{3,1},{4,6},{5,7},{6,4},{7,5},{8,10},{9,11},{10,... | collective-permute-start | bytes 786440 | tf_op jit(solution)/shard_map/ppermute | solution.py:322
  34.7 4.9 %collective-permute-start = (bf16[128,1024]{1,0:T(8,128)(2,1)S(1)}, bf16[128,1024]{1,0:T(8,128)(2,1)S(1)}, u32[]{:S(2)}, u32[]{:S(2)}) collective-permute-start(bf16[128,1024]{1,0:T(8,128)(2,1)S(1)} %bitcast.35), channel_id=1, source_target_pairs={{0,1},{1,0},{2,3},{3,2},{4,5},{5,4},{6,7},{7,6},{8,9},{9,8},{10,11... | collective-permute-start | bytes 786440 | tf_op jit(solution)/shard_map/ppermute | solution.py:322
  34.7 4.9 %collective-permute-start.2 = (bf16[128,1024]{1,0:T(8,128)(2,1)S(1)}, bf16[128,1024]{1,0:T(8,128)(2,1)S(1)}, u32[]{:S(2)}, u32[]{:S(2)}) collective-permute-start(bf16[128,1024]{1,0:T(8,128)(2,1)S(1)} %collective-permute-done.1.x2), channel_id=1, source_target_pairs={{0,1},{1,0},{2,3},{3,2},{4,5},{5,4},{6,7},{7,6},{8,9},{9,8},{10,11... | collective-permute-start | bytes 786440 | tf_op jit(solution)/shard_map/ppermute | solution.py:322
  35.2 15.2 %collective-permute-start.5 = (bf16[128,1024]{1,0:T(8,128)(2,1)S(1)}, bf16[128,1024]{1,0:T(8,128)(2,1)S(1)}, u32[]{:S(2)}, u32[]{:S(2)}) collective-permute-start(bf16[128,1024]{1,0:T(8,128)(2,1)S(1)} %bitcast.39), channel_id=1, source_target_pairs={{0,1},{1,0},{2,3},{3,2},{4,5},{5,4},{6,7},{7,6},{8,9},{9,8},{10,11... | collective-permute-start | bytes 786440 | tf_op jit(solution)/shard_map/ppermute | solution.py:322
  39.5 10.8 %copy-start.8 = (bf16[128,1024]{1,0:T(8,128)(2,1)}, bf16[128,1024]{1,0:T(8,128)(2,1)S(1)}, u32[]{:S(2)}) copy-start(bf16[128,1024]{1,0:T(8,128)(2,1)S(1)} %collective-permute-done.6.d2) | copy-start | bytes 786436
  39.5 10.8 %collective-permute-start.7 = (bf16[128,1024]{1,0:T(8,128)(2,1)S(1)}, bf16[128,1024]{1,0:T(8,128)(2,1)S(1)}, u32[]{:S(2)}, u32[]{:S(2)}) collective-permute-start(bf16[128,1024]{1,0:T(8,128)(2,1)S(1)} %collective-permute-done.6.d2), channel_id=1, source_target_pairs={{0,1},{1,0},{2,3},{3,2},{4,5},{5,4},{6,7},{7,6},{8,9},{9,8},{10,11... | collective-permute-start | bytes 786440 | tf_op jit(solution)/shard_map/ppermute | solution.py:322
  39.5 10.3 %copy-start.10 = (bf16[128,1024]{1,0:T(8,128)(2,1)}, bf16[128,1024]{1,0:T(8,128)(2,1)S(1)}, u32[]{:S(2)}) copy-start(bf16[128,1024]{1,0:T(8,128)(2,1)S(1)} %collective-permute-done.x1) | copy-start | bytes 786436
  39.5 10.3 %copy-start.12 = (bf16[128,1024]{1,0:T(8,128)(2,1)}, bf16[128,1024]{1,0:T(8,128)(2,1)S(1)}, u32[]{:S(2)}) copy-start(bf16[128,1024]{1,0:T(8,128)(2,1)S(1)} %collective-permute-done.2.x3) | copy-start | bytes 786436
  49.8 6.2 %copy-start.22 = (bf16[128,384]{1,0:T(8,128)(2,1)}, bf16[128,384]{1,0:T(8,128)(2,1)S(1)}, u32[]{:S(2)}) copy-start(bf16[128,384]{1,0:T(8,128)(2,1)S(1)} %get-tuple-element.40.hidden) | copy-start | bytes 294916
  49.8 6.4 %collective-permute-start.3 = (bf16[2,128,1024]{2,1,0:T(8,128)(2,1)S(1)}, bf16[2,128,1024]{2,1,0:T(8,128)(2,1)S(1)}, u32[]{:S(2)}, u32[]{:S(2)}) collective-permute-start(bf16[2,128,1024]{2,1,0:T(8,128)(2,1)S(1)} %get-tuple-element.28), channel_id=1, source_target_pairs={{0,1},{1,0},{2,3},{3,2},{4,5},{5,4},{6,7},{7,6},{8,9},{9,8},{10,11... | collective-permute-start | bytes 1572872 | tf_op jit(solution)/shard_map/ppermute | solution.py:322
  50.3 5.7 %copy-start.16 = (bf16[128,1024]{1,0:T(8,128)(2,1)}, bf16[128,1024]{1,0:T(8,128)(2,1)S(1)}, u32[]{:S(2)}) copy-start(bf16[128,1024]{1,0:T(8,128)(2,1)S(1)} %collective-permute-done.7.d3) | copy-start | bytes 786436
  56.0 10.2 %copy-start.24 = (bf16[128,384]{1,0:T(8,128)(2,1)}, bf16[128,384]{1,0:T(8,128)(2,1)S(1)}, u32[]{:S(2)}) copy-start(bf16[128,384]{1,0:T(8,128)(2,1)S(1)} %get-tuple-element.41.dact) | copy-start | bytes 294916
  56.0 10.2 %copy-start.26 = (bf16[128,384]{1,0:T(8,128)(2,1)}, bf16[128,384]{1,0:T(8,128)(2,1)S(1)}, u32[]{:S(2)}) copy-start(bf16[128,384]{1,0:T(8,128)(2,1)S(1)} %get-tuple-element.42.dlin) | copy-start | bytes 294916
  56.0 26.9 %copy-start.7 = (bf16[128,1024]{1,0:T(8,128)(2,1)S(1)}, bf16[128,1024]{1,0:T(8,128)(2,1)}, u32[]{:S(2)}) copy-start(bf16[128,1024]{1,0:T(8,128)(2,1)} %d_out.3) | copy-start | bytes 786436
  56.0 26.9 %copy-start.20 = (s32[128,8]{0,1:T(8,128)S(1)}, s32[128,8]{0,1:T(8,128)}, u32[]{:S(2)}) copy-start(s32[128,8]{0,1:T(8,128)} %param.8) | copy-start | bytes 12292
  56.1 2.0 %collective-permute-start.8 = (bf16[2,128,1024]{2,1,0:T(8,128)(2,1)S(1)}, bf16[2,128,1024]{2,1,0:T(8,128)(2,1)S(1)}, u32[]{:S(2)}, u32[]{:S(2)}) collective-permute-start(bf16[2,128,1024]{2,1,0:T(8,128)(2,1)S(1)} %get-tuple-element.37), channel_id=1, source_target_pairs={{0,1},{1,0},{2,3},{3,2},{4,5},{5,4},{6,7},{7,6},{8,9},{9,8},{10,11... | collective-permute-start | bytes 1572872 | tf_op jit(solution)/shard_map/ppermute | solution.py:322
  56.3 9.2 %collective-permute-start.4 = (bf16[128,1024]{1,0:T(8,128)(2,1)S(1)}, bf16[128,1024]{1,0:T(8,128)(2,1)S(1)}, u32[]{:S(2)}, u32[]{:S(2)}) collective-permute-start(bf16[128,1024]{1,0:T(8,128)(2,1)S(1)} %fusion.2), channel_id=1, source_target_pairs={{0,2},{1,3},{2,0},{3,1},{4,6},{5,7},{6,4},{7,5},{8,10},{9,11},{10,... | collective-permute-start | bytes 786440 | tf_op jit(solution)/shard_map/ppermute | solution.py:322
  58.1 13.0 %collective-permute-start.9 = (bf16[128,1024]{1,0:T(8,128)(2,1)S(1)}, bf16[128,1024]{1,0:T(8,128)(2,1)S(1)}, u32[]{:S(2)}, u32[]{:S(2)}) collective-permute-start(bf16[128,1024]{1,0:T(8,128)(2,1)S(1)} %fusion.3), channel_id=1, source_target_pairs={{0,2},{1,3},{2,0},{3,1},{4,6},{5,7},{6,4},{7,5},{8,10},{9,11},{10,... | collective-permute-start | bytes 786440 | tf_op jit(solution)/shard_map/ppermute | solution.py:322
  66.3 13.2 %all-to-all-start.1 = ((bf16[8,16,1024]{2,1,0:T(8,128)(2,1)}), bf16[8,16,1024]{2,1,0:T(8,128)(2,1)S(1)}, u32[]{:S(2)}, u32[]{:S(2)}) async-start(bf16[8,16,1024]{2,1,0:T(8,128)(2,1)} %bitcast.8), calls=%async_computation.1 | async-start | bytes 524288 | tf_op jit(solution)/shard_map/all_to_all | solution.py:326
  79.5 18.9 %all-to-all-start.3 = ((bf16[8,16,1024]{2,1,0:T(8,128)(2,1)}), bf16[8,16,1024]{2,1,0:T(8,128)(2,1)S(1)}, u32[]{:S(2)}, u32[]{:S(2)}) async-start(bf16[8,16,1024]{2,1,0:T(8,128)(2,1)} %bitcast.13), calls=%async_computation.3 | async-start | bytes 524288 | tf_op jit(solution)/shard_map/all_to_all | solution.py:326
  84.0 1.2 %collective-permute-start.10 = (f32[8,128]{1,0:T(8,128)S(1)}, f32[8,128]{1,0:T(8,128)S(1)}, u32[]{:S(2)}, u32[]{:S(2)}) collective-permute-start(f32[8,128]{1,0:T(8,128)S(1)} %get-tuple-element.39), channel_id=1, source_target_pairs={{0,1},{1,0},{2,3},{3,2},{4,5},{5,4},{6,7},{7,6},{8,9},{9,8},{10,11... | collective-permute-start | bytes 12296 | tf_op jit(solution)/shard_map/ppermute | solution.py:322
  85.1 14.1 %collective-permute-start.11 = (f32[8,128]{1,0:T(8,128)S(1)}, f32[8,128]{1,0:T(8,128)S(1)}, u32[]{:S(2)}, u32[]{:S(2)}) collective-permute-start(f32[8,128]{1,0:T(8,128)S(1)} %add.40), channel_id=1, source_target_pairs={{0,2},{1,3},{2,0},{3,1},{4,6},{5,7},{6,4},{7,5},{8,10},{9,11},{10,... | collective-permute-start | bytes 12296 | tf_op jit(solution)/shard_map/ppermute | solution.py:322
  (19 other events, 37.0 us)

commit v2 on v1

v2 whole, which is shorter than its diff:
```python
import functools

import jax
import jax.numpy as jnp
from jax import lax
from jax.experimental import pallas as pl
from jax.experimental.pallas import tpu as pltpu
from jax.sharding import PartitionSpec as P

CAP = 16
F32 = jnp.float32
BF16 = jnp.bfloat16
NN = (((1,), (0,)), ((), ()))
NT = (((1,), (1,)), ((), ()))
TN = (((0,), (0,)), ((), ()))


def dot(a, b, dims=NN):
    return lax.dot_general(a, b, dims, preferred_element_type=F32)


def params(mib=16):
    return pltpu.CompilerParams(vmem_limit_bytes=mib * 1024 * 1024)


def cost(flops, nbytes):
    return pl.CostEstimate(flops=flops, bytes_accessed=nbytes, transcendentals=0)


def vspec():
    return pl.BlockSpec(memory_space=pltpu.VMEM)


def hspec():
    return pl.BlockSpec(memory_space=pltpu.HBM)


def aspec():
    return pl.BlockSpec(memory_space=pl.ANY)


def fixed(x):
    return pltpu.with_memory_space_constraint(x, pltpu.HBM)


def dispatch_kernel(
    routes_in, gates_in, tokens_in, d_in, slots_out, sel, pick, w_hi, w_lo, routes, gates, tokens, d_out, sem
):
    experts, cap2, quarter = slots_out.shape
    cap = cap2 // 2
    topk, tok = routes.shape
    slots = experts * cap
    loads = [
        pltpu.make_async_copy(src, dst, sem.at[i])
        for i, (src, dst) in enumerate(
            ((routes_in, routes), (gates_in, gates), (tokens_in, tokens), (d_in, d_out))
        )
    ]
    for load in loads:
        load.start()
    loads[0].wait()
    loads[1].wait()
    match = routes[...][None] == lax.broadcasted_iota(jnp.int32, (experts, topk, tok), 0)
    hit = jnp.sum(jnp.where(match, 1.0, 0.0), axis=1)
    gate = jnp.sum(jnp.where(match, gates[...][None], 0.0), axis=1)
    earlier = lax.broadcasted_iota(jnp.int32, (tok, tok), 0) < lax.broadcasted_iota(
        jnp.int32, (tok, tok), 1
    )
    before = dot(hit.astype(BF16), jnp.where(earlier, 1.0, 0.0).astype(BF16))
    place = jnp.where(hit > 0.0, before, -1.0)[:, None, :]
    row = lax.broadcasted_iota(jnp.int32, (experts, cap, tok), 1).astype(F32)
    chosen = jnp.where(place == row, 1.0, 0.0)
    weight = (chosen * gate[:, None, :]).reshape(slots, tok)
    chosen = chosen.reshape(slots, tok)
    select = chosen.astype(BF16)
    loads[2].wait()
    x = dot(select, tokens[...]).astype(BF16)
    slots_out[:, :cap, :] = x.reshape(experts, cap, quarter)
    slot_gate = jnp.sum(weight, axis=1, keepdims=True)
    loads[3].wait()
    d = (slot_gate * dot(select, d_out[...])).astype(BF16)
    slots_out[:, cap:, :] = d.reshape(experts, cap, quarter)
    sel[...] = select
    pick[...] = chosen.T.astype(BF16)
    back = weight.T
    high = back.astype(BF16)
    w_hi[...] = high
    w_lo[...] = (back - high.astype(F32)).astype(BF16)


def dispatch(routes_t, gates_t, tokens, d_out, experts):
    tok, quarter = tokens.shape
    slots = experts * CAP
    return pl.pallas_call(
        dispatch_kernel,
        out_shape=(
            jax.ShapeDtypeStruct((experts, 2 * CAP, quarter), BF16),
            jax.ShapeDtypeStruct((slots, tok), BF16),
            jax.ShapeDtypeStruct((tok, slots), BF16),
            jax.ShapeDtypeStruct((tok, slots), BF16),
            jax.ShapeDtypeStruct((tok, slots), BF16),
        ),
        in_specs=[hspec()] * 4,
        out_specs=(vspec(),) * 5,
        scratch_shapes=[
            pltpu.VMEM(routes_t.shape, jnp.int32),
            pltpu.VMEM(gates_t.shape, F32),
            pltpu.VMEM(tokens.shape, BF16),
            pltpu.VMEM(d_out.shape, BF16),
            pltpu.SemaphoreType.DMA((4,)),
        ],
        compiler_params=params(),
        cost_estimate=cost(4 * slots * tok * quarter, 8 * tok * quarter),
        name="dispatch",
    )(*(fixed(v) for v in (routes_t, gates_t, tokens, d_out)))


def quarter_of(me, flip, size):
    return pl.ds(pl.multiple_of((me ^ flip) * size, size), size)


def fetch(src, dst, sem, part):
    copy = pltpu.make_async_copy(src.at[part], dst.at[part], sem)
    copy.start()
    return copy


def forward_kernel(
    x0, x1, x2, x3, wg, wu, wd, act, lin, hidden, vg, vu, vd, send_far, send_near, keep_far, keep_own, sem
):
    me = lax.axis_index("tp")
    size = x0.shape[1]
    xs = (x0, x1, x2, x3)
    loads, last = [], []
    for i in range(4):
        part = (quarter_of(me, i, size), slice(None))
        loads.append((fetch(wg, vg, sem.at[0, i], part), fetch(wu, vu, sem.at[1, i], part)))
    for n, i in enumerate((3, 2, 1, 0)):
        last.append(fetch(wd, vd, sem.at[2, n], (slice(None), quarter_of(me, i, size))))
    a = b = None
    for i in range(4):
        part = quarter_of(me, i, size)
        x = xs[i][...]
        loads[i][0].wait()
        pa = dot(x, vg[part, :])
        loads[i][1].wait()
        pb = dot(x, vu[part, :])
        a = pa if a is None else a + pa
        b = pb if b is None else b + pb
    act[...] = a
    lin[...] = b
    h = (a * jax.nn.sigmoid(a) * b).astype(BF16)
    hidden[...] = h
    for n, (i, out) in enumerate(((3, send_far), (2, keep_far), (1, send_near), (0, keep_own))):
        last[n].wait()
        out[...] = dot(h, vd[:, quarter_of(me, i, size)]).astype(out.dtype)


def forward(xs, wg, wu, wd):
    rows, size = xs[0].shape
    d, ff = wg.shape
    return pl.pallas_call(
        forward_kernel,
        out_shape=(
            jax.ShapeDtypeStruct((rows, ff), F32),
            jax.ShapeDtypeStruct((rows, ff), F32),
            jax.ShapeDtypeStruct((rows, ff), BF16),
            jax.ShapeDtypeStruct((d, ff), BF16),
            jax.ShapeDtypeStruct((d, ff), BF16),
            jax.ShapeDtypeStruct((ff, d), BF16),
            jax.ShapeDtypeStruct((rows, size), BF16),
            jax.ShapeDtypeStruct((rows, size), BF16),
            jax.ShapeDtypeStruct((rows, size), F32),
            jax.ShapeDtypeStruct((rows, size), F32),
        ),
        in_specs=[vspec()] * 4 + [hspec()] * 3,
        out_specs=(vspec(),) * 10,
        scratch_shapes=[pltpu.SemaphoreType.DMA((3, 4))],
        compiler_params=params(),
        cost_estimate=cost(6 * rows * d * ff, 6 * d * ff + 6 * rows * d),
        name="forward",
    )(*xs, fixed(wg), fixed(wu), fixed(wd))


def hidden_grad_kernel(d0, d1, d2, d3, act, lin, vd, dact, dlin):
    me = lax.axis_index("tp")
    size = d0.shape[1]
    ds = (d0, d1, d2, d3)
    dhid = None
    for i in range(4):
        p = dot(ds[i][...], vd[:, quarter_of(me, i, size)], NT)
        dhid = p if dhid is None else dhid + p
    a = act[...]
    s = jax.nn.sigmoid(a)
    dlin[...] = (dhid * (a * s)).astype(BF16)
    dact[...] = (dhid * lin[...] * s * (1.0 + a * (1.0 - s))).astype(BF16)


def hidden_grad(ds, act, lin, vd):
    rows, size = ds[0].shape
    ff, d = vd.shape
    return pl.pallas_call(
        hidden_grad_kernel,
        out_shape=(
            jax.ShapeDtypeStruct((rows, ff), BF16),
            jax.ShapeDtypeStruct((rows, ff), BF16),
        ),
        in_specs=[vspec()] * 7,
        out_specs=(vspec(),) * 2,
        compiler_params=params(),
        cost_estimate=cost(2 * rows * d * ff, 2 * d * ff + 2 * rows * d),
        name="hidden_grad",
    )(*ds, act, lin, vd)


def input_grad_kernel(flips, after, dact, dlin, vg, vu, send, keep):
    me = lax.axis_index("tp")
    size = send.shape[1]
    da = dact[...]
    dl = dlin[...]
    for i, out in zip(flips, (send, keep)):
        part = quarter_of(me, i, size)
        p = dot(da, vg[part, :], NT) + dot(dl, vu[part, :], NT)
        out[...] = p.astype(out.dtype)


def input_grad(flips, after, dact, dlin, vg, vu):
    rows, ff = dact.shape
    d = vg.shape[0]
    return pl.pallas_call(
        functools.partial(input_grad_kernel, flips),
        out_shape=(
            jax.ShapeDtypeStruct((rows, d // 4), BF16),
            jax.ShapeDtypeStruct((rows, d // 4), F32),
        ),
        in_specs=[aspec()] + [vspec()] * 4,
        out_specs=(vspec(),) * 2,
        compiler_params=params(),
        cost_estimate=cost(2 * rows * d * ff, 2 * d * ff + 3 * rows * d),
        name="input_grad",
    )(after, dact, dlin, vg, vu)


def grads_kernel(*refs):
    given, (gg, gu, gd), held, (vg, vu, vd, sem, load_sem) = (
        refs[:11],
        refs[11:14],
        refs[14:25],
        refs[25:],
    )
    me = lax.axis_index("tp")
    size = given[0].shape[1]
    loads = [
        pltpu.make_async_copy(src, dst, load_sem.at[i])
        for i, (src, dst) in enumerate(zip(given, held))
    ]
    for i in (8, 9, 10, 0, 4, 1, 5, 2, 6, 3, 7):
        loads[i].start()
    for i in (8, 9, 10):
        loads[i].wait()
    h, da, dl = (held[i][...] for i in (8, 9, 10))
    stores = []
    for i in range(4):
        part = quarter_of(me, i, size)
        rows = (part, slice(None))
        cols = (slice(None), part)
        loads[i].wait()
        x = held[i][...]
        vg[part, :] = dot(x, da, TN).astype(BF16)
        stores.append(fetch(vg, gg, sem.at[0, i], rows))
        vu[part, :] = dot(x, dl, TN).astype(BF16)
        stores.append(fetch(vu, gu, sem.at[1, i], rows))
        loads[4 + i].wait()
        vd[:, part] = dot(h, held[4 + i][...], TN).astype(BF16)
        stores.append(fetch(vd, gd, sem.at[2, i], cols))
    for store in stores:
        store.wait()


def grads(xs, ds, hidden, dact, dlin):
    rows, size = xs[0].shape
    ff = hidden.shape[1]
    d = 4 * size
    return pl.pallas_call(
        grads_kernel,
        out_shape=(
            jax.ShapeDtypeStruct((d, ff), BF16),
            jax.ShapeDtypeStruct((d, ff), BF16),
            jax.ShapeDtypeStruct((ff, d), BF16),
        ),
        in_specs=[hspec()] * 11,
        out_specs=(hspec(),) * 3,
        scratch_shapes=[pltpu.VMEM((rows, size), BF16)] * 8
        + [pltpu.VMEM((rows, ff), BF16)] * 3
        + [
            pltpu.VMEM((d, ff), BF16),
            pltpu.VMEM((d, ff), BF16),
            pltpu.VMEM((ff, d), BF16),
            pltpu.SemaphoreType.DMA((3, 4)),
            pltpu.SemaphoreType.DMA((11,)),
        ],
        compiler_params=params(32),
        cost_estimate=cost(6 * rows * d * ff, 6 * d * ff + 4 * rows * d),
        name="grads",
    )(*(fixed(v) for v in (*xs, *ds, hidden, dact, dlin)))


def total_kernel(after, keep, near, far, out):
    out[...] = (keep[...] + near[...].astype(F32) + far[...].astype(F32)).astype(BF16)


def total(after, keep, near, far):
    return pl.pallas_call(
        total_kernel,
        out_shape=jax.ShapeDtypeStruct(far.shape, BF16),
        in_specs=[aspec()] + [vspec()] * 3,
        out_specs=vspec(),
        compiler_params=params(),
        cost_estimate=cost(2 * far.size, 12 * far.size),
        name="total",
    )(after, keep, near, far)


def mix_kernel(back, w_hi, w_lo, sel, d_out, routes, mixed, dots):
    slots, tok = sel.shape
    topk = routes.shape[0]
    experts = slots // CAP
    o = back[...]
    mixed[...] = (dot(w_hi[...], o) + dot(w_lo[...], o)).astype(BF16)
    select = sel[...]
    per_slot = jnp.sum(dot(select, d_out[...]) * o.astype(F32), axis=1, keepdims=True)
    spread = select.astype(F32) * per_slot
    per_expert = jnp.sum(spread.reshape(experts, CAP, tok), axis=1)
    match = routes[...][None] == lax.broadcasted_iota(jnp.int32, (experts, topk, tok), 0)
    dots[...] = jnp.sum(jnp.where(match, per_expert[:, None, :], 0.0), axis=0)


def mix(back, w_hi, w_lo, sel, d_out, routes_t):
    slots, quarter = back.shape
    topk, tok = routes_t.shape
    return pl.pallas_call(
        mix_kernel,
        out_shape=(
            jax.ShapeDtypeStruct((tok, quarter), BF16),
            jax.ShapeDtypeStruct((topk, tok), F32),
        ),
        in_specs=[vspec()] * 6,
        out_specs=(vspec(),) * 2,
        compiler_params=params(),
        cost_estimate=cost(6 * slots * tok * quarter, 6 * tok * quarter),
        name="mix",
    )(back, w_hi, w_lo, sel, d_out, routes_t)


def collect_kernel(back, pick, d_tokens):
    d_tokens[...] = dot(pick[...], back[...]).astype(BF16)


def collect(back, pick):
    slots, quarter = back.shape
    tok = pick.shape[0]
    return pl.pallas_call(
        collect_kernel,
        out_shape=jax.ShapeDtypeStruct((tok, quarter), BF16),
        in_specs=[vspec()] * 2,
        out_specs=vspec(),
        compiler_params=params(),
        cost_estimate=cost(2 * slots * tok * quarter, 4 * tok * quarter),
        name="collect",
    )(back, pick)


def swap(x, flip):
    return lax.ppermute(x, "tp", [(i, i ^ flip) for i in range(4)])


def exchange(x):
    return lax.all_to_all(x, "ctx", split_axis=0, concat_axis=0, tiled=True)


def gather(own):
    near = swap(own, 1)
    far = swap(own, 2)
    return (own, near, far, swap(far, 1))


def plus(keep, *others):
    return sum((o.astype(F32) for o in others), keep).astype(BF16)


def on_device(tokens, routes, gates, w_gate, w_up, w_down, d_out):
    tok, quarter = tokens.shape
    sources = lax.axis_size("ctx")
    experts = sources * w_gate.shape[0]
    slots = experts * CAP
    rows = sources * CAP
    routes_t = routes.T
    outgoing, sel, pick, w_hi, w_lo = dispatch(routes_t, gates.T, tokens, d_out, experts)
    arrived = exchange(outgoing)
    xq = gather(arrived[:, :CAP].reshape(rows, quarter))
    dq = gather(arrived[:, CAP:].reshape(rows, quarter))
    act, lin, hidden, vg, vu, vd, send_far, send_near, keep_far, keep_own = forward(
        xq, w_gate[0], w_up[0], w_down[0]
    )
    half_out = plus(keep_far, swap(send_far, 1))
    near_out = swap(send_near, 1)
    dact, dlin = hidden_grad(dq, act, lin, vd)
    send_dx_far, keep_dx_far = input_grad((3, 2), half_out, dact, dlin, vg, vu)
    far_out = swap(half_out, 2)
    half_dx = plus(keep_dx_far, swap(send_dx_far, 1))
    send_dx_near, keep_dx_own = input_grad((1, 0), send_dx_far, dact, dlin, vg, vu)
    far_dx = swap(half_dx, 2)
    near_dx = swap(send_dx_near, 1)
    out_rows = plus(keep_own, near_out, far_out)
    back_out = exchange(out_rows.reshape(sources, CAP, quarter)).reshape(slots, quarter)
    grad_gate, grad_up, grad_down = grads(xq, dq, hidden, dact, dlin)
    dx_rows = total(fixed(grad_gate), keep_dx_own, near_dx, far_dx)
    back_dx = exchange(dx_rows.reshape(sources, CAP, quarter)).reshape(slots, quarter)
    mixed, dots = mix(back_out, w_hi, w_lo, sel, d_out, routes_t)
    dots = dots + swap(dots, 1)
    dots = dots + swap(dots, 2)
    d_tokens = collect(back_dx, pick)
    return (mixed, d_tokens, dots.T, grad_gate[None], grad_up[None], grad_down[None])


def solution(mesh):
    placed = (
        P("ctx", "tp"),
        P("ctx", None),
        P("ctx", None),
        P("ctx", None, "tp"),
        P("ctx", None, "tp"),
        P("ctx", "tp", None),
        P("ctx", "tp"),
    )
    return jax.shard_map(
        on_device,
        mesh=mesh,
        in_specs=placed,
        out_specs=(
            P("ctx", "tp"),
            P("ctx", "tp"),
            P("ctx", None),
            P("ctx", None, "tp"),
            P("ctx", None, "tp"),
            P("ctx", "tp", None),
        ),
        check_vma=False,
    )
```

time: 101 us -> 77.6 us (0.77)
  local copies, waits for them, and re-layouts: 16.7 us -> 0.1 us
  waiting for transfers between devices: 26.1 us -> 15.3 us
  blocking collectives: 15.9 us -> 21.6 us
  starting transfers between devices: 20.8 us -> 19 us
  Pallas kernels: 17.2 us -> 18.7 us
    unnamed x56 -> x26, local copies, waits for them, and re-layouts: 16.7 us -> 0.06 us
    all_to_all x3 -> x2, waiting for transfers between devices: 14.7 us -> 1.78 us  [exchange(): return lax.all_to_all(x, 'ctx', split_axis=0, concat_axis=0, tiled=True)]
    all_to_all x1, blocking collectives: 15.9 us -> 21.6 us  [exchange(): return lax.all_to_all(x, 'ctx', split_axis=0, concat_axis=0, tiled=True)]
    ppermute x12 -> x14, waiting for transfers between devices: 11.4 us -> 13.6 us  [swap(): return lax.ppermute(x, 'tp', [(i, i ^ flip) for i in range(4)])]
    pallas_call x1, Pallas kernels: 4.22 us -> 6.07 us  [grads(): pl.pallas_call(grads_kernel, out_shape=(jax.ShapeDtypeStruct((d, ff), BF1...]
    pallas_call x1 -> x4, Pallas kernels: 5.58 us -> 4.07 us  [the longest x2 2.2 us: input_grad(): pl.pallas_call(functools.partial(input_grad_kernel, flips), out_shape=(ja...]
    all_to_all x3 -> x2, starting transfers between devices: 11.8 us -> 10.4 us  [exchange(): return lax.all_to_all(x, 'ctx', split_axis=0, concat_axis=0, tiled=True)]
    ppermute x12 -> x14, starting transfers between devices: 8.94 us -> 8.66 us  [swap(): return lax.ppermute(x, 'tp', [(i, i ^ flip) for i in range(4)])]
  transfers between devices with their start and end apart: 15 -> 16, of which waited for: 6 -> 6; matrix products, arithmetic and copies ran while one was open for 2% -> 2% of each run, Pallas kernels for 16% -> 21%
where the time goes in v2:
time: 77.6 us; the launch traced here: 77.2 us
  blocking collectives  21.6 us (28%)
  starting transfers between devices  19 us (24%)
  Pallas kernels  18.7 us (24%)
  waiting for transfers between devices  15.3 us (20%)
  other arithmetic  1.5 us (2%)
  between operations  0.91 us (1%)
    all_to_all x1, blocking collectives, exchange(): return lax.all_to_all(x, 'ctx', split_axis=0, concat_axis=0, tiled=True)  21.6 us
    ppermute x14, waiting for transfers between devices, swap(): return lax.ppermute(x, 'tp', [(i, i ^ flip) for i in range(4)])  13.6 us
    all_to_all x2, starting transfers between devices, exchange(): return lax.all_to_all(x, 'ctx', split_axis=0, concat_axis=0, tiled=True)  10.4 us
    ppermute x14, starting transfers between devices, swap(): return lax.ppermute(x, 'tp', [(i, i ^ flip) for i in range(4)])  8.66 us
    pallas_call x1, Pallas kernels, grads(): pl.pallas_call(grads_kernel, out_shape=(jax.ShapeDtypeStruct((d, ff), BF1...  6.07 us
    pallas_call x1, Pallas kernels, forward(): pl.pallas_call(forward_kernel, out_shape=(jax.ShapeDtypeStruct((rows, ff)...  5.15 us
    pallas_call x2, Pallas kernels, input_grad(): pl.pallas_call(functools.partial(input_grad_kernel, flips), out_shape=(ja...  2.2 us
    all_to_all x2, waiting for transfers between devices, exchange(): return lax.all_to_all(x, 'ctx', split_axis=0, concat_axis=0, tiled=True)  1.78 us
  transfers between devices with their start and end apart: 16, of which 6 were waited for; matrix products, arithmetic and copies ran while one was open for 2% of the time, Pallas kernels for 21%

profile of v2, /device:TPU:0, one launch (start us, length us, event | category | flops | bytes accessed | tf_op | source)
XLA Modules:
  0.0 77.2 jit_solution(16444335730183776885)
XLA Ops:
  0.6 1.5 %dispatch.1 = (bf16[8,32,1024]{2,1,0:T(8,128)(2,1)S(1)}, bf16[128,128]{1,0:T(8,128)(2,1)S(1)}, bf16[128,128]{1,0:T(8,128)(2,1)S(1)}, bf16[128,128]{1,0:T(8,128)(2,1)S(1)}, bf16[128,128]{1,0:T(8,128)(2,1)S(1)}) custom-call(s32[8,128]{1,0:T(8,128)} %bitcast.26, f32[8,128]{1,0:T(8,128)} %bitcast.32, bf16[128,1024]{1,0:T(8,128)(2,1)} %tokens_in.1, ...), custom_call_target="tpu_custom_call" | custom-call | flops 67108864 | bytes 1048576 | tf_op jit(solution)/shard_map/dispatch/pallas_call | solution.py:94
  2.1 21.6 %all_to_all.15 = bf16[8,32,1024]{2,1,0:T(8,128)(2,1)S(1)} all-to-all(bf16[8,32,1024]{2,1,0:T(8,128)(2,1)S(1)} %get-tuple-element.32), channel_id=1, replica_groups=mesh['ctx'=8,'tp'=4] {'ctx'}, dimensions={0} | all-to-all | bytes 1048576 | tf_op jit(solution)/shard_map/all_to_all | solution.py:378
  23.8 1.6 %collective-permute-start.1 = (bf16[128,1024]{1,0:T(8,128)(2,1)S(1)}, bf16[128,1024]{1,0:T(8,128)(2,1)S(1)}, u32[]{:S(2)}, u32[]{:S(2)}) collective-permute-start(bf16[128,1024]{1,0:T(8,128)(2,1)S(1)} %bitcast.20), channel_id=1, source_target_pairs={{0,2},{1,3},{2,0},{3,1},{4,6},{5,7},{6,4},{7,5},{8,10},{9,11},{10,... | collective-permute-start | bytes 786440 | tf_op jit(solution)/shard_map/ppermute | solution.py:374
  25.4 5.4 %collective-permute-done.1.x2.refs_2_ = bf16[128,1024]{1,0:T(8,128)(2,1)S(1)} collective-permute-done((bf16[128,1024]{1,0:T(8,128)(2,1)S(1)}, bf16[128,1024]{1,0:T(8,128)(2,1)S(1)}, u32[]{:S(2)}, u32[]{:S(2)}) %collective-permute-start.1) | collective-permute-done | bytes 262176 | tf_op jit(solution)/shard_map/ppermute | solution.py:374
  30.8 1.5 %collective-permute-start.7 = (bf16[128,1024]{1,0:T(8,128)(2,1)S(1)}, bf16[128,1024]{1,0:T(8,128)(2,1)S(1)}, u32[]{:S(2)}, u32[]{:S(2)}) collective-permute-start(bf16[128,1024]{1,0:T(8,128)(2,1)S(1)} %bitcast.16), channel_id=1, source_target_pairs={{0,2},{1,3},{2,0},{3,1},{4,6},{5,7},{6,4},{7,5},{8,10},{9,11},{10,... | collective-permute-start | bytes 786440 | tf_op jit(solution)/shard_map/ppermute | solution.py:374
  32.3 5.2 %forward.1 = (f32[128,384]{1,0:T(8,128)S(1)}, f32[128,384]{1,0:T(8,128)S(1)}, bf16[128,384]{1,0:T(8,128)(2,1)S(1)}, bf16[4096,384]{1,0:T(8,128)(2,1)S(1)}, bf16[...) custom-call(bf16[128,1024]{1,0:T(8,128)(2,1)S(1)} %bitcast.22, ...), custom_call_target="tpu_custom_call" | custom-call | flops 1207959552 | bytes 12582912 | tf_op jit(solution)/shard_map/forward/pallas_call | solution.py:162
  38.1 1.4 %collective-permute-done.7.d2.refs_6_ = bf16[128,1024]{1,0:T(8,128)(2,1)S(1)} collective-permute-done((bf16[128,1024]{1,0:T(8,128)(2,1)S(1)}, bf16[128,1024]{1,0:T(8,128)(2,1)S(1)}, u32[]{:S(2)}, u32[]{:S(2)}) %collective-permute-start.7) | collective-permute-done | bytes 262176 | tf_op jit(solution)/shard_map/ppermute | solution.py:374
  40.0 1.6 %collective-permute-start.5 = (bf16[128,1024]{1,0:T(8,128)(2,1)S(1)}, bf16[128,1024]{1,0:T(8,128)(2,1)S(1)}, u32[]{:S(2)}, u32[]{:S(2)}) collective-permute-start(bf16[128,1024]{1,0:T(8,128)(2,1)S(1)} %add_convert_fusion.2.after), channel_id=1, source_target_pairs={{0,2},{1,3},{2,0},{3,1},{4,6},{5,7},{6,4},{7,5},{8,10},{9,11},{10,... | collective-permute-start | bytes 786440 | tf_op jit(solution)/shard_map/ppermute | solution.py:374
  41.7 1.1 %hidden_grad.1 = (bf16[128,384]{1,0:T(8,128)(2,1)S(1)}, bf16[128,384]{1,0:T(8,128)(2,1)S(1)}) custom-call(bf16[128,1024]{1,0:T(8,128)(2,1)S(1)} %bitcast.18, bf16[128,1024]{1,0:T(8,128)(2,1)S(1)} %collective-permute-done.6.d1.refs_5_, bf16[128,1024]{1,0:T(8,128)(2,1)S(1)} %collective-permute-done.7.d2.refs_6_, ...), custom_call_target="tpu_custom_call" | custom-call | flops 402653184 | bytes 4194304 | tf_op jit(solution)/shard_map/hidden_grad/pallas_call | solution.py:202
  42.8 1.1 %input_grad.2 = (bf16[128,1024]{1,0:T(8,128)(2,1)S(1)}, f32[128,1024]{1,0:T(8,128)S(1)}) custom-call(bf16[128,1024]{1,0:T(8,128)(2,1)S(1)} %add_convert_fusion.2.after, bf16[128,384]{1,0:T(8,128)(2,1)S(1)} %get-tuple-element.45.refs_9_.dact, bf16[128,384]{1,0:T(8,128)(2,1)S(1)} %get-tuple-element.46.refs_10_.dlin, ...), custom_call_target="tpu_custom_call" | custom-call | flops 402653184 | bytes 4718592 | tf_op jit(solution)/shard_map/input_grad/pallas_call | solution.py:230
  44.0 1.1 %input_grad.3 = (bf16[128,1024]{1,0:T(8,128)(2,1)S(1)}, f32[128,1024]{1,0:T(8,128)S(1)}) custom-call(bf16[128,1024]{1,0:T(8,128)(2,1)S(1)} %get-tuple-element.50.after, bf16[128,384]{1,0:T(8,128)(2,1)S(1)} %get-tuple-element.45.refs_9_.dact, bf16[128,384]{1,0:T(8,128)(2,1)S(1)} %get-tuple-element.46.refs_10_.dlin, ...), custom_call_target="tpu_custom_call" | custom-call | flops 402653184 | bytes 4718592 | tf_op jit(solution)/shard_map/input_grad/pallas_call | solution.py:230
  45.7 2.7 %collective-permute-done.5 = bf16[128,1024]{1,0:T(8,128)(2,1)S(1)} collective-permute-done((bf16[128,1024]{1,0:T(8,128)(2,1)S(1)}, bf16[128,1024]{1,0:T(8,128)(2,1)S(1)}, u32[]{:S(2)}, u32[]{:S(2)}) %collective-permute-start.5) | collective-permute-done | bytes 262176 | tf_op jit(solution)/shard_map/ppermute | solution.py:374
  48.3 0.8 %add_convert_fusion.1 = bf16[128,1024]{1,0:T(8,128)(2,1)} fusion(bf16[128,1024]{1,0:T(8,128)(2,1)S(1)} %collective-permute-done.5, f32[128,1024]{1,0:T(8,128)S(1)} %get-tuple-element.33, bf16[128,1024]{1,0:T(8,128)(2,1)S(1)} %collective-permute-done.3), kind=kLoop, calls=%fused_computation.1 | loop fusion | flops 655360 | bytes 1310720 | tf_op jit(solution)/shard_map/convert_element_type | solution.py:388
  49.1 4.4 %all-to-all-start.1 = ((bf16[8,16,1024]{2,1,0:T(8,128)(2,1)}), bf16[8,16,1024]{2,1,0:T(8,128)(2,1)S(1)}, u32[]{:S(2)}, u32[]{:S(2)}) async-start(bf16[8,16,1024]{2,1,0:T(8,128)(2,1)} %bitcast.6), calls=%async_computation.1 | async-start | bytes 524288 | tf_op jit(solution)/shard_map/all_to_all | solution.py:378
  53.6 1.6 %collective-permute-start.11 = (bf16[128,1024]{1,0:T(8,128)(2,1)S(1)}, bf16[128,1024]{1,0:T(8,128)(2,1)S(1)}, u32[]{:S(2)}, u32[]{:S(2)}) collective-permute-start(bf16[128,1024]{1,0:T(8,128)(2,1)S(1)} %add_convert_fusion), channel_id=1, source_target_pairs={{0,2},{1,3},{2,0},{3,1},{4,6},{5,7},{6,4},{7,5},{8,10},{9,11},{10,... | collective-permute-start | bytes 786440 | tf_op jit(solution)/shard_map/ppermute | solution.py:374
  55.2 6.1 %grads.1 = (bf16[4096,384]{1,0:T(8,128)(2,1)}, bf16[4096,384]{1,0:T(8,128)(2,1)}, bf16[384,4096]{1,0:T(8,128)(2,1)}) custom-call(bf16[128,1024]{1,0:T(8,128)(2,1)} %bitcast.23, bf16[128,1024]{1,0:T(8,128)(2,1)} %copy-done.6, bf16[128,1024]{1,0:T(8,128)(2,1)} %copy-done.5, bf16[128,1024]{1,0:T(8,128)(2,1)} %copy-done.7, bf16[128,1024]{1,0:T(8,128)(2,1)} %bitcast.19, ...), custom_call_target="tpu_custom_call" | custom-call | flops 1207959552 | bytes 11534336 | tf_op jit(solution)/shard_map/grads/pallas_call | solution.py:284
  61.3 0.8 %total.1 = bf16[128,1024]{1,0:T(8,128)(2,1)} custom-call(bf16[4096,384]{1,0:T(8,128)(2,1)} %get-tuple-element.47.after, f32[128,1024]{1,0:T(8,128)S(1)} %get-tuple-element.51.keep, bf16[128,1024]{1,0:T(8,128)(2,1)S(1)} %collective-permute-done.9.near, bf16[128,1024]{1,0:T(8,128)(2,1)S(1)} %collective-permute-done.11.far), custom_call_target="tpu_custom_call" | custom-call | flops 262144 | bytes 1572864 | tf_op jit(solution)/shard_map/total/pallas_call | solution.py:313
  62.1 6.0 %all-to-all-start.2 = ((bf16[8,16,1024]{2,1,0:T(8,128)(2,1)}), bf16[8,16,1024]{2,1,0:T(8,128)(2,1)S(1)}, u32[]{:S(2)}, u32[]{:S(2)}) async-start(bf16[8,16,1024]{2,1,0:T(8,128)(2,1)} %bitcast.9), calls=%async_computation.2 | async-start | bytes 524288 | tf_op jit(solution)/shard_map/all_to_all | solution.py:378
  68.1 1.1 %mix.1 = (bf16[128,1024]{1,0:T(8,128)(2,1)}, f32[8,128]{1,0:T(8,128)S(1)}) custom-call(bf16[128,1024]{1,0:T(8,128)(2,1)S(1)} %bitcast.24, bf16[128,128]{1,0:T(8,128)(2,1)S(1)} %get-tuple-element.37.w_hi, bf16[128,128]{1,0:T(8,128)(2,1)S(1)} %get-tuple-element.38.w_lo, bf16[128,128]{1,0:T(8,128)(2,1)S(1)} %get-tuple-element.39.sel, ...), custom_call_target="tpu_custom_call" | custom-call | flops 100663296 | bytes 786432 | tf_op jit(solution)/shard_map/mix/pallas_call | solution.py:341
  69.1 1.2 %collective-permute-done.12 = f32[8,128]{1,0:T(8,128)S(1)} collective-permute-done((f32[8,128]{1,0:T(8,128)S(1)}, f32[8,128]{1,0:T(8,128)S(1)}, u32[]{:S(2)}, u32[]{:S(2)}) %collective-permute-start.12) | collective-permute-done | bytes 4128 | tf_op jit(solution)/shard_map/ppermute | solution.py:374
  70.3 0.7 collective-permute-start.13
  71.0 2.9 %collective-permute-done.13 = f32[8,128]{1,0:T(8,128)S(1)} collective-permute-done((f32[8,128]{1,0:T(8,128)S(1)}, f32[8,128]{1,0:T(8,128)S(1)}, u32[]{:S(2)}, u32[]{:S(2)}) %collective-permute-start.13) | collective-permute-done | bytes 4128 | tf_op jit(solution)/shard_map/ppermute | solution.py:374
  74.5 1.8 %all-to-all-done.2 = bf16[8,16,1024]{2,1,0:T(8,128)(2,1)S(1)} async-done(((bf16[8,16,1024]{2,1,0:T(8,128)(2,1)}), bf16[8,16,1024]{2,1,0:T(8,128)(2,1)S(1)}, u32[]{:S(2)}, u32[]{:S(2)}) %all-to-all-start.2) | async-done | bytes 262176 | tf_op jit(solution)/shard_map/all_to_all | solution.py:378
  76.3 0.9 %collect.1 = bf16[128,1024]{1,0:T(8,128)(2,1)} custom-call(bf16[128,1024]{1,0:T(8,128)(2,1)S(1)} %bitcast.25, bf16[128,128]{1,0:T(8,128)(2,1)S(1)} %get-tuple-element.54.pick), custom_call_target="tpu_custom_call" | custom-call | flops 33554432 | bytes 524288 | tf_op jit(solution)/shard_map/collect/pallas_call | solution.py:362
  (50 shorter events, 2.5 us)
Async XLA Ops:
  23.7 13.7 %copy-start.2 = (bf16[8,16,1024]{2,1,0:T(8,128)(2,1)}, bf16[8,16,1024]{2,1,0:T(8,128)(2,1)S(1)}, u32[]{:S(2)}) copy-start(bf16[8,16,1024]{2,1,0:T(8,128)(2,1)S(1)} %get-tuple-element.59) | copy-start | bytes 786436
  23.8 17.9 %copy-start.1 = (bf16[8,16,1024]{2,1,0:T(8,128)(2,1)}, bf16[8,16,1024]{2,1,0:T(8,128)(2,1)S(1)}, u32[]{:S(2)}) copy-start(bf16[8,16,1024]{2,1,0:T(8,128)(2,1)S(1)} %get-tuple-element.58) | copy-start | bytes 786436
  23.8 7.0 %collective-permute-start.1 = (bf16[128,1024]{1,0:T(8,128)(2,1)S(1)}, bf16[128,1024]{1,0:T(8,128)(2,1)S(1)}, u32[]{:S(2)}, u32[]{:S(2)}) collective-permute-start(bf16[128,1024]{1,0:T(8,128)(2,1)S(1)} %bitcast.20), channel_id=1, source_target_pairs={{0,2},{1,3},{2,0},{3,1},{4,6},{5,7},{6,4},{7,5},{8,10},{9,11},{10,... | collective-permute-start | bytes 786440 | tf_op jit(solution)/shard_map/ppermute | solution.py:374
  25.4 6.9 %collective-permute-start = (bf16[128,1024]{1,0:T(8,128)(2,1)S(1)}, bf16[128,1024]{1,0:T(8,128)(2,1)S(1)}, u32[]{:S(2)}, u32[]{:S(2)}) collective-permute-start(bf16[128,1024]{1,0:T(8,128)(2,1)S(1)} %bitcast.21), channel_id=1, source_target_pairs={{0,1},{1,0},{2,3},{3,2},{4,5},{5,4},{6,7},{7,6},{8,9},{9,8},{10,11... | collective-permute-start | bytes 786440 | tf_op jit(solution)/shard_map/ppermute | solution.py:374
  30.7 6.7 %copy-start.5 = (bf16[128,1024]{1,0:T(8,128)(2,1)}, bf16[128,1024]{1,0:T(8,128)(2,1)S(1)}, u32[]{:S(2)}) copy-start(bf16[128,1024]{1,0:T(8,128)(2,1)S(1)} %collective-permute-done.1.x2.refs_2_) | copy-start | bytes 786436
  30.8 1.5 %collective-permute-start.2 = (bf16[128,1024]{1,0:T(8,128)(2,1)S(1)}, bf16[128,1024]{1,0:T(8,128)(2,1)S(1)}, u32[]{:S(2)}, u32[]{:S(2)}) collective-permute-start(bf16[128,1024]{1,0:T(8,128)(2,1)S(1)} %collective-permute-done.1.x2.refs_2_), channel_id=1, source_target_pairs={{0,1},{1,0},{2,3},{3,2},{4,5},{5,4},{6,7},{7,6},{8,9},{9,8},{10,11... | collective-permute-start | bytes 786440 | tf_op jit(solution)/shard_map/ppermute | solution.py:374
  30.8 8.7 %collective-permute-start.7 = (bf16[128,1024]{1,0:T(8,128)(2,1)S(1)}, bf16[128,1024]{1,0:T(8,128)(2,1)S(1)}, u32[]{:S(2)}, u32[]{:S(2)}) collective-permute-start(bf16[128,1024]{1,0:T(8,128)(2,1)S(1)} %bitcast.16), channel_id=1, source_target_pairs={{0,2},{1,3},{2,0},{3,1},{4,6},{5,7},{6,4},{7,5},{8,10},{9,11},{10,... | collective-permute-start | bytes 786440 | tf_op jit(solution)/shard_map/ppermute | solution.py:374
  32.3 5.2 %copy-start.6 = (bf16[128,1024]{1,0:T(8,128)(2,1)}, bf16[128,1024]{1,0:T(8,128)(2,1)S(1)}, u32[]{:S(2)}) copy-start(bf16[128,1024]{1,0:T(8,128)(2,1)S(1)} %collective-permute-done.x1.refs_1_) | copy-start | bytes 786436
  32.3 5.2 %copy-start.7 = (bf16[128,1024]{1,0:T(8,128)(2,1)}, bf16[128,1024]{1,0:T(8,128)(2,1)S(1)}, u32[]{:S(2)}) copy-start(bf16[128,1024]{1,0:T(8,128)(2,1)S(1)} %collective-permute-done.2.x3.refs_3_) | copy-start | bytes 786436
  37.5 6.4 %copy-start.12 = (bf16[128,384]{1,0:T(8,128)(2,1)}, bf16[128,384]{1,0:T(8,128)(2,1)S(1)}, u32[]{:S(2)}) copy-start(bf16[128,384]{1,0:T(8,128)(2,1)S(1)} %get-tuple-element.41.refs_8_) | copy-start | bytes 294916
  37.5 2.5 %collective-permute-start.4 = (bf16[128,1024]{1,0:T(8,128)(2,1)S(1)}, bf16[128,1024]{1,0:T(8,128)(2,1)S(1)}, u32[]{:S(2)}, u32[]{:S(2)}) collective-permute-start(bf16[128,1024]{1,0:T(8,128)(2,1)S(1)} %get-tuple-element.36), channel_id=1, source_target_pairs={{0,1},{1,0},{2,3},{3,2},{4,5},{5,4},{6,7},{7,6},{8,9},{9,8},{10,11... | collective-permute-start | bytes 786440 | tf_op jit(solution)/shard_map/ppermute | solution.py:374
  37.8 3.8 %collective-permute-start.6 = (bf16[128,1024]{1,0:T(8,128)(2,1)S(1)}, bf16[128,1024]{1,0:T(8,128)(2,1)S(1)}, u32[]{:S(2)}, u32[]{:S(2)}) collective-permute-start(bf16[128,1024]{1,0:T(8,128)(2,1)S(1)} %bitcast.17), channel_id=1, source_target_pairs={{0,1},{1,0},{2,3},{3,2},{4,5},{5,4},{6,7},{7,6},{8,9},{9,8},{10,11... | collective-permute-start | bytes 786440 | tf_op jit(solution)/shard_map/ppermute | solution.py:374
  39.5 2.2 %collective-permute-start.8 = (bf16[128,1024]{1,0:T(8,128)(2,1)S(1)}, bf16[128,1024]{1,0:T(8,128)(2,1)S(1)}, u32[]{:S(2)}, u32[]{:S(2)}) collective-permute-start(bf16[128,1024]{1,0:T(8,128)(2,1)S(1)} %collective-permute-done.7.d2.refs_6_), channel_id=1, source_target_pairs={{0,1},{1,0},{2,3},{3,2},{4,5},{5,4},{6,7},{7,6},{8,9},{9,8},{10,11... | collective-permute-start | bytes 786440 | tf_op jit(solution)/shard_map/ppermute | solution.py:374
  39.5 6.2 %collective-permute-start.3 = (bf16[128,1024]{1,0:T(8,128)(2,1)S(1)}, bf16[128,1024]{1,0:T(8,128)(2,1)S(1)}, u32[]{:S(2)}, u32[]{:S(2)}) collective-permute-start(bf16[128,1024]{1,0:T(8,128)(2,1)S(1)} %get-tuple-element.34), channel_id=1, source_target_pairs={{0,1},{1,0},{2,3},{3,2},{4,5},{5,4},{6,7},{7,6},{8,9},{9,8},{10,11... | collective-permute-start | bytes 786440 | tf_op jit(solution)/shard_map/ppermute | solution.py:374
  40.0 8.3 %collective-permute-start.5 = (bf16[128,1024]{1,0:T(8,128)(2,1)S(1)}, bf16[128,1024]{1,0:T(8,128)(2,1)S(1)}, u32[]{:S(2)}, u32[]{:S(2)}) collective-permute-start(bf16[128,1024]{1,0:T(8,128)(2,1)S(1)} %add_convert_fusion.2.after), channel_id=1, source_target_pairs={{0,2},{1,3},{2,0},{3,1},{4,6},{5,7},{6,4},{7,5},{8,10},{9,11},{10,... | collective-permute-start | bytes 786440 | tf_op jit(solution)/shard_map/ppermute | solution.py:374
  43.9 9.6 %collective-permute-start.10 = (bf16[128,1024]{1,0:T(8,128)(2,1)S(1)}, bf16[128,1024]{1,0:T(8,128)(2,1)S(1)}, u32[]{:S(2)}, u32[]{:S(2)}) collective-permute-start(bf16[128,1024]{1,0:T(8,128)(2,1)S(1)} %get-tuple-element.50.after), channel_id=1, source_target_pairs={{0,1},{1,0},{2,3},{3,2},{4,5},{5,4},{6,7},{7,6},{8,9},{9,8},{10,11... | collective-permute-start | bytes 786440 | tf_op jit(solution)/shard_map/ppermute | solution.py:374
  45.1 16.1 %collective-permute-start.9 = (bf16[128,1024]{1,0:T(8,128)(2,1)S(1)}, bf16[128,1024]{1,0:T(8,128)(2,1)S(1)}, u32[]{:S(2)}, u32[]{:S(2)}) collective-permute-start(bf16[128,1024]{1,0:T(8,128)(2,1)S(1)} %get-tuple-element.52), channel_id=1, source_target_pairs={{0,1},{1,0},{2,3},{3,2},{4,5},{5,4},{6,7},{7,6},{8,9},{9,8},{10,11... | collective-permute-start | bytes 786440 | tf_op jit(solution)/shard_map/ppermute | solution.py:374
  49.1 12.9 %all-to-all-start.1 = ((bf16[8,16,1024]{2,1,0:T(8,128)(2,1)}), bf16[8,16,1024]{2,1,0:T(8,128)(2,1)S(1)}, u32[]{:S(2)}, u32[]{:S(2)}) async-start(bf16[8,16,1024]{2,1,0:T(8,128)(2,1)} %bitcast.6), calls=%async_computation.1 | async-start | bytes 524288 | tf_op jit(solution)/shard_map/all_to_all | solution.py:378
  53.6 7.7 %collective-permute-start.11 = (bf16[128,1024]{1,0:T(8,128)(2,1)S(1)}, bf16[128,1024]{1,0:T(8,128)(2,1)S(1)}, u32[]{:S(2)}, u32[]{:S(2)}) collective-permute-start(bf16[128,1024]{1,0:T(8,128)(2,1)S(1)} %add_convert_fusion), channel_id=1, source_target_pairs={{0,2},{1,3},{2,0},{3,1},{4,6},{5,7},{6,4},{7,5},{8,10},{9,11},{10,... | collective-permute-start | bytes 786440 | tf_op jit(solution)/shard_map/ppermute | solution.py:374
  61.2 6.8 %copy-start = (bf16[128,1024]{1,0:T(8,128)(2,1)S(1)}, bf16[128,1024]{1,0:T(8,128)(2,1)}, u32[]{:S(2)}) copy-start(bf16[128,1024]{1,0:T(8,128)(2,1)} %d_out.1) | copy-start | bytes 786436
  61.2 6.8 %copy-start.11 = (s32[128,8]{0,1:T(8,128)S(1)}, s32[128,8]{0,1:T(8,128)}, u32[]{:S(2)}) copy-start(s32[128,8]{0,1:T(8,128)} %param.8) | copy-start | bytes 12292
  62.1 14.2 %all-to-all-start.2 = ((bf16[8,16,1024]{2,1,0:T(8,128)(2,1)}), bf16[8,16,1024]{2,1,0:T(8,128)(2,1)S(1)}, u32[]{:S(2)}, u32[]{:S(2)}) async-start(bf16[8,16,1024]{2,1,0:T(8,128)(2,1)} %bitcast.9), calls=%async_computation.2 | async-start | bytes 524288 | tf_op jit(solution)/shard_map/all_to_all | solution.py:378
  69.1 1.2 %collective-permute-start.12 = (f32[8,128]{1,0:T(8,128)S(1)}, f32[8,128]{1,0:T(8,128)S(1)}, u32[]{:S(2)}, u32[]{:S(2)}) collective-permute-start(f32[8,128]{1,0:T(8,128)S(1)} %get-tuple-element.55), channel_id=1, source_target_pairs={{0,1},{1,0},{2,3},{3,2},{4,5},{5,4},{6,7},{7,6},{8,9},{9,8},{10,11... | collective-permute-start | bytes 12296 | tf_op jit(solution)/shard_map/ppermute | solution.py:374
  70.3 3.6 %collective-permute-start.13 = (f32[8,128]{1,0:T(8,128)S(1)}, f32[8,128]{1,0:T(8,128)S(1)}, u32[]{:S(2)}, u32[]{:S(2)}) collective-permute-start(f32[8,128]{1,0:T(8,128)S(1)} %add.22), channel_id=1, source_target_pairs={{0,2},{1,3},{2,0},{3,1},{4,6},{5,7},{6,4},{7,5},{8,10},{9,11},{10,... | collective-permute-start | bytes 12296 | tf_op jit(solution)/shard_map/ppermute | solution.py:374
  (5 other events, 11.5 us)

commit v3 on v2

v3 whole, which is shorter than its diff:
```python
import functools

import jax
import jax.numpy as jnp
from jax import lax
from jax.experimental import pallas as pl
from jax.experimental.pallas import tpu as pltpu
from jax.sharding import PartitionSpec as P

CAP = 16
F32 = jnp.float32
BF16 = jnp.bfloat16
NN = (((1,), (0,)), ((), ()))
NT = (((1,), (1,)), ((), ()))
TN = (((0,), (0,)), ((), ()))


def dot(a, b, dims=NN):
    return lax.dot_general(a, b, dims, preferred_element_type=F32)


def params(mib=16):
    return pltpu.CompilerParams(vmem_limit_bytes=mib * 1024 * 1024)


def cost(flops, nbytes):
    return pl.CostEstimate(flops=flops, bytes_accessed=nbytes, transcendentals=0)


def vspec():
    return pl.BlockSpec(memory_space=pltpu.VMEM)


def hspec():
    return pl.BlockSpec(memory_space=pltpu.HBM)


def aspec():
    return pl.BlockSpec(memory_space=pl.ANY)


def fixed(x):
    return pltpu.with_memory_space_constraint(x, pltpu.HBM)


def step(place, count):
    return (count - place) & (count - 1)


def relative(experts, topk, tok):
    place = lax.broadcasted_iota(jnp.int32, (experts, topk, tok), 0)
    return step(place, experts) ^ lax.axis_index("ctx")


def dispatch_kernel(experts, *refs):
    routes_in, gates_in, tokens_in, d_in = refs[:4]
    outs = refs[4 : 4 + experts]
    sel, pick, w_hi, w_lo, routes, gates, tokens, d_out, sem = refs[4 + experts :]
    topk, tok = routes.shape
    slots = experts * CAP
    loads = [
        pltpu.make_async_copy(src, dst, sem.at[i])
        for i, (src, dst) in enumerate(
            ((routes_in, routes), (gates_in, gates), (tokens_in, tokens), (d_in, d_out))
        )
    ]
    for load in loads:
        load.start()
    loads[0].wait()
    loads[1].wait()
    match = routes[...][None] == relative(experts, topk, tok)
    hit = jnp.sum(jnp.where(match, 1.0, 0.0), axis=1)
    gate = jnp.sum(jnp.where(match, gates[...][None], 0.0), axis=1)
    earlier = lax.broadcasted_iota(jnp.int32, (tok, tok), 0) < lax.broadcasted_iota(
        jnp.int32, (tok, tok), 1
    )
    before = dot(hit.astype(BF16), jnp.where(earlier, 1.0, 0.0).astype(BF16))
    place = jnp.where(hit > 0.0, before, -1.0)[:, None, :]
    row = lax.broadcasted_iota(jnp.int32, (experts, CAP, tok), 1).astype(F32)
    chosen = jnp.where(place == row, 1.0, 0.0)
    weight = (chosen * gate[:, None, :]).reshape(slots, tok)
    chosen = chosen.reshape(slots, tok)
    select = chosen.astype(BF16)
    loads[2].wait()
    x = dot(select, tokens[...]).astype(BF16)
    slot_gate = jnp.sum(weight, axis=1, keepdims=True)
    loads[3].wait()
    d = (slot_gate * dot(select, d_out[...])).astype(BF16)
    for e, out in enumerate(outs):
        out[:CAP] = x[e * CAP : (e + 1) * CAP]
        out[CAP:] = d[e * CAP : (e + 1) * CAP]
    sel[...] = select
    pick[...] = chosen.T.astype(BF16)
    back = weight.T
    high = back.astype(BF16)
    w_hi[...] = high
    w_lo[...] = (back - high.astype(F32)).astype(BF16)


def dispatch(routes_t, gates_t, tokens, d_out, experts):
    tok, quarter = tokens.shape
    slots = experts * CAP
    results = pl.pallas_call(
        functools.partial(dispatch_kernel, experts),
        out_shape=(jax.ShapeDtypeStruct((2 * CAP, quarter), BF16),) * experts
        + (
            jax.ShapeDtypeStruct((slots, tok), BF16),
            jax.ShapeDtypeStruct((tok, slots), BF16),
            jax.ShapeDtypeStruct((tok, slots), BF16),
            jax.ShapeDtypeStruct((tok, slots), BF16),
        ),
        in_specs=[hspec()] * 4,
        out_specs=(vspec(),) * (experts + 4),
        scratch_shapes=[
            pltpu.VMEM(routes_t.shape, jnp.int32),
            pltpu.VMEM(gates_t.shape, F32),
            pltpu.VMEM(tokens.shape, BF16),
            pltpu.VMEM(d_out.shape, BF16),
            pltpu.SemaphoreType.DMA((4,)),
        ],
        compiler_params=params(),
        cost_estimate=cost(4 * slots * tok * quarter, 8 * tok * quarter),
        name="dispatch",
    )(*(fixed(v) for v in (routes_t, gates_t, tokens, d_out)))
    return results[:experts], results[experts:]


def quarter_of(me, flip, size):
    return pl.ds(pl.multiple_of((me ^ flip) * size, size), size)


def fetch(src, dst, sem, part):
    copy = pltpu.make_async_copy(src.at[part], dst.at[part], sem)
    copy.start()
    return copy


def load_kernel(after, wg, wu, wd, vg, vu, vd, sem):
    rows = wg.shape[0] // 4
    copies = []
    for i in range(4):
        part = (pl.ds(i * rows, rows), slice(None))
        cols = (slice(None), pl.ds(i * rows, rows))
        copies.append(fetch(wg, vg, sem.at[0, i], part))
        copies.append(fetch(wu, vu, sem.at[1, i], part))
        copies.append(fetch(wd, vd, sem.at[2, i], cols))
    for copy in copies:
        copy.wait()


def load(after, *weights):
    return pl.pallas_call(
        load_kernel,
        out_shape=tuple(jax.ShapeDtypeStruct(w.shape, w.dtype) for w in weights),
        in_specs=[aspec()] + [hspec()] * 3,
        out_specs=(vspec(),) * 3,
        scratch_shapes=[pltpu.SemaphoreType.DMA((3, 4))],
        compiler_params=params(4),
        cost_estimate=cost(0, 0),
        name="load",
    )(after, *(fixed(w) for w in weights))


def pass_kernel(after, x, out):
    out[...] = x[...]


def pass_on(after, x):
    return pl.pallas_call(
        pass_kernel,
        out_shape=jax.ShapeDtypeStruct(x.shape, x.dtype),
        in_specs=[aspec(), vspec()],
        out_specs=vspec(),
        compiler_params=params(4),
        cost_estimate=cost(0, 0),
        name="pass_on",
    )(after, x)


def forward_kernel(
    x0, x1, x2, x3, vg, vu, vd, act, lin, hidden, send_far, send_near, keep_far, keep_own
):
    me = lax.axis_index("tp")
    size = x0.shape[1]
    xs = (x0, x1, x2, x3)
    a = b = None
    for i in range(4):
        part = quarter_of(me, i, size)
        x = xs[i][...]
        pa = dot(x, vg[part, :])
        pb = dot(x, vu[part, :])
        a = pa if a is None else a + pa
        b = pb if b is None else b + pb
    act[...] = a
    lin[...] = b
    h = (a * jax.nn.sigmoid(a) * b).astype(BF16)
    hidden[...] = h
    for i, out in ((3, send_far), (2, keep_far), (1, send_near), (0, keep_own)):
        out[...] = dot(h, vd[:, quarter_of(me, i, size)]).astype(out.dtype)


def forward(xs, vg, vu, vd):
    rows, size = xs[0].shape
    d, ff = vg.shape
    return pl.pallas_call(
        forward_kernel,
        out_shape=(
            jax.ShapeDtypeStruct((rows, ff), F32),
            jax.ShapeDtypeStruct((rows, ff), F32),
            jax.ShapeDtypeStruct((rows, ff), BF16),
            jax.ShapeDtypeStruct((rows, size), BF16),
            jax.ShapeDtypeStruct((rows, size), BF16),
            jax.ShapeDtypeStruct((rows, size), F32),
            jax.ShapeDtypeStruct((rows, size), F32),
        ),
        in_specs=[vspec()] * 7,
        out_specs=(vspec(),) * 7,
        compiler_params=params(),
        cost_estimate=cost(0, 0),
        name="forward",
    )(*xs, vg, vu, vd)


def hidden_grad_kernel(d0, d1, d2, d3, act, lin, hidden, vd, dact, dlin, dots):
    me = lax.axis_index("tp")
    rows, size = d0.shape
    ds = (d0, d1, d2, d3)
    dhid = None
    for i in range(4):
        p = dot(ds[i][...], vd[:, quarter_of(me, i, size)], NT)
        dhid = p if dhid is None else dhid + p
    a = act[...]
    s = jax.nn.sigmoid(a)
    dlin[...] = (dhid * (a * s)).astype(BF16)
    dact[...] = (dhid * lin[...] * s * (1.0 + a * (1.0 - s))).astype(BF16)
    per_row = jnp.sum(dhid * hidden[...].astype(F32), axis=1, keepdims=True)
    dots[...] = jnp.broadcast_to(per_row, (rows, 128)).T[:8]


def hidden_grad(ds, act, lin, hidden, vd):
    rows, size = ds[0].shape
    ff, d = vd.shape
    return pl.pallas_call(
        hidden_grad_kernel,
        out_shape=(
            jax.ShapeDtypeStruct((rows, ff), BF16),
            jax.ShapeDtypeStruct((rows, ff), BF16),
            jax.ShapeDtypeStruct((8, rows), F32),
        ),
        in_specs=[vspec()] * 8,
        out_specs=(vspec(),) * 3,
        compiler_params=params(),
        cost_estimate=cost(0, 0),
        name="hidden_grad",
    )(*ds, act, lin, hidden, vd)


def input_grad_kernel(flips, after, dact, dlin, vg, vu, send, keep):
    me = lax.axis_index("tp")
    size = send.shape[1]
    da = dact[...]
    dl = dlin[...]
    for i, out in zip(flips, (send, keep)):
        part = quarter_of(me, i, size)
        p = dot(da, vg[part, :], NT) + dot(dl, vu[part, :], NT)
        out[...] = p.astype(out.dtype)


def input_grad(flips, after, dact, dlin, vg, vu):
    rows, ff = dact.shape
    d = vg.shape[0]
    return pl.pallas_call(
        functools.partial(input_grad_kernel, flips),
        out_shape=(
            jax.ShapeDtypeStruct((rows, d // 4), BF16),
            jax.ShapeDtypeStruct((rows, d // 4), F32),
        ),
        in_specs=[aspec()] + [vspec()] * 4,
        out_specs=(vspec(),) * 2,
        compiler_params=params(),
        cost_estimate=cost(0, 0),
        name="input_grad",
    )(after, dact, dlin, vg, vu)


def grads_kernel(*refs):
    given, (gg, gu, gd), held, (vg, vu, vd, sem, load_sem) = (
        refs[:11],
        refs[11:14],
        refs[14:25],
        refs[25:],
    )
    me = lax.axis_index("tp")
    size = given[0].shape[1]
    loads = [
        pltpu.make_async_copy(src, dst, load_sem.at[i])
        for i, (src, dst) in enumerate(zip(given, held))
    ]
    for i in (8, 9, 10, 0, 4, 1, 5, 2, 6, 3, 7):
        loads[i].start()
    for i in (8, 9, 10):
        loads[i].wait()
    h, da, dl = (held[i][...] for i in (8, 9, 10))
    stores = []
    for i in range(4):
        part = quarter_of(me, i, size)
        rows = (part, slice(None))
        cols = (slice(None), part)
        loads[i].wait()
        x = held[i][...]
        vg[part, :] = dot(x, da, TN).astype(BF16)
        stores.append(fetch(vg, gg, sem.at[0, i], rows))
        vu[part, :] = dot(x, dl, TN).astype(BF16)
        stores.append(fetch(vu, gu, sem.at[1, i], rows))
        loads[4 + i].wait()
        vd[:, part] = dot(h, held[4 + i][...], TN).astype(BF16)
        stores.append(fetch(vd, gd, sem.at[2, i], cols))
    for store in stores:
        store.wait()


def grads(xs, ds, hidden, dact, dlin):
    rows, size = xs[0].shape
    ff = hidden.shape[1]
    d = 4 * size
    return pl.pallas_call(
        grads_kernel,
        out_shape=(
            jax.ShapeDtypeStruct((d, ff), BF16),
            jax.ShapeDtypeStruct((d, ff), BF16),
            jax.ShapeDtypeStruct((ff, d), BF16),
        ),
        in_specs=[hspec()] * 11,
        out_specs=(hspec(),) * 3,
        scratch_shapes=[pltpu.VMEM((rows, size), BF16)] * 8
        + [pltpu.VMEM((rows, ff), BF16)] * 3
        + [
            pltpu.VMEM((d, ff), BF16),
            pltpu.VMEM((d, ff), BF16),
            pltpu.VMEM((ff, d), BF16),
            pltpu.SemaphoreType.DMA((3, 4)),
            pltpu.SemaphoreType.DMA((11,)),
        ],
        compiler_params=params(32),
        cost_estimate=cost(6 * rows * d * ff, 6 * d * ff),
        name="grads",
    )(*(fixed(v) for v in (*xs, *ds, hidden, dact, dlin)))


def total_kernel(after, o_keep, o_near, o_far, x_keep, x_near, x_far, dots, *outs):
    tiles, cap, lanes = outs[0].shape
    rows, size = o_keep.shape
    half = tiles // 2

    def place(at, value):
        value = value.astype(BF16)
        for e, out in enumerate(outs):
            out[at] = value[e * cap : (e + 1) * cap]

    for j in range(half):
        part = slice(j * lanes, (j + 1) * lanes)
        for base, (keep, near, far) in ((0, (o_keep, o_near, o_far)), (half, (x_keep, x_near, x_far))):
            place(base + j, keep[:, part] + near[:, part].astype(F32) + far[:, part].astype(F32))
    d = jnp.broadcast_to(dots[:1], (lanes, rows)).T
    high = d.astype(BF16).astype(F32)
    first = lax.broadcasted_iota(jnp.int32, (rows, lanes), 1) < lanes // 2
    place(tiles - 1, jnp.where(first, high, d - high))


def total(after, out_parts, dx_parts, dots):
    rows, size = out_parts[0].shape
    tiles = 2 * (size // 128) + 1
    count = rows // CAP
    return pl.pallas_call(
        total_kernel,
        out_shape=(jax.ShapeDtypeStruct((tiles, CAP, 128), BF16),) * count,
        in_specs=[aspec()] + [vspec()] * 7,
        out_specs=(vspec(),) * count,
        compiler_params=params(),
        cost_estimate=cost(0, 0),
        name="total",
    )(fixed(after), *out_parts, *dx_parts, dots)


def combine_kernel(*refs):
    w_hi, w_lo, pick, sel, routes, gates = refs[:6]
    back = refs[6:-3]
    mixed, d_tokens, d_gates = refs[-3:]
    tiles, cap, lanes = back[0].shape
    slots, tok = sel.shape
    topk = routes.shape[0]
    experts = len(back)
    half = tiles // 2

    def rows_of(first):
        return jnp.concatenate(
            [jnp.concatenate([b[first + j] for j in range(half)], axis=1) for b in back], axis=0
        )

    o = rows_of(0)
    mixed[...] = (dot(w_hi[...], o) + dot(w_lo[...], o)).astype(BF16)
    d_tokens[...] = dot(pick[...], rows_of(half)).astype(BF16)
    both = jnp.concatenate([b[tiles - 1] for b in back], axis=0).astype(F32)
    per_slot = both[:, :1] + both[:, lanes // 2 : lanes // 2 + 1]
    spread = sel[...].astype(F32) * per_slot
    per_expert = jnp.sum(spread.reshape(experts, cap, tok), axis=1)
    match = routes[...][None] == relative(experts, topk, tok)
    scaled = jnp.sum(jnp.where(match, per_expert[:, None, :], 0.0), axis=0)
    d_gates[...] = scaled / gates[...]


def combine(back, w_hi, w_lo, pick, sel, routes_t, gates_t):
    quarter = back[0].shape[0] // 2 * 128
    topk, tok = routes_t.shape
    return pl.pallas_call(
        combine_kernel,
        out_shape=(
            jax.ShapeDtypeStruct((tok, quarter), BF16),
            jax.ShapeDtypeStruct((tok, quarter), BF16),
            jax.ShapeDtypeStruct((topk, tok), F32),
        ),
        in_specs=[vspec()] * (6 + len(back)),
        out_specs=(vspec(),) * 3,
        compiler_params=params(),
        cost_estimate=cost(0, 0),
        name="combine",
    )(w_hi, w_lo, pick, sel, routes_t, gates_t, *back)


def swap(x, flip):
    return lax.ppermute(x, "tp", [(i, i ^ flip) for i in range(4)])


def exchange(parts):
    count = len(parts)
    assert count & (count - 1) == 0
    return [parts[0]] + [
        lax.ppermute(parts[p], "ctx", [(i, i ^ step(p, count)) for i in range(count)])
        for p in range(1, count)
    ]


def gather(own):
    near = swap(own, 1)
    far = swap(own, 2)
    return (own, near, far, swap(far, 1))


def plus(keep, *others):
    return sum((o.astype(F32) for o in others), keep).astype(BF16)


def on_device(tokens, routes, gates, w_gate, w_up, w_down, d_out):
    tok, quarter = tokens.shape
    sources = lax.axis_size("ctx")
    experts = sources * w_gate.shape[0]
    slots = experts * CAP
    rows = sources * CAP
    routes_t = routes.T
    gates_t = gates.T
    outgoing, (sel, pick, w_hi, w_lo) = dispatch(routes_t, gates_t, tokens, d_out, experts)
    arrived = exchange(outgoing)
    x0 = jnp.concatenate([part[:CAP] for part in arrived], axis=0)
    x2 = swap(x0, 2)
    dq = gather(jnp.concatenate([part[CAP:] for part in arrived], axis=0))
    vg, vu, vd = load(x0, w_gate[0], w_up[0], w_down[0])
    xq = (x0, swap(x0, 1), x2, swap(pass_on(vg, x2), 1))
    act, lin, hidden, send_far, send_near, keep_far, keep_own = forward(xq, vg, vu, vd)
    half_out = plus(keep_far, swap(send_far, 1))
    near_out = swap(send_near, 1)
    dact, dlin, dots = hidden_grad(dq, act, lin, hidden, vd)
    send_dx_far, keep_dx_far = input_grad((3, 2), half_out, dact, dlin, vg, vu)
    far_out = swap(half_out, 2)
    half_dx = plus(keep_dx_far, swap(send_dx_far, 1))
    send_dx_near, keep_dx_own = input_grad((1, 0), send_dx_far, dact, dlin, vg, vu)
    far_dx = swap(half_dx, 2)
    near_dx = swap(send_dx_near, 1)
    dots = dots + swap(dots, 1)
    dots = dots + swap(dots, 2)
    grad_gate, grad_up, grad_down = grads(xq, dq, hidden, dact, dlin)
    back = exchange(
        total(grad_gate, (keep_own, near_out, far_out), (keep_dx_own, near_dx, far_dx), dots)
    )
    mixed, d_tokens, d_gates = combine(back, w_hi, w_lo, pick, sel, routes_t, gates_t)
    return (mixed, d_tokens, d_gates.T, grad_gate[None], grad_up[None], grad_down[None])


def solution(mesh):
    placed = (
        P("ctx", "tp"),
        P("ctx", None),
        P("ctx", None),
        P("ctx", None, "tp"),
        P("ctx", None, "tp"),
        P("ctx", "tp", None),
        P("ctx", "tp"),
    )
    return jax.shard_map(
        on_device,
        mesh=mesh,
        in_specs=placed,
        out_specs=(
            P("ctx", "tp"),
            P("ctx", "tp"),
            P("ctx", None),
            P("ctx", None, "tp"),
            P("ctx", None, "tp"),
            P("ctx", "tp", None),
        ),
        check_vma=False,
    )
```

time: 77.6 us -> 70.2 us (0.905)
  blocking collectives: 21.6 us -> 0 us
  starting transfers between devices: 19 us -> 32.1 us
  waiting for transfers between devices: 15.3 us -> 18.7 us
  other arithmetic: 1.5 us -> 0.13 us
    ppermute x0 -> x14, starting transfers between devices: none -> 24.4 us  [exchange(): lax.ppermute(parts[p], 'ctx', [(i, i ^ step(p, count)) for i in range(cou...]
    all_to_all x1 -> x0, blocking collectives: 21.6 us -> none  [exchange(): return lax.all_to_all(x, 'ctx', split_axis=0, concat_axis=0, tiled=True)]
    all_to_all x2 -> x0, starting transfers between devices: 10.4 us -> none  [exchange(): return lax.all_to_all(x, 'ctx', split_axis=0, concat_axis=0, tiled=True)]
    ppermute x0 -> x14, waiting for transfers between devices: none -> 9.32 us  [exchange(): lax.ppermute(parts[p], 'ctx', [(i, i ^ step(p, count)) for i in range(cou...]
    ppermute x14, waiting for transfers between devices: 13.6 us -> 9.34 us  [swap(): return lax.ppermute(x, 'tp', [(i, i ^ flip) for i in range(4)])]
    pallas_call x1, Pallas kernels: 5.15 us -> 1.93 us  [forward(): pl.pallas_call(forward_kernel, out_shape=(jax.ShapeDtypeStruct((rows, ff)...]
    pallas_call x4 -> x5, Pallas kernels: 4.23 us -> 6.66 us  [the longest x1 3.8 us: load(): pl.pallas_call(load_kernel, out_shape=tuple((jax.ShapeDtypeStruct(w.shape...]
    all_to_all x2 -> x0, waiting for transfers between devices: 1.78 us -> none  [exchange(): return lax.all_to_all(x, 'ctx', split_axis=0, concat_axis=0, tiled=True)]
  transfers between devices with their start and end apart: 16 -> 28, of which waited for: 6 -> 12; matrix products, arithmetic and copies ran while one was open for 2% -> 0% of each run, Pallas kernels for 21% -> 20%
where the time goes in v3:
time: 70.2 us; the launch traced here: 70 us
  starting transfers between devices  32.1 us (46%)
  waiting for transfers between devices  18.7 us (27%)
  Pallas kernels  18.1 us (26%)
  between operations  0.94 us (1%)
    ppermute x14, starting transfers between devices, exchange(): lax.ppermute(parts[p], 'ctx', [(i, i ^ step(p, count)) for i in range(cou...  24.4 us
    ppermute x14, waiting for transfers between devices, swap(): return lax.ppermute(x, 'tp', [(i, i ^ flip) for i in range(4)])  9.34 us
    ppermute x14, waiting for transfers between devices, exchange(): lax.ppermute(parts[p], 'ctx', [(i, i ^ step(p, count)) for i in range(cou...  9.32 us
    ppermute x14, starting transfers between devices, swap(): return lax.ppermute(x, 'tp', [(i, i ^ flip) for i in range(4)])  7.68 us
    pallas_call x1, Pallas kernels, grads(): pl.pallas_call(grads_kernel, out_shape=(jax.ShapeDtypeStruct((d, ff), BF1...  6.08 us
    pallas_call x1, Pallas kernels, load(): pl.pallas_call(load_kernel, out_shape=tuple((jax.ShapeDtypeStruct(w.shape...  3.8 us
    pallas_call x2, Pallas kernels, input_grad(): pl.pallas_call(functools.partial(input_grad_kernel, flips), out_shape=(ja...  2.19 us
    pallas_call x1, Pallas kernels, forward(): pl.pallas_call(forward_kernel, out_shape=(jax.ShapeDtypeStruct((rows, ff)...  1.93 us
  transfers between devices with their start and end apart: 28, of which 12 were waited for; matrix products, arithmetic and copies ran while one was open for 0% of the time, Pallas kernels for 20%

profile of v3, /device:TPU:0, one launch (start us, length us, event | category | flops | bytes accessed | tf_op | source)
XLA Modules:
  0.0 70.0 jit_solution(9716969198712863197)
XLA Ops:
  0.6 1.5 %dispatch.1 = (bf16[32,1024]{1,0:T(8,128)(2,1)S(1)}, bf16[32,1024]{1,0:T(8,128)(2,1)S(1)}, bf16[32,1024]{1,0:T(8,128)(2,1)S(1)}, bf16[32,1024]{1,0:T(8,128)(2,1)...) custom-call(s32[8,128]{1,0:T(8,128)} %bitcast.9, ...), custom_call_target="tpu_custom_call" | custom-call | flops 67108864 | bytes 1048576 | tf_op jit(solution)/shard_map/dispatch/pallas_call | solution.py:103
  2.1 6.0 %collective-permute-start = (bf16[32,1024]{1,0:T(8,128)(2,1)S(1)}, bf16[32,1024]{1,0:T(8,128)(2,1)S(1)}, u32[]{:S(2)}, u32[]{:S(2)}) collective-permute-start(bf16[32,1024]{1,0:T(8,128)(2,1)S(1)} %get-tuple-element.54), channel_id=1, source_target_pairs={{0,28},{4,24},{8,20},{12,16},{16,12},{20,8},{24,4},{28,0},{1,29},{... | collective-permute-start | bytes 196616 | tf_op jit(solution)/shard_map/ppermute | solution.py:438
  9.2 2.0 %collective-permute-start.3 = (bf16[32,1024]{1,0:T(8,128)(2,1)S(1)}, bf16[32,1024]{1,0:T(8,128)(2,1)S(1)}, u32[]{:S(2)}, u32[]{:S(2)}) collective-permute-start(bf16[32,1024]{1,0:T(8,128)(2,1)S(1)} %get-tuple-element.57), channel_id=1, source_target_pairs={{0,16},{4,20},{8,24},{12,28},{16,0},{20,4},{24,8},{28,12},{1,17},{... | collective-permute-start | bytes 196616 | tf_op jit(solution)/shard_map/ppermute | solution.py:438
  11.2 2.3 %collective-permute-start.4 = (bf16[32,1024]{1,0:T(8,128)(2,1)S(1)}, bf16[32,1024]{1,0:T(8,128)(2,1)S(1)}, u32[]{:S(2)}, u32[]{:S(2)}) collective-permute-start(bf16[32,1024]{1,0:T(8,128)(2,1)S(1)} %get-tuple-element.58), channel_id=1, source_target_pairs={{0,12},{4,8},{8,4},{12,0},{16,28},{20,24},{24,20},{28,16},{1,13},{... | collective-permute-start | bytes 196616 | tf_op jit(solution)/shard_map/ppermute | solution.py:438
  14.9 2.8 %collective-permute-done.2 = bf16[32,1024]{1,0:T(8,128)(2,1)S(1)} collective-permute-done((bf16[32,1024]{1,0:T(8,128)(2,1)S(1)}, bf16[32,1024]{1,0:T(8,128)(2,1)S(1)}, u32[]{:S(2)}, u32[]{:S(2)}) %collective-permute-start.2) | collective-permute-done | bytes 65568 | tf_op jit(solution)/shard_map/ppermute | solution.py:438
  17.8 1.6 %collective-permute-done.3 = bf16[32,1024]{1,0:T(8,128)(2,1)S(1)} collective-permute-done((bf16[32,1024]{1,0:T(8,128)(2,1)S(1)}, bf16[32,1024]{1,0:T(8,128)(2,1)S(1)}, u32[]{:S(2)}, u32[]{:S(2)}) %collective-permute-start.3) | collective-permute-done | bytes 65568 | tf_op jit(solution)/shard_map/ppermute | solution.py:438
  19.9 1.6 %collective-permute-start.8 = (bf16[128,1024]{1,0:T(8,128)(2,1)S(1)}, bf16[128,1024]{1,0:T(8,128)(2,1)S(1)}, u32[]{:S(2)}, u32[]{:S(2)}) collective-permute-start(bf16[128,1024]{1,0:T(8,128)(2,1)S(1)} %get-tuple-element.93.after.x0.refs_0_), channel_id=1, source_target_pairs={{0,2},{1,3},{2,0},{3,1},{4,6},{5,7},{6,4},{7,5},{8,10},{9,11},{10,... | collective-permute-start | bytes 786440 | tf_op jit(solution)/shard_map/ppermute | solution.py:431
  22.0 3.8 %load.1 = (bf16[4096,384]{1,0:T(8,128)(2,1)S(1)}, bf16[4096,384]{1,0:T(8,128)(2,1)S(1)}, bf16[384,4096]{1,0:T(8,128)(2,1)S(1)}) custom-call(bf16[128,1024]{1,0:T(8,128)(2,1)S(1)} %get-tuple-element.93.after.x0.refs_0_, bf16[4096,384]{1,0:T(8,128)(2,1)} %bitcast.14, bf16[4096,384]{1,0:T(8,128)(2,1)} %bitcast.15, bf16[384,4096]{1,0:T(8,128)(2,1)} %bitcast.16), custom_call_target="tpu_custom_call" | custom-call | tf_op jit(solution)/shard_map/load/pallas_call | solution.py:152
  25.8 3.4 %collective-permute-done.8.x.x2.refs_2_ = bf16[128,1024]{1,0:T(8,128)(2,1)S(1)} collective-permute-done((bf16[128,1024]{1,0:T(8,128)(2,1)S(1)}, bf16[128,1024]{1,0:T(8,128)(2,1)S(1)}, u32[]{:S(2)}, u32[]{:S(2)}) %collective-permute-start.8) | collective-permute-done | bytes 262176 | tf_op jit(solution)/shard_map/ppermute | solution.py:431
  29.8 2.9 %collective-permute-done.11.d2.refs_6_ = bf16[128,1024]{1,0:T(8,128)(2,1)S(1)} collective-permute-done((bf16[128,1024]{1,0:T(8,128)(2,1)S(1)}, bf16[128,1024]{1,0:T(8,128)(2,1)S(1)}, u32[]{:S(2)}, u32[]{:S(2)}) %collective-permute-start.11) | collective-permute-done | bytes 262176 | tf_op jit(solution)/shard_map/ppermute | solution.py:431
  32.8 1.9 %forward.1 = (f32[128,384]{1,0:T(8,128)S(1)}, f32[128,384]{1,0:T(8,128)S(1)}, bf16[128,384]{1,0:T(8,128)(2,1)S(1)}, bf16[128,1024]{1,0:T(8,128)(2,1)S(1)}, bf16[...) custom-call(bf16[128,1024]{1,0:T(8,128)(2,1)S(1)} %get-tuple-element.93.after.x0.refs_0_, ...), custom_call_target="tpu_custom_call" | custom-call | tf_op jit(solution)/shard_map/forward/pallas_call | solution.py:205
  35.4 1.2 %hidden_grad.1 = (bf16[128,384]{1,0:T(8,128)(2,1)S(1)}, bf16[128,384]{1,0:T(8,128)(2,1)S(1)}, f32[8,128]{1,0:T(8,128)S(1)}) custom-call(bf16[128,1024]{1,0:T(8,128)(2,1)S(1)} %get-tuple-element.92.d0.refs_4_, bf16[128,1024]{1,0:T(8,128)(2,1)S(1)} %collective-permute-done.10.d1.refs_5_, bf16[128,1024]{1,0:T(8,128)(2,1)S(1)} %collective-permute-done.11.d2.refs_6_, ...), custom_call_target="tpu_custom_call" | custom-call | tf_op jit(solution)/shard_map/hidden_grad/pallas_call | solution.py:243
  36.7 1.1 %input_grad.2 = (bf16[128,1024]{1,0:T(8,128)(2,1)S(1)}, f32[128,1024]{1,0:T(8,128)S(1)}) custom-call(bf16[128,1024]{1,0:T(8,128)(2,1)S(1)} %add_convert_fusion.1.after, bf16[128,384]{1,0:T(8,128)(2,1)S(1)} %get-tuple-element.67.refs_9_.dact, bf16[128,384]{1,0:T(8,128)(2,1)S(1)} %get-tuple-element.68.refs_10_.dlin, ...), custom_call_target="tpu_custom_call" | custom-call | tf_op jit(solution)/shard_map/input_grad/pallas_call | solution.py:272
  38.4 1.5 %collective-permute-start.15 = (bf16[128,1024]{1,0:T(8,128)(2,1)S(1)}, bf16[128,1024]{1,0:T(8,128)(2,1)S(1)}, u32[]{:S(2)}, u32[]{:S(2)}) collective-permute-start(bf16[128,1024]{1,0:T(8,128)(2,1)S(1)} %add_convert_fusion.1.after), channel_id=1, source_target_pairs={{0,2},{1,3},{2,0},{3,1},{4,6},{5,7},{6,4},{7,5},{8,10},{9,11},{10,... | collective-permute-start | bytes 786440 | tf_op jit(solution)/shard_map/ppermute | solution.py:431
  39.9 1.1 %input_grad.3 = (bf16[128,1024]{1,0:T(8,128)(2,1)S(1)}, f32[128,1024]{1,0:T(8,128)S(1)}) custom-call(bf16[128,1024]{1,0:T(8,128)(2,1)S(1)} %get-tuple-element.74.after, bf16[128,384]{1,0:T(8,128)(2,1)S(1)} %get-tuple-element.67.refs_9_.dact, bf16[128,384]{1,0:T(8,128)(2,1)S(1)} %get-tuple-element.68.refs_10_.dlin, ...), custom_call_target="tpu_custom_call" | custom-call | tf_op jit(solution)/shard_map/input_grad/pallas_call | solution.py:272
  42.9 1.5 %collective-permute-start.20 = (f32[8,128]{1,0:T(8,128)S(1)}, f32[8,128]{1,0:T(8,128)S(1)}, u32[]{:S(2)}, u32[]{:S(2)}) collective-permute-start(f32[8,128]{1,0:T(8,128)S(1)} %add.14), channel_id=1, source_target_pairs={{0,2},{1,3},{2,0},{3,1},{4,6},{5,7},{6,4},{7,5},{8,10},{9,11},{10,... | collective-permute-start | bytes 12296 | tf_op jit(solution)/shard_map/ppermute | solution.py:431
  44.4 6.1 %grads.1 = (bf16[4096,384]{1,0:T(8,128)(2,1)}, bf16[4096,384]{1,0:T(8,128)(2,1)}, bf16[384,4096]{1,0:T(8,128)(2,1)}) custom-call(bf16[128,1024]{1,0:T(8,128)(2,1)} %copy-done, bf16[128,1024]{1,0:T(8,128)(2,1)} %copy-done.5, bf16[128,1024]{1,0:T(8,128)(2,1)} %copy-done.1, bf16[128,1024]{1,0:T(8,128)(2,1)} %copy-done.7, bf16[128,1024]{1,0:T(8,128)(2,1)} %copy-done.4, ...), custom_call_target="tpu_custom_call" | custom-call | flops 1207959552 | bytes 9437184 | tf_op jit(solution)/shard_map/grads/pallas_call | solution.py:326
  50.5 2.0 %collective-permute-done.20 = f32[8,128]{1,0:T(8,128)S(1)} collective-permute-done((f32[8,128]{1,0:T(8,128)S(1)}, f32[8,128]{1,0:T(8,128)S(1)}, u32[]{:S(2)}, u32[]{:S(2)}) %collective-permute-start.20) | collective-permute-done | bytes 4128 | tf_op jit(solution)/shard_map/ppermute | solution.py:431
  52.9 3.1 %collective-permute-start.21 = (bf16[17,16,128]{2,1,0:T(8,128)(2,1)S(1)}, bf16[17,16,128]{2,1,0:T(8,128)(2,1)S(1)}, u32[]{:S(2)}, u32[]{:S(2)}) collective-permute-start(bf16[17,16,128]{2,1,0:T(8,128)(2,1)S(1)} %get-tuple-element.80), channel_id=1, source_target_pairs={{0,28},{4,24},{8,20},{12,16},{16,12},{20,8},{24,4},{28,0},{1,29},{... | collective-permute-start | bytes 208904 | tf_op jit(solution)/shard_map/ppermute | solution.py:438
  56.0 1.4 %collective-permute-start.22 = (bf16[17,16,128]{2,1,0:T(8,128)(2,1)S(1)}, bf16[17,16,128]{2,1,0:T(8,128)(2,1)S(1)}, u32[]{:S(2)}, u32[]{:S(2)}) collective-permute-start(bf16[17,16,128]{2,1,0:T(8,128)(2,1)S(1)} %get-tuple-element.81), channel_id=1, source_target_pairs={{0,24},{4,28},{8,16},{12,20},{16,8},{20,12},{24,0},{28,4},{1,25},{... | collective-permute-start | bytes 208904 | tf_op jit(solution)/shard_map/ppermute | solution.py:438
  58.2 2.4 %collective-permute-start.24 = (bf16[17,16,128]{2,1,0:T(8,128)(2,1)S(1)}, bf16[17,16,128]{2,1,0:T(8,128)(2,1)S(1)}, u32[]{:S(2)}, u32[]{:S(2)}) collective-permute-start(bf16[17,16,128]{2,1,0:T(8,128)(2,1)S(1)} %get-tuple-element.83), channel_id=1, source_target_pairs={{0,16},{4,20},{8,24},{12,28},{16,0},{20,4},{24,8},{28,12},{1,17},{... | collective-permute-start | bytes 208904 | tf_op jit(solution)/shard_map/ppermute | solution.py:438
  61.3 3.3 %collective-permute-start.26 = (bf16[17,16,128]{2,1,0:T(8,128)(2,1)S(1)}, bf16[17,16,128]{2,1,0:T(8,128)(2,1)S(1)}, u32[]{:S(2)}, u32[]{:S(2)}) collective-permute-start(bf16[17,16,128]{2,1,0:T(8,128)(2,1)S(1)} %get-tuple-element.85), channel_id=1, source_target_pairs={{0,8},{4,12},{8,0},{12,4},{16,24},{20,28},{24,16},{28,20},{1,9},{5... | collective-permute-start | bytes 208904 | tf_op jit(solution)/shard_map/ppermute | solution.py:438
  64.6 3.2 %collective-permute-done.23.refs_9_ = bf16[17,16,128]{2,1,0:T(8,128)(2,1)S(1)} collective-permute-done((bf16[17,16,128]{2,1,0:T(8,128)(2,1)S(1)}, bf16[17,16,128]{2,1,0:T(8,128)(2,1)S(1)}, u32[]{:S(2)}, u32[]{:S(2)}) %collective-permute-start.23) | collective-permute-done | bytes 69664 | tf_op jit(solution)/shard_map/ppermute | solution.py:438
  68.9 1.1 %combine.1 = (bf16[128,1024]{1,0:T(8,128)(2,1)}, bf16[128,1024]{1,0:T(8,128)(2,1)}, f32[8,128]{1,0:T(8,128)}) custom-call(bf16[128,128]{1,0:T(8,128)(2,1)S(1)} %get-tuple-element.49.refs_0_, bf16[128,128]{1,0:T(8,128)(2,1)S(1)} %get-tuple-element.50.refs_1_, bf16[128,128]{1,0:T(8,128)(2,1)S(1)} %get-tuple-element.51.refs_2_, ...), custom_call_target="tpu_custom_call" | custom-call | tf_op jit(solution)/shard_map/combine/pallas_call | solution.py:415
  (80 shorter events, 10.1 us)
Async XLA Ops:
  2.1 11.3 %collective-permute-start = (bf16[32,1024]{1,0:T(8,128)(2,1)S(1)}, bf16[32,1024]{1,0:T(8,128)(2,1)S(1)}, u32[]{:S(2)}, u32[]{:S(2)}) collective-permute-start(bf16[32,1024]{1,0:T(8,128)(2,1)S(1)} %get-tuple-element.54), channel_id=1, source_target_pairs={{0,28},{4,24},{8,20},{12,16},{16,12},{20,8},{24,4},{28,0},{1,29},{... | collective-permute-start | bytes 196616 | tf_op jit(solution)/shard_map/ppermute | solution.py:438
  8.2 6.3 %collective-permute-start.1 = (bf16[32,1024]{1,0:T(8,128)(2,1)S(1)}, bf16[32,1024]{1,0:T(8,128)(2,1)S(1)}, u32[]{:S(2)}, u32[]{:S(2)}) collective-permute-start(bf16[32,1024]{1,0:T(8,128)(2,1)S(1)} %get-tuple-element.55), channel_id=1, source_target_pairs={{0,24},{4,28},{8,16},{12,20},{16,8},{20,12},{24,0},{28,4},{1,25},{... | collective-permute-start | bytes 196616 | tf_op jit(solution)/shard_map/ppermute | solution.py:438
  8.4 9.4 %collective-permute-start.2 = (bf16[32,1024]{1,0:T(8,128)(2,1)S(1)}, bf16[32,1024]{1,0:T(8,128)(2,1)S(1)}, u32[]{:S(2)}, u32[]{:S(2)}) collective-permute-start(bf16[32,1024]{1,0:T(8,128)(2,1)S(1)} %get-tuple-element.56), channel_id=1, source_target_pairs={{0,20},{4,16},{8,28},{12,24},{16,4},{20,0},{24,12},{28,8},{1,21},{... | collective-permute-start | bytes 196616 | tf_op jit(solution)/shard_map/ppermute | solution.py:438
  9.2 10.2 %collective-permute-start.3 = (bf16[32,1024]{1,0:T(8,128)(2,1)S(1)}, bf16[32,1024]{1,0:T(8,128)(2,1)S(1)}, u32[]{:S(2)}, u32[]{:S(2)}) collective-permute-start(bf16[32,1024]{1,0:T(8,128)(2,1)S(1)} %get-tuple-element.57), channel_id=1, source_target_pairs={{0,16},{4,20},{8,24},{12,28},{16,0},{20,4},{24,8},{28,12},{1,17},{... | collective-permute-start | bytes 196616 | tf_op jit(solution)/shard_map/ppermute | solution.py:438
  11.2 8.2 %collective-permute-start.4 = (bf16[32,1024]{1,0:T(8,128)(2,1)S(1)}, bf16[32,1024]{1,0:T(8,128)(2,1)S(1)}, u32[]{:S(2)}, u32[]{:S(2)}) collective-permute-start(bf16[32,1024]{1,0:T(8,128)(2,1)S(1)} %get-tuple-element.58), channel_id=1, source_target_pairs={{0,12},{4,8},{8,4},{12,0},{16,28},{20,24},{24,20},{28,16},{1,13},{... | collective-permute-start | bytes 196616 | tf_op jit(solution)/shard_map/ppermute | solution.py:438
  13.5 6.4 %collective-permute-start.5 = (bf16[32,1024]{1,0:T(8,128)(2,1)S(1)}, bf16[32,1024]{1,0:T(8,128)(2,1)S(1)}, u32[]{:S(2)}, u32[]{:S(2)}) collective-permute-start(bf16[32,1024]{1,0:T(8,128)(2,1)S(1)} %get-tuple-element.59), channel_id=1, source_target_pairs={{0,8},{4,12},{8,0},{12,4},{16,24},{20,28},{24,16},{28,20},{1,9},{5... | collective-permute-start | bytes 196616 | tf_op jit(solution)/shard_map/ppermute | solution.py:438
  14.4 5.4 %collective-permute-start.6 = (bf16[32,1024]{1,0:T(8,128)(2,1)S(1)}, bf16[32,1024]{1,0:T(8,128)(2,1)S(1)}, u32[]{:S(2)}, u32[]{:S(2)}) collective-permute-start(bf16[32,1024]{1,0:T(8,128)(2,1)S(1)} %get-tuple-element.60), channel_id=1, source_target_pairs={{0,4},{4,0},{8,12},{12,8},{16,20},{20,16},{24,28},{28,24},{1,5},{5... | collective-permute-start | bytes 196616 | tf_op jit(solution)/shard_map/ppermute | solution.py:438
  19.9 9.3 %collective-permute-start.8 = (bf16[128,1024]{1,0:T(8,128)(2,1)S(1)}, bf16[128,1024]{1,0:T(8,128)(2,1)S(1)}, u32[]{:S(2)}, u32[]{:S(2)}) collective-permute-start(bf16[128,1024]{1,0:T(8,128)(2,1)S(1)} %get-tuple-element.93.after.x0.refs_0_), channel_id=1, source_target_pairs={{0,2},{1,3},{2,0},{3,1},{4,6},{5,7},{6,4},{7,5},{8,10},{9,11},{10,... | collective-permute-start | bytes 786440 | tf_op jit(solution)/shard_map/ppermute | solution.py:431
  21.5 11.3 %collective-permute-start.7 = (bf16[128,1024]{1,0:T(8,128)(2,1)S(1)}, bf16[128,1024]{1,0:T(8,128)(2,1)S(1)}, u32[]{:S(2)}, u32[]{:S(2)}) collective-permute-start(bf16[128,1024]{1,0:T(8,128)(2,1)S(1)} %get-tuple-element.93.after.x0.refs_0_), channel_id=1, source_target_pairs={{0,1},{1,0},{2,3},{3,2},{4,5},{5,4},{6,7},{7,6},{8,9},{9,8},{10,11... | collective-permute-start | bytes 786440 | tf_op jit(solution)/shard_map/ppermute | solution.py:431
  21.5 11.2 %collective-permute-start.11 = (bf16[128,1024]{1,0:T(8,128)(2,1)S(1)}, bf16[128,1024]{1,0:T(8,128)(2,1)S(1)}, u32[]{:S(2)}, u32[]{:S(2)}) collective-permute-start(bf16[128,1024]{1,0:T(8,128)(2,1)S(1)} %get-tuple-element.92.d0.refs_4_), channel_id=1, source_target_pairs={{0,2},{1,3},{2,0},{3,1},{4,6},{5,7},{6,4},{7,5},{8,10},{9,11},{10,... | collective-permute-start | bytes 786440 | tf_op jit(solution)/shard_map/ppermute | solution.py:431
  29.3 3.5 %collective-permute-start.9 = (bf16[128,1024]{1,0:T(8,128)(2,1)S(1)}, bf16[128,1024]{1,0:T(8,128)(2,1)S(1)}, u32[]{:S(2)}, u32[]{:S(2)}) collective-permute-start(bf16[128,1024]{1,0:T(8,128)(2,1)S(1)} %pass_on.1), channel_id=1, source_target_pairs={{0,1},{1,0},{2,3},{3,2},{4,5},{5,4},{6,7},{7,6},{8,9},{9,8},{10,11... | collective-permute-start | bytes 786440 | tf_op jit(solution)/shard_map/ppermute | solution.py:431
  29.3 6.0 %collective-permute-start.10 = (bf16[128,1024]{1,0:T(8,128)(2,1)S(1)}, bf16[128,1024]{1,0:T(8,128)(2,1)S(1)}, u32[]{:S(2)}, u32[]{:S(2)}) collective-permute-start(bf16[128,1024]{1,0:T(8,128)(2,1)S(1)} %get-tuple-element.92.d0.refs_4_), channel_id=1, source_target_pairs={{0,1},{1,0},{2,3},{3,2},{4,5},{5,4},{6,7},{7,6},{8,9},{9,8},{10,11... | collective-permute-start | bytes 786440 | tf_op jit(solution)/shard_map/ppermute | solution.py:431
  38.1 14.4 %collective-permute-start.13 = (bf16[128,1024]{1,0:T(8,128)(2,1)S(1)}, bf16[128,1024]{1,0:T(8,128)(2,1)S(1)}, u32[]{:S(2)}, u32[]{:S(2)}) collective-permute-start(bf16[128,1024]{1,0:T(8,128)(2,1)S(1)} %get-tuple-element.71), channel_id=1, source_target_pairs={{0,1},{1,0},{2,3},{3,2},{4,5},{5,4},{6,7},{7,6},{8,9},{9,8},{10,11... | collective-permute-start | bytes 786440 | tf_op jit(solution)/shard_map/ppermute | solution.py:431
  38.4 14.2 %collective-permute-start.15 = (bf16[128,1024]{1,0:T(8,128)(2,1)S(1)}, bf16[128,1024]{1,0:T(8,128)(2,1)S(1)}, u32[]{:S(2)}, u32[]{:S(2)}) collective-permute-start(bf16[128,1024]{1,0:T(8,128)(2,1)S(1)} %add_convert_fusion.1.after), channel_id=1, source_target_pairs={{0,2},{1,3},{2,0},{3,1},{4,6},{5,7},{6,4},{7,5},{8,10},{9,11},{10,... | collective-permute-start | bytes 786440 | tf_op jit(solution)/shard_map/ppermute | solution.py:431
  41.0 11.6 %collective-permute-start.16 = (bf16[128,1024]{1,0:T(8,128)(2,1)S(1)}, bf16[128,1024]{1,0:T(8,128)(2,1)S(1)}, u32[]{:S(2)}, u32[]{:S(2)}) collective-permute-start(bf16[128,1024]{1,0:T(8,128)(2,1)S(1)} %get-tuple-element.76), channel_id=1, source_target_pairs={{0,1},{1,0},{2,3},{3,2},{4,5},{5,4},{6,7},{7,6},{8,9},{9,8},{10,11... | collective-permute-start | bytes 786440 | tf_op jit(solution)/shard_map/ppermute | solution.py:431
  41.1 11.4 %collective-permute-start.18 = (bf16[128,1024]{1,0:T(8,128)(2,1)S(1)}, bf16[128,1024]{1,0:T(8,128)(2,1)S(1)}, u32[]{:S(2)}, u32[]{:S(2)}) collective-permute-start(bf16[128,1024]{1,0:T(8,128)(2,1)S(1)} %add_convert_fusion), channel_id=1, source_target_pairs={{0,2},{1,3},{2,0},{3,1},{4,6},{5,7},{6,4},{7,5},{8,10},{9,11},{10,... | collective-permute-start | bytes 786440 | tf_op jit(solution)/shard_map/ppermute | solution.py:431
  42.9 9.7 %collective-permute-start.20 = (f32[8,128]{1,0:T(8,128)S(1)}, f32[8,128]{1,0:T(8,128)S(1)}, u32[]{:S(2)}, u32[]{:S(2)}) collective-permute-start(f32[8,128]{1,0:T(8,128)S(1)} %add.14), channel_id=1, source_target_pairs={{0,2},{1,3},{2,0},{3,1},{4,6},{5,7},{6,4},{7,5},{8,10},{9,11},{10,... | collective-permute-start | bytes 12296 | tf_op jit(solution)/shard_map/ppermute | solution.py:431
  52.9 8.4 %collective-permute-start.21 = (bf16[17,16,128]{2,1,0:T(8,128)(2,1)S(1)}, bf16[17,16,128]{2,1,0:T(8,128)(2,1)S(1)}, u32[]{:S(2)}, u32[]{:S(2)}) collective-permute-start(bf16[17,16,128]{2,1,0:T(8,128)(2,1)S(1)} %get-tuple-element.80), channel_id=1, source_target_pairs={{0,28},{4,24},{8,20},{12,16},{16,12},{20,8},{24,4},{28,0},{1,29},{... | collective-permute-start | bytes 208904 | tf_op jit(solution)/shard_map/ppermute | solution.py:438
  56.0 8.6 %collective-permute-start.22 = (bf16[17,16,128]{2,1,0:T(8,128)(2,1)S(1)}, bf16[17,16,128]{2,1,0:T(8,128)(2,1)S(1)}, u32[]{:S(2)}, u32[]{:S(2)}) collective-permute-start(bf16[17,16,128]{2,1,0:T(8,128)(2,1)S(1)} %get-tuple-element.81), channel_id=1, source_target_pairs={{0,24},{4,28},{8,16},{12,20},{16,8},{20,12},{24,0},{28,4},{1,25},{... | collective-permute-start | bytes 208904 | tf_op jit(solution)/shard_map/ppermute | solution.py:438
  57.4 10.4 %collective-permute-start.23 = (bf16[17,16,128]{2,1,0:T(8,128)(2,1)S(1)}, bf16[17,16,128]{2,1,0:T(8,128)(2,1)S(1)}, u32[]{:S(2)}, u32[]{:S(2)}) collective-permute-start(bf16[17,16,128]{2,1,0:T(8,128)(2,1)S(1)} %get-tuple-element.82), channel_id=1, source_target_pairs={{0,20},{4,16},{8,28},{12,24},{16,4},{20,0},{24,12},{28,8},{1,21},{... | collective-permute-start | bytes 208904 | tf_op jit(solution)/shard_map/ppermute | solution.py:438
  58.2 9.8 %collective-permute-start.24 = (bf16[17,16,128]{2,1,0:T(8,128)(2,1)S(1)}, bf16[17,16,128]{2,1,0:T(8,128)(2,1)S(1)}, u32[]{:S(2)}, u32[]{:S(2)}) collective-permute-start(bf16[17,16,128]{2,1,0:T(8,128)(2,1)S(1)} %get-tuple-element.83), channel_id=1, source_target_pairs={{0,16},{4,20},{8,24},{12,28},{16,0},{20,4},{24,8},{28,12},{1,17},{... | collective-permute-start | bytes 208904 | tf_op jit(solution)/shard_map/ppermute | solution.py:438
  60.6 7.4 %collective-permute-start.25 = (bf16[17,16,128]{2,1,0:T(8,128)(2,1)S(1)}, bf16[17,16,128]{2,1,0:T(8,128)(2,1)S(1)}, u32[]{:S(2)}, u32[]{:S(2)}) collective-permute-start(bf16[17,16,128]{2,1,0:T(8,128)(2,1)S(1)} %get-tuple-element.84), channel_id=1, source_target_pairs={{0,12},{4,8},{8,4},{12,0},{16,28},{20,24},{24,20},{28,16},{1,13},{... | collective-permute-start | bytes 208904 | tf_op jit(solution)/shard_map/ppermute | solution.py:438
  61.3 7.5 %collective-permute-start.26 = (bf16[17,16,128]{2,1,0:T(8,128)(2,1)S(1)}, bf16[17,16,128]{2,1,0:T(8,128)(2,1)S(1)}, u32[]{:S(2)}, u32[]{:S(2)}) collective-permute-start(bf16[17,16,128]{2,1,0:T(8,128)(2,1)S(1)} %get-tuple-element.85), channel_id=1, source_target_pairs={{0,8},{4,12},{8,0},{12,4},{16,24},{20,28},{24,16},{28,20},{1,9},{5... | collective-permute-start | bytes 208904 | tf_op jit(solution)/shard_map/ppermute | solution.py:438
  64.6 4.3 %collective-permute-start.27 = (bf16[17,16,128]{2,1,0:T(8,128)(2,1)S(1)}, bf16[17,16,128]{2,1,0:T(8,128)(2,1)S(1)}, u32[]{:S(2)}, u32[]{:S(2)}) collective-permute-start(bf16[17,16,128]{2,1,0:T(8,128)(2,1)S(1)} %get-tuple-element.86), channel_id=1, source_target_pairs={{0,4},{4,0},{8,12},{12,8},{16,20},{20,16},{24,28},{28,24},{1,5},{5... | collective-permute-start | bytes 208904 | tf_op jit(solution)/shard_map/ppermute | solution.py:438
  (17 other events, 100.5 us)

commit v4 on v0

v4 whole, which is shorter than its diff:
```python
import functools

import jax
import jax.numpy as jnp
from jax import lax
from jax.experimental import pallas as pl
from jax.experimental.pallas import tpu as pltpu
from jax.sharding import PartitionSpec as P

CAP = 16
LANES = 128
F32 = jnp.float32
BF16 = jnp.bfloat16
NN = (((1,), (0,)), ((), ()))
NT = (((1,), (1,)), ((), ()))
TN = (((0,), (0,)), ((), ()))


def dot(a, b, dims=NN):
    return lax.dot_general(a, b, dims, preferred_element_type=F32)


def vspec():
    return pl.BlockSpec(memory_space=pltpu.VMEM)


def hspec():
    return pl.BlockSpec(memory_space=pltpu.HBM)


def aspec():
    return pl.BlockSpec(memory_space=pl.ANY)


def fixed(x):
    return pltpu.with_memory_space_constraint(x, pltpu.HBM)


def array(shape, dtype=BF16):
    return jax.ShapeDtypeStruct(shape, dtype)


def call(kernel, name, out_shape, in_specs, out_spec, scratch=(), mib=16, flops=0, nbytes=0):
    out_specs = (out_spec,) * len(out_shape) if isinstance(out_shape, tuple) else out_spec
    return pl.pallas_call(
        kernel,
        out_shape=out_shape,
        in_specs=in_specs,
        out_specs=out_specs,
        scratch_shapes=list(scratch),
        compiler_params=pltpu.CompilerParams(vmem_limit_bytes=mib * 1024 * 1024),
        cost_estimate=pl.CostEstimate(flops=flops, bytes_accessed=nbytes, transcendentals=0),
        name=name,
    )


def fetch(src, dst, sem):
    copy = pltpu.make_async_copy(src, dst, sem)
    copy.start()
    return copy


def steps(count):
    return [0] + sorted(range(1, count), key=lambda s: ([3,6,7,1,2,4,5].index(s) if count == 8 else -s))


def groups(count):
    if count == 8:
        listed = [[7, 6], [3, 5, 4], [2, 1, 0]]
    else:
        far = sorted(range(1, count), reverse=True) + [0]
        third = -(-count // 3)
        listed = [far[:third], far[third : 2 * third], far[2 * third :]]
    order = steps(count)
    return [[order.index(s) for s in group] for group in listed]


def relative(experts, topk, tok):
    place = lax.broadcasted_iota(jnp.int32, (experts, topk, tok), 0)
    distance = jnp.zeros_like(place)
    for p, s in enumerate(steps(experts)):
        distance = jnp.where(place == p, s, distance)
    return distance ^ lax.axis_index("ctx")


def dispatch_kernel(experts, *refs):
    routes_in, gates_in, tokens_in, d_in = refs[:4]
    outs = refs[4 : 4 + experts]
    sel, pick, w_hi, w_lo, routes, gates, tokens, d_out, sem = refs[4 + experts :]
    topk, tok = routes.shape
    slots = experts * CAP
    pairs = ((routes_in, routes), (gates_in, gates), (tokens_in, tokens), (d_in, d_out))
    loads = [fetch(src, dst, sem.at[i]) for i, (src, dst) in enumerate(pairs)]
    loads[0].wait()
    loads[1].wait()
    match = routes[...][None] == relative(experts, topk, tok)
    hit = jnp.sum(jnp.where(match, 1.0, 0.0), axis=1)
    gate = jnp.sum(jnp.where(match, gates[...][None], 0.0), axis=1)
    earlier = lax.broadcasted_iota(jnp.int32, (tok, tok), 0) < lax.broadcasted_iota(
        jnp.int32, (tok, tok), 1
    )
    before = dot(hit.astype(BF16), jnp.where(earlier, 1.0, 0.0).astype(BF16))
    place = jnp.where(hit > 0.0, before, -1.0)[:, None, :]
    row = lax.broadcasted_iota(jnp.int32, (experts, CAP, tok), 1).astype(F32)
    chosen = jnp.where(place == row, 1.0, 0.0)
    weight = (chosen * gate[:, None, :]).reshape(slots, tok)
    chosen = chosen.reshape(slots, tok)
    select = chosen.astype(BF16)
    loads[2].wait()
    x = dot(select, tokens[...]).astype(BF16)
    slot_gate = jnp.sum(weight, axis=1, keepdims=True)
    loads[3].wait()
    d = (slot_gate * dot(select, d_out[...])).astype(BF16)
    for e, out in enumerate(outs):
        out[0] = x[e * CAP : (e + 1) * CAP]
        out[1] = d[e * CAP : (e + 1) * CAP]
    sel[...] = select
    pick[...] = chosen.T.astype(BF16)
    back = weight.T
    high = back.astype(BF16)
    w_hi[...] = high
    w_lo[...] = (back - high.astype(F32)).astype(BF16)


def dispatch(routes_t, gates_t, tokens, d_out, experts):
    tok, quarter = tokens.shape
    slots = experts * CAP
    results = call(
        functools.partial(dispatch_kernel, experts),
        "dispatch",
        (array((2, CAP, quarter)),) * experts
        + (array((slots, tok)),)
        + (array((tok, slots)),) * 3,
        [hspec()] * 4,
        vspec(),
        [
            pltpu.VMEM(routes_t.shape, jnp.int32),
            pltpu.VMEM(gates_t.shape, F32),
            pltpu.VMEM(tokens.shape, BF16),
            pltpu.VMEM(d_out.shape, BF16),
            pltpu.SemaphoreType.DMA((4,)),
        ],
    )(*(fixed(v) for v in (routes_t, gates_t, tokens, d_out)))
    return results[:experts], results[experts:]


def quarter_of(me, flip, size):
    return pl.ds(pl.multiple_of((me ^ flip) * size, size), size)


def load_kernel(after, wg, wu, wd, vg, vu, vd, sem):
    rows = wg.shape[0] // 4
    copies = []
    for i in range(4):
        part = (pl.ds(i * rows, rows), slice(None))
        cols = (slice(None), pl.ds(i * rows, rows))
        copies.append(fetch(wg.at[part], vg.at[part], sem.at[0, i]))
        copies.append(fetch(wu.at[part], vu.at[part], sem.at[1, i]))
        copies.append(fetch(wd.at[cols], vd.at[cols], sem.at[2, i]))
    for copy in copies:
        copy.wait()


def load(after, *weights):
    return call(
        load_kernel,
        "load",
        tuple(array(w.shape) for w in weights),
        [aspec()] + [hspec()] * 3,
        vspec(),
        [pltpu.SemaphoreType.DMA((3, 4))],
        mib=4,
    )(after, *(fixed(w) for w in weights))


def pass_kernel(after, x, *outs):
    count = outs[0].shape[0]
    for n, out in enumerate(outs):
        out[...] = x[n * count : (n + 1) * count]


def pass_on(after, x, pieces):
    shape = (x.shape[0] // pieces, *x.shape[1:])
    out_shape = (array(shape),) * pieces
    return call(pass_kernel, "pass_on", out_shape, [aspec(), vspec()], vspec(), mib=4)(after, x)


def rows_of(first, rest, which):
    size = first.shape[3]
    return jnp.concatenate(
        [first[:, which].reshape(-1, size), rest[...].reshape(-1, size)], axis=0
    )


def forward_kernel(after, after_too, *refs):
    firsts, rests = refs[:4], refs[4:8]
    vg, vu, vd, act, lin, hidden, send, keep_far, keep_own = refs[8:]
    me = lax.axis_index("tp")
    size = firsts[0].shape[3]
    a = b = None
    for i in range(4):
        part = quarter_of(me, i, size)
        x = rows_of(firsts[i], rests[i], 0)
        pa = dot(x, vg[part, :])
        pb = dot(x, vu[part, :])
        a = pa if a is None else a + pa
        b = pb if b is None else b + pb
    act[...] = a
    lin[...] = b
    h = (a * jax.nn.sigmoid(a) * b).astype(BF16)
    hidden[...] = h
    for i, out in ((3, send.at[0]), (1, send.at[1]), (2, keep_far), (0, keep_own)):
        out[...] = dot(h, vd[:, quarter_of(me, i, size)]).astype(out.dtype)


def forward(after, after_too, firsts, rests, vg, vu, vd):
    size = firsts[0].shape[3]
    rows = (firsts[0].shape[0] + rests[0].shape[0]) * CAP
    ff = vg.shape[1]
    return call(
        forward_kernel,
        "forward",
        (array((rows, ff), F32),) * 2
        + (array((rows, ff)),)
        + (array((2, rows, size)),)
        + (array((rows, size), F32),) * 2,
        [aspec()] * 2 + [vspec()] * 11,
        vspec(),
    )(after, after_too, *firsts, *rests, vg, vu, vd)


def hidden_grad_kernel(*refs):
    firsts, rests = refs[:4], refs[4:8]
    act, lin, hidden, vd, dact, dlin, dots = refs[8:]
    me = lax.axis_index("tp")
    size = firsts[0].shape[3]
    rows = act.shape[0]
    dhid = None
    for i in range(4):
        p = dot(rows_of(firsts[i], rests[i], 1), vd[:, quarter_of(me, i, size)], NT)
        dhid = p if dhid is None else dhid + p
    a = act[...]
    s = jax.nn.sigmoid(a)
    dlin[...] = (dhid * (a * s)).astype(BF16)
    dact[...] = (dhid * lin[...] * s * (1.0 + a * (1.0 - s))).astype(BF16)
    per_row = jnp.sum(dhid * hidden[...].astype(F32), axis=1, keepdims=True)
    dots[...] = jnp.broadcast_to(per_row, (rows, LANES)).T[:8]


def hidden_grad(firsts, rests, act, lin, hidden, vd):
    rows, ff = act.shape
    return call(
        hidden_grad_kernel,
        "hidden_grad",
        (array((rows, ff)),) * 2 + (array((8, rows), F32),),
        [vspec()] * 12,
        vspec(),
    )(*firsts, *rests, act, lin, hidden, vd)


def pack_dots(dots, size):
    wide = jnp.concatenate([dots, jnp.zeros((8, size - dots.shape[1]), F32)], axis=1)
    high = wide.astype(BF16).astype(F32)
    top = lax.broadcasted_iota(jnp.int32, wide.shape, 0) == 0
    block = jnp.where(top, high, wide - high)
    return jnp.concatenate([block, block], axis=0).astype(BF16)


def unpack_dots(block, rows):
    block = block.astype(F32)
    return jnp.broadcast_to(block[0:1, :rows] + block[1:2, :rows], (8, rows))


def input_grad_kernel(flips, after, dots, dact, dlin, vg, vu, send, keep):
    me = lax.axis_index("tp")
    rows, size = keep.shape
    da = dact[...]
    dl = dlin[...]
    for i, out in zip(flips, (send, keep)):
        part = quarter_of(me, i, size)
        p = dot(da, vg[part, :], NT) + dot(dl, vu[part, :], NT)
        out[:rows] = p.astype(out.dtype)
    if send.shape[0] > rows:
        send[rows:] = pack_dots(dots[...], size)


def input_grad(flips, after, dots, dact, dlin, vg, vu, more=0):
    rows = dact.shape[0]
    size = vg.shape[0] // 4
    return call(
        functools.partial(input_grad_kernel, flips),
        "input_grad",
        (array((rows + more, size)), array((rows, size), F32)),
        [aspec()] + [vspec()] * 5,
        vspec(),
    )(after, dots, dact, dlin, vg, vu)


def half_kernel(places, after, o_keep, o_near, x_keep, x_near, dots, out):
    rows, size = o_keep.shape
    count = len(places) * CAP
    for n, p in enumerate(places):
        span = slice(p * CAP, (p + 1) * CAP)
        o = o_keep[span] + o_near[0, span].astype(F32)
        x = x_keep[span] + x_near[span].astype(F32)
        out[n * CAP : (n + 1) * CAP] = o.astype(BF16)
        out[count + n * CAP : count + (n + 1) * CAP] = x.astype(BF16)
    if out.shape[0] > 2 * count:
        out[2 * count :] = pack_dots(dots[...] + unpack_dots(x_near[rows:], rows), size)


def half(after, places, o_keep, o_near, x_keep, x_near, dots, more=0):
    size = o_keep.shape[1]
    return call(
        functools.partial(half_kernel, places),
        "half",
        array((2 * CAP * len(places) + more, size)),
        [aspec()] + [vspec()] * 5,
        vspec(),
    )(after, o_keep, o_near, x_keep, x_near, dots)


def grads_kernel(which, count, after, *refs):
    firsts, rests = refs[:4], refs[4:8]
    given = refs[8 : 8 + count]
    outs = refs[8 + count : 8 + 2 * count]
    made = refs[8 + 2 * count : 8 + 3 * count]
    sem = refs[8 + 3 * count]
    me = lax.axis_index("tp")
    size = firsts[0].shape[3]
    values = [g[...] for g in given]
    stores = []
    for i in range(4):
        part = quarter_of(me, i, size)
        rows = rows_of(firsts[i], rests[i], which)
        for n in range(count):
            if which == 0:
                at = (part, slice(None))
                made[n][at] = dot(rows, values[n], TN).astype(BF16)
            else:
                at = (slice(None), part)
                made[n][at] = dot(values[n], rows, TN).astype(BF16)
            stores.append(fetch(made[n].at[at], outs[n].at[at], sem.at[n, i]))
    for copy in stores:
        copy.wait()


def grads(after, which, firsts, rests, given):
    size = firsts[0].shape[3]
    rows, ff = given[0].shape
    count = len(given)
    shape = (4 * size, ff) if which == 0 else (ff, 4 * size)
    return call(
        functools.partial(grads_kernel, which, count),
        "grads",
        (array(shape),) * count,
        [aspec()] + [vspec()] * (8 + count),
        hspec(),
        [pltpu.VMEM(shape, BF16)] * count + [pltpu.SemaphoreType.DMA((count, 4))],
        mib=20,
        flops=2 * count * rows * ff * 4 * size,
        nbytes=2 * count * ff * 4 * size,
    )(after, *firsts, *rests, *given)


def total_kernel(places, after, o_keep, o_near, x_keep, x_near, far, dots, x_send, first, *outs):
    tiles, cap, lanes = outs[0].shape
    count = len(outs) * cap
    rows, size = o_keep.shape
    middle = tiles // 2
    d = dots[...] + unpack_dots(x_send[rows:], rows) + unpack_dots(first[first.shape[0] - 16 :], rows)
    d = jnp.broadcast_to(d[:1], (lanes, rows)).T
    high = d.astype(BF16).astype(F32)
    left = lax.broadcasted_iota(jnp.int32, (rows, lanes), 1) < lanes // 2
    d = jnp.where(left, high, d - high)
    for n, (p, out) in enumerate(zip(places, outs)):
        span = slice(p * cap, (p + 1) * cap)
        at = slice(n * cap, (n + 1) * cap)
        also = slice(count + n * cap, count + (n + 1) * cap)
        for j in range(middle):
            part = slice(j * lanes, (j + 1) * lanes)
            o = o_near[1, span, part].astype(F32) + far[at, part].astype(F32)
            out[j] = (o_keep[span, part] + o).astype(BF16)
            x = x_near[span, part].astype(F32) + far[also, part].astype(F32)
            out[middle + j] = (x_keep[span, part] + x).astype(BF16)
        out[tiles - 1] = d[span].astype(BF16)


def total(after, places, keeps, far, sums):
    size = far.shape[1]
    tiles = 2 * (size // LANES) + 1
    return call(
        functools.partial(total_kernel, places),
        "total",
        (array((tiles, CAP, LANES)),) * len(places),
        [aspec()] + [vspec()] * 8,
        vspec(),
    )(after, *keeps, far, *sums)


def combine_kernel(places, *refs):
    w_hi, w_lo, pick, sel, routes, gates = refs[:6]
    back = [refs[6 + places.index(p)] for p in range(len(places))]
    mixed, d_tokens, d_gates = refs[-3:]
    tiles, cap, lanes = back[0].shape
    slots, tok = sel.shape
    topk = routes.shape[0]
    experts = len(back)
    middle = tiles // 2

    def all_rows(first):
        return jnp.concatenate(
            [jnp.concatenate([b[first + j] for j in range(middle)], axis=1) for b in back], axis=0
        )

    o = all_rows(0)
    mixed[...] = (dot(w_hi[...], o) + dot(w_lo[...], o)).astype(BF16)
    d_tokens[...] = dot(pick[...], all_rows(middle)).astype(BF16)
    both = jnp.concatenate([b[tiles - 1] for b in back], axis=0).astype(F32)
    per_slot = both[:, :1] + both[:, lanes // 2 : lanes // 2 + 1]
    spread = sel[...].astype(F32) * per_slot
    per_expert = jnp.sum(spread.reshape(experts, cap, tok), axis=1)
    match = routes[...][None] == relative(experts, topk, tok)
    scaled = jnp.sum(jnp.where(match, per_expert[:, None, :], 0.0), axis=0)
    d_gates[...] = scaled / gates[...]


def combine(places, back, w_hi, w_lo, pick, sel, routes_t, gates_t):
    quarter = back[0].shape[0] // 2 * LANES
    topk, tok = routes_t.shape
    return call(
        functools.partial(combine_kernel, places),
        "combine",
        (array((tok, quarter)), array((tok, quarter)), array((topk, tok), F32)),
        [vspec()] * (6 + len(back)),
        vspec(),
    )(w_hi, w_lo, pick, sel, routes_t, gates_t, *back)


def swap(x, flip):
    return lax.ppermute(x, "tp", [(i, i ^ flip) for i in range(4)])


def exchange(parts, places, count):
    assert count & (count - 1) == 0
    order = steps(count)
    return [
        lax.ppermute(part, "ctx", [(i, i ^ order[p]) for i in range(count)]) if p else part
        for part, p in zip(parts, places)
    ]


def on_device(tokens, routes, gates, w_gate, w_up, w_down, d_out):
    sources = lax.axis_size("ctx")
    routes_t, gates_t = routes.T, gates.T
    parts, (sel, pick, w_hi, w_lo) = dispatch(routes_t, gates_t, tokens, d_out, sources)
    got = exchange(parts, range(sources), sources)
    early = sources // 2
    cut = early * CAP
    rows = sources * CAP
    first = jnp.stack(got[:early])
    rest_x = jnp.stack([g[0] for g in got[early:]])
    rest_d = jnp.stack([g[1] for g in got[early:]])
    far_first = swap(first, 2)
    far_x = swap(rest_x, 2)
    far_d = swap(rest_d, 2)
    vg, vu, vd = load(first, w_gate[0], w_up[0], w_down[0])
    firsts = (first, swap(first, 1), far_first, swap(far_first, 1))
    across = jnp.concatenate([swap(piece, 1) for piece in pass_on(vg, far_x, 1)])
    xs = (rest_x, swap(rest_x, 1), far_x, across)
    ds = (rest_d, swap(rest_d, 1), far_d, swap(far_d, 1))

    act, lin, hidden, send, keep_far, keep_own = forward(ds[3], ds[1], firsts, xs, vg, vu, vd)
    near_out = swap(send, 1)
    dact, dlin, dots = hidden_grad(firsts, ds, act, lin, hidden, vd)
    send_dx, keep_dx = input_grad((3, 2), dots, dots, dact, dlin, vg, vu, more=16)
    near_send = swap(send_dx, 1)
    send_dx_near, keep_dx_own = input_grad((1, 0), send_dx, dots, dact, dlin, vg, vu)
    near_dx = swap(send_dx_near, 1)
    one, two, three = groups(sources)
    halves = (keep_far, near_out, keep_dx, near_send, dots)
    half_one = half(keep_dx_own, one, *halves, more=16)
    half_two = half(half_one, two, *halves)
    grad_gate, grad_up = grads(half_one, 0, firsts, xs, (dact, dlin))
    half_three = half(fixed(grad_gate), three, *halves)
    far_one, far_two, far_three = swap(half_one, 2), swap(half_two, 2), swap(half_three, 2)
    (grad_down,) = grads(half_one, 1, firsts, ds, (hidden,))
    keeps = (keep_own, near_out, keep_dx_own, near_dx)
    sums = (dots, near_send, far_one)
    back_one = total(fixed(grad_up), one, keeps, far_one, sums)
    back_two = total(back_one[0], two, keeps, far_two, sums)
    back_three = total(back_two[0], three, keeps, far_three, sums)
    places = [*one, *two, *three]
    back = exchange([*back_one, *back_two, *back_three], places, sources)
    mixed, d_tokens, d_gates = combine(places, back, w_hi, w_lo, pick, sel, routes_t, gates_t)
    return (mixed, d_tokens, d_gates.T, grad_gate[None], grad_up[None], grad_down[None])


def solution(mesh):
    placed = (
        P("ctx", "tp"),
        P("ctx", None),
        P("ctx", None),
        P("ctx", None, "tp"),
        P("ctx", None, "tp"),
        P("ctx", "tp", None),
        P("ctx", "tp"),
    )
    return jax.shard_map(
        on_device,
        mesh=mesh,
        in_specs=placed,
        out_specs=(
            P("ctx", "tp"),
            P("ctx", "tp"),
            P("ctx", None),
            P("ctx", None, "tp"),
            P("ctx", None, "tp"),
            P("ctx", "tp", None),
        ),
        check_vma=False,
    )
```

time: 175 us -> 60.8 us (0.35)
  waiting for transfers between devices: 65.5 us -> 5.57 us
  blocking collectives: 39.1 us -> 0 us
  matrix products: 32.5 us -> 0 us
  starting transfers between devices: 11.2 us -> 36.7 us
  Pallas kernels: 0 us -> 17.4 us
  between operations: 13.9 us -> 0.82 us
  other arithmetic: 8.35 us -> 0.07 us
  local copies, waits for them, and re-layouts: 3.96 us -> 0.03 us
    reduce_scatter x2 -> x0, waiting for transfers between devices: 46.2 us -> none  [the longest x1 25.9 us: on_device(): lax.psum_scatter(partial_out, 'tp', scatter_dimension=1, tiled=True)]
    ppermute x0 -> x29, starting transfers between devices: none -> 36.7 us  [the longest x14 26.5 us: exchange(): lax.ppermute(part, 'ctx', [(i, i ^ order[p]) for i in range(count)])]
    dot_general x15 -> x0, matrix products: 32.5 us -> none  [the longest x1 4.23 us: expert_backward(): jnp.dot(hidden.T, dfull, preferred_element_type=jnp.float32)]
    all_to_all x2 -> x0, blocking collectives: 28.1 us -> none  [the longest x1 16.1 us: on_device(): lax.all_to_all(xslots, 'ctx', split_axis=0, concat_axis=0, tiled=True)]
    pallas_call x0 -> x16, Pallas kernels: none -> 17.4 us  [the longest x2 5.3 us: grads(): call(functools.partial(grads_kernel, which, count), 'grads', (array(shape...]
    all_gather x2 -> x0, waiting for transfers between devices: 15.5 us -> none  [the longest x1 13.2 us: on_device(): dfull = lax.all_gather(drecv, 'tp', axis=2, tiled=True).reshape(rows, -1)]
    all_to_all x2 -> x0, starting transfers between devices: 11 us -> none  [the longest x1 5.51 us: on_device(): lax.all_to_all(out_rows, 'ctx', split_axis=0, concat_axis=0, tiled=True)]
    psum x1 -> x0, blocking collectives: 11 us -> none  [on_device(): d_gates = lax.psum(pair_dots, 'tp').reshape(tok_rows, topk)]
  transfers between devices with their start and end apart: 6 -> 29, of which waited for: 5 -> 11; matrix products, arithmetic and copies ran while one was open for 16% -> 0% of each run, Pallas kernels for 0% -> 21%
where the time goes in v4:
time: 60.8 us; the launch traced here: 60.7 us
  starting transfers between devices  36.7 us (60%)
  Pallas kernels  17.4 us (29%)
  waiting for transfers between devices  5.57 us (9%)
  between operations  0.82 us (1%)
    ppermute x14, starting transfers between devices, exchange(): lax.ppermute(part, 'ctx', [(i, i ^ order[p]) for i in range(count)])  26.5 us
    ppermute x15, starting transfers between devices, swap(): return lax.ppermute(x, 'tp', [(i, i ^ flip) for i in range(4)])  10.2 us
    pallas_call x2, Pallas kernels, grads(): call(functools.partial(grads_kernel, which, count), 'grads', (array(shape...  5.3 us
    pallas_call x1, Pallas kernels, load(): call(load_kernel, 'load', tuple((array(w.shape) for w in weights)), [aspe...  3.8 us
    ppermute x14, waiting for transfers between devices, exchange(): lax.ppermute(part, 'ctx', [(i, i ^ order[p]) for i in range(count)])  3.36 us
    ppermute x15, waiting for transfers between devices, swap(): return lax.ppermute(x, 'tp', [(i, i ^ flip) for i in range(4)])  2.21 us
    pallas_call x2, Pallas kernels, input_grad(): call(functools.partial(input_grad_kernel, flips), 'input_grad', (array((r...  2.2 us
    pallas_call x1, Pallas kernels, forward(): call(forward_kernel, 'forward', (array((rows, ff), F32),) * 2 + (array((r...  1.91 us
  transfers between devices with their start and end apart: 29, of which 11 were waited for; matrix products, arithmetic and copies ran while one was open for 0% of the time, Pallas kernels for 21%

profile of v4, /device:TPU:0, one launch (start us, length us, event | category | flops | bytes accessed | tf_op | source)
XLA Modules:
  0.0 60.7 jit_solution(13284902214916750088)
XLA Ops:
  0.6 1.5 %dispatch.1 = (bf16[2,16,1024]{2,1,0:T(8,128)(2,1)S(1)}, bf16[2,16,1024]{2,1,0:T(8,128)(2,1)S(1)}, bf16[2,16,1024]{2,1,0:T(8,128)(2,1)S(1)}, bf16[2,16,1024]{2,1...) custom-call(s32[8,128]{1,0:T(8,128)} %bitcast.14, ...), custom_call_target="tpu_custom_call" | custom-call | tf_op jit(solution)/shard_map/dispatch/pallas_call | solution.py:128
  2.1 6.0 %collective-permute-start.2 = (bf16[2,16,1024]{2,1,0:T(8,128)(2,1)S(1)}, bf16[2,16,1024]{2,1,0:T(8,128)(2,1)S(1)}, u32[]{:S(2)}, u32[]{:S(2)}) collective-permute-start(bf16[2,16,1024]{2,1,0:T(8,128)(2,1)S(1)} %get-tuple-element.54), channel_id=1, source_target_pairs={{0,28},{4,24},{8,20},{12,16},{16,12},{20,8},{24,4},{28,0},{1,29},{... | collective-permute-start | bytes 196616 | tf_op jit(solution)/shard_map/ppermute | solution.py:448
  8.4 5.1 %collective-permute-start.9 = (bf16[2,16,1024]{2,1,0:T(8,128)(2,1)S(1)}, bf16[2,16,1024]{2,1,0:T(8,128)(2,1)S(1)}, u32[]{:S(2)}, u32[]{:S(2)}) collective-permute-start(bf16[2,16,1024]{2,1,0:T(8,128)(2,1)S(1)} %get-tuple-element.58), channel_id=1, source_target_pairs={{0,20},{4,16},{8,28},{12,24},{16,4},{20,0},{24,12},{28,8},{1,21},{... | collective-permute-start | bytes 196616 | tf_op jit(solution)/shard_map/ppermute | solution.py:448
  14.2 0.8 %collective-permute-done.1 = bf16[2,16,1024]{2,1,0:T(8,128)(2,1)S(1)} collective-permute-done((bf16[2,16,1024]{2,1,0:T(8,128)(2,1)S(1)}, bf16[2,16,1024]{2,1,0:T(8,128)(2,1)S(1)}, u32[]{:S(2)}, u32[]{:S(2)}) %collective-permute-start.1) | collective-permute-done | bytes 65568 | tf_op jit(solution)/shard_map/ppermute | solution.py:448
  15.6 1.6 %collective-permute-start.4 = (bf16[4,2,16,1024]{3,2,1,0:T(8,128)(2,1)S(1)}, bf16[4,2,16,1024]{3,2,1,0:T(8,128)(2,1)S(1)}, u32[]{:S(2)}, u32[]{:S(2)}) collective-permute-start(bf16[4,2,16,1024]{3,2,1,0:T(8,128)(2,1)S(1)} %pad_maximum_fusion.after.refs_0_), channel_id=1, source_target_pairs={{0,2},{1,3},{2,0},{3,1},{4,6},{5,7},{6,4},{7,5},{8,10},{9,11},{10,... | collective-permute-start | bytes 786440 | tf_op jit(solution)/shard_map/ppermute | solution.py:441
  17.2 1.3 %collective-permute-done.9 = bf16[2,16,1024]{2,1,0:T(8,128)(2,1)S(1)} collective-permute-done((bf16[2,16,1024]{2,1,0:T(8,128)(2,1)S(1)}, bf16[2,16,1024]{2,1,0:T(8,128)(2,1)S(1)}, u32[]{:S(2)}, u32[]{:S(2)}) %collective-permute-start.9) | collective-permute-done | bytes 65568 | tf_op jit(solution)/shard_map/ppermute | solution.py:448
  18.5 0.8 %collective-permute-done.8 = bf16[2,16,1024]{2,1,0:T(8,128)(2,1)S(1)} collective-permute-done((bf16[2,16,1024]{2,1,0:T(8,128)(2,1)S(1)}, bf16[2,16,1024]{2,1,0:T(8,128)(2,1)S(1)}, u32[]{:S(2)}, u32[]{:S(2)}) %collective-permute-start.8) | collective-permute-done | bytes 65568 | tf_op jit(solution)/shard_map/ppermute | solution.py:448
  19.4 1.6 %collective-permute-start.11 = (bf16[4,16,1024]{2,1,0:T(8,128)(2,1)S(1)}, bf16[4,16,1024]{2,1,0:T(8,128)(2,1)S(1)}, u32[]{:S(2)}, u32[]{:S(2)}) collective-permute-start(bf16[4,16,1024]{2,1,0:T(8,128)(2,1)S(1)} %pad_maximum_fusion.1.refs_4_), channel_id=1, source_target_pairs={{0,2},{1,3},{2,0},{3,1},{4,6},{5,7},{6,4},{7,5},{8,10},{9,11},{10,... | collective-permute-start | bytes 393224 | tf_op jit(solution)/shard_map/ppermute | solution.py:441
  22.4 3.8 %load.1 = (bf16[4096,384]{1,0:T(8,128)(2,1)S(1)}, bf16[4096,384]{1,0:T(8,128)(2,1)S(1)}, bf16[384,4096]{1,0:T(8,128)(2,1)S(1)}) custom-call(bf16[4,2,16,1024]{3,2,1,0:T(8,128)(2,1)S(1)} %pad_maximum_fusion.after.refs_0_, bf16[4096,384]{1,0:T(8,128)(2,1)} %bitcast.21, bf16[4096,384]{1,0:T(8,128)(2,1)} %bitcast.22, bf16[384,4096]{1,0:T(8,128)(2,1)} %bitcast.23), custom_call_target="tpu_custom_call" | custom-call | tf_op jit(solution)/shard_map/load/pallas_call | solution.py:165
  26.8 0.9 %collective-permute-done.14.x.refs_6_ = bf16[4,16,1024]{2,1,0:T(8,128)(2,1)S(1)} collective-permute-done((bf16[4,16,1024]{2,1,0:T(8,128)(2,1)S(1)}, bf16[4,16,1024]{2,1,0:T(8,128)(2,1)S(1)}, u32[]{:S(2)}, u32[]{:S(2)}) %collective-permute-start.14) | collective-permute-done | bytes 131104 | tf_op jit(solution)/shard_map/ppermute | solution.py:441
  29.3 1.9 %forward.1 = (f32[128,384]{1,0:T(8,128)S(1)}, f32[128,384]{1,0:T(8,128)S(1)}, bf16[128,384]{1,0:T(8,128)(2,1)S(1)}, bf16[2,128,1024]{2,1,0:T(8,128)(2,1)S(1)}, f...) custom-call(bf16[4,16,1024]{2,1,0:T(8,128)(2,1)S(1)} %collective-permute-done.12.after.refs_7_, ...), custom_call_target="tpu_custom_call" | custom-call | tf_op jit(solution)/shard_map/forward/pallas_call | solution.py:220
  31.6 1.2 %hidden_grad.1 = (bf16[128,384]{1,0:T(8,128)(2,1)S(1)}, bf16[128,384]{1,0:T(8,128)(2,1)S(1)}, f32[8,128]{1,0:T(8,128)S(1)}) custom-call(bf16[4,2,16,1024]{3,2,1,0:T(8,128)(2,1)S(1)} %pad_maximum_fusion.after.refs_0_, bf16[4,2,16,1024]{3,2,1,0:T(8,128)(2,1)S(1)} %collective-permute-done.3.refs_1_, ...), custom_call_target="tpu_custom_call" | custom-call | tf_op jit(solution)/shard_map/hidden_grad/pallas_call | solution.py:252
  32.8 1.1 %input_grad.2 = (bf16[144,1024]{1,0:T(8,128)(2,1)S(1)}, f32[128,1024]{1,0:T(8,128)S(1)}) custom-call(f32[8,128]{1,0:T(8,128)S(1)} %get-tuple-element.65.after.dots, f32[8,128]{1,0:T(8,128)S(1)} %get-tuple-element.65.after.dots, bf16[128,384]{1,0:T(8,128)(2,1)S(1)} %get-tuple-element.66.dact.refs_8_, bf16[128,384]{1,0:T(8,128)(2,1)S(1)} %get-tuple-element.67.dlin.refs_9_, ...), custom_call_target="tpu_custom_call" | custom-call | tf_op jit(solution)/shard_map/input_grad/pallas_call | solution.py:290
  34.1 1.1 %input_grad.3 = (bf16[128,1024]{1,0:T(8,128)(2,1)S(1)}, f32[128,1024]{1,0:T(8,128)S(1)}) custom-call(bf16[144,1024]{1,0:T(8,128)(2,1)S(1)} %get-tuple-element.68.after, f32[8,128]{1,0:T(8,128)S(1)} %get-tuple-element.65.after.dots, bf16[128,384]{1,0:T(8,128)(2,1)S(1)} %get-tuple-element.66.dact.refs_8_, bf16[128,384]{1,0:T(8,128)(2,1)S(1)} %get-tuple-element.67.dlin.refs_9_, ...), custom_call_target="tpu_custom_call" | custom-call | tf_op jit(solution)/shard_map/input_grad/pallas_call | solution.py:290
  35.7 1.6 %collective-permute-start.19 = (bf16[80,1024]{1,0:T(8,128)(2,1)S(1)}, bf16[80,1024]{1,0:T(8,128)(2,1)S(1)}, u32[]{:S(2)}, u32[]{:S(2)}) collective-permute-start(bf16[80,1024]{1,0:T(8,128)(2,1)S(1)} %half.3.after), channel_id=1, source_target_pairs={{0,2},{1,3},{2,0},{3,1},{4,6},{5,7},{6,4},{7,5},{8,10},{9,11},{10,... | collective-permute-start | bytes 491528 | tf_op jit(solution)/shard_map/ppermute | solution.py:441
  37.9 3.2 %grads.2 = (bf16[4096,384]{1,0:T(8,128)(2,1)}, bf16[4096,384]{1,0:T(8,128)(2,1)}) custom-call(bf16[80,1024]{1,0:T(8,128)(2,1)S(1)} %half.3.after, bf16[4,2,16,1024]{3,2,1,0:T(8,128)(2,1)S(1)} %pad_maximum_fusion.after.refs_0_, bf16[4,2,16,1024]{3,2,1,0:T(8,128)(2,1)S(1)} %collective-permute-done.3.refs_1_, ...), custom_call_target="tpu_custom_call" | custom-call | flops 805306368 | bytes 6291456 | tf_op jit(solution)/shard_map/grads/pallas_call | solution.py:353
  41.2 1.6 %collective-permute-start.26 = (bf16[96,1024]{1,0:T(8,128)(2,1)S(1)}, bf16[96,1024]{1,0:T(8,128)(2,1)S(1)}, u32[]{:S(2)}, u32[]{:S(2)}) collective-permute-start(bf16[96,1024]{1,0:T(8,128)(2,1)S(1)} %half.5), channel_id=1, source_target_pairs={{0,2},{1,3},{2,0},{3,1},{4,6},{5,7},{6,4},{7,5},{8,10},{9,11},{10,... | collective-permute-start | bytes 589832 | tf_op jit(solution)/shard_map/ppermute | solution.py:441
  42.9 5.5 %collective-permute-start.20 = (bf16[17,16,128]{2,1,0:T(8,128)(2,1)S(1)}, bf16[17,16,128]{2,1,0:T(8,128)(2,1)S(1)}, u32[]{:S(2)}, u32[]{:S(2)}) collective-permute-start(bf16[17,16,128]{2,1,0:T(8,128)(2,1)S(1)} %get-tuple-element.76.after), channel_id=1, source_target_pairs={{0,28},{4,24},{8,20},{12,16},{16,12},{20,8},{24,4},{28,0},{1,29},{... | collective-permute-start | bytes 208904 | tf_op jit(solution)/shard_map/ppermute | solution.py:448
  48.5 1.7 %collective-permute-start.23 = (bf16[17,16,128]{2,1,0:T(8,128)(2,1)S(1)}, bf16[17,16,128]{2,1,0:T(8,128)(2,1)S(1)}, u32[]{:S(2)}, u32[]{:S(2)}) collective-permute-start(bf16[17,16,128]{2,1,0:T(8,128)(2,1)S(1)} %get-tuple-element.78.after), channel_id=1, source_target_pairs={{0,12},{4,8},{8,4},{12,0},{16,28},{20,24},{24,20},{28,16},{1,13},{... | collective-permute-start | bytes 208904 | tf_op jit(solution)/shard_map/ppermute | solution.py:448
  50.2 3.6 %collective-permute-start.24 = (bf16[17,16,128]{2,1,0:T(8,128)(2,1)S(1)}, bf16[17,16,128]{2,1,0:T(8,128)(2,1)S(1)}, u32[]{:S(2)}, u32[]{:S(2)}) collective-permute-start(bf16[17,16,128]{2,1,0:T(8,128)(2,1)S(1)} %get-tuple-element.79), channel_id=1, source_target_pairs={{0,20},{4,16},{8,28},{12,24},{16,4},{20,0},{24,12},{28,8},{1,21},{... | collective-permute-start | bytes 208904 | tf_op jit(solution)/shard_map/ppermute | solution.py:448
  54.0 1.1 %collective-permute-start.27 = (bf16[17,16,128]{2,1,0:T(8,128)(2,1)S(1)}, bf16[17,16,128]{2,1,0:T(8,128)(2,1)S(1)}, u32[]{:S(2)}, u32[]{:S(2)}) collective-permute-start(bf16[17,16,128]{2,1,0:T(8,128)(2,1)S(1)} %get-tuple-element.82), channel_id=1, source_target_pairs={{0,8},{4,12},{8,0},{12,4},{16,24},{20,28},{24,16},{28,20},{1,9},{5... | collective-permute-start | bytes 208904 | tf_op jit(solution)/shard_map/ppermute | solution.py:448
  55.1 2.0 %collective-permute-start.28 = (bf16[17,16,128]{2,1,0:T(8,128)(2,1)S(1)}, bf16[17,16,128]{2,1,0:T(8,128)(2,1)S(1)}, u32[]{:S(2)}, u32[]{:S(2)}) collective-permute-start(bf16[17,16,128]{2,1,0:T(8,128)(2,1)S(1)} %get-tuple-element.83), channel_id=1, source_target_pairs={{0,4},{4,0},{8,12},{12,8},{16,20},{20,16},{24,28},{28,24},{1,5},{5... | collective-permute-start | bytes 208904 | tf_op jit(solution)/shard_map/ppermute | solution.py:448
  57.2 2.1 %grads.3 = bf16[384,4096]{1,0:T(8,128)(2,1)} custom-call(bf16[80,1024]{1,0:T(8,128)(2,1)S(1)} %half.3.after, bf16[4,2,16,1024]{3,2,1,0:T(8,128)(2,1)S(1)} %pad_maximum_fusion.after.refs_0_, bf16[4,2,16,1024]{3,2,1,0:T(8,128)(2,1)S(1)} %collective-permute-done.3.refs_1_, bf16[4,2,16,1024]{3,2,1,0:T(8,128)(2,1)S(1)} %collective-permute-done.4.refs_2_, ...), custom_call_target="tpu_custom_call" | custom-call | flops 402653184 | bytes 3145728 | tf_op jit(solution)/shard_map/grads/pallas_call | solution.py:353
  59.6 1.1 %combine.1 = (bf16[128,1024]{1,0:T(8,128)(2,1)}, bf16[128,1024]{1,0:T(8,128)(2,1)}, f32[8,128]{1,0:T(8,128)}) custom-call(bf16[128,128]{1,0:T(8,128)(2,1)S(1)} %get-tuple-element.47.refs_0_, bf16[128,128]{1,0:T(8,128)(2,1)S(1)} %get-tuple-element.48.refs_1_, bf16[128,128]{1,0:T(8,128)(2,1)S(1)} %get-tuple-element.49.refs_2_, ...), custom_call_target="tpu_custom_call" | custom-call | tf_op jit(solution)/shard_map/combine/pallas_call | solution.py:431
  (61 shorter events, 7.6 us)
Async XLA Ops:
  2.1 11.3 %collective-permute-start.2 = (bf16[2,16,1024]{2,1,0:T(8,128)(2,1)S(1)}, bf16[2,16,1024]{2,1,0:T(8,128)(2,1)S(1)}, u32[]{:S(2)}, u32[]{:S(2)}) collective-permute-start(bf16[2,16,1024]{2,1,0:T(8,128)(2,1)S(1)} %get-tuple-element.54), channel_id=1, source_target_pairs={{0,28},{4,24},{8,20},{12,16},{16,12},{20,8},{24,4},{28,0},{1,29},{... | collective-permute-start | bytes 196616 | tf_op jit(solution)/shard_map/ppermute | solution.py:448
  8.2 6.9 %collective-permute-start.1 = (bf16[2,16,1024]{2,1,0:T(8,128)(2,1)S(1)}, bf16[2,16,1024]{2,1,0:T(8,128)(2,1)S(1)}, u32[]{:S(2)}, u32[]{:S(2)}) collective-permute-start(bf16[2,16,1024]{2,1,0:T(8,128)(2,1)S(1)} %get-tuple-element.53), channel_id=1, source_target_pairs={{0,24},{4,28},{8,16},{12,20},{16,8},{20,12},{24,0},{28,4},{1,25},{... | collective-permute-start | bytes 196616 | tf_op jit(solution)/shard_map/ppermute | solution.py:448
  8.4 7.2 %collective-permute-start = (bf16[2,16,1024]{2,1,0:T(8,128)(2,1)S(1)}, bf16[2,16,1024]{2,1,0:T(8,128)(2,1)S(1)}, u32[]{:S(2)}, u32[]{:S(2)}) collective-permute-start(bf16[2,16,1024]{2,1,0:T(8,128)(2,1)S(1)} %get-tuple-element.52), channel_id=1, source_target_pairs={{0,12},{4,8},{8,4},{12,0},{16,28},{20,24},{24,20},{28,16},{1,13},{... | collective-permute-start | bytes 196616 | tf_op jit(solution)/shard_map/ppermute | solution.py:448
  8.4 10.1 %collective-permute-start.9 = (bf16[2,16,1024]{2,1,0:T(8,128)(2,1)S(1)}, bf16[2,16,1024]{2,1,0:T(8,128)(2,1)S(1)}, u32[]{:S(2)}, u32[]{:S(2)}) collective-permute-start(bf16[2,16,1024]{2,1,0:T(8,128)(2,1)S(1)} %get-tuple-element.58), channel_id=1, source_target_pairs={{0,20},{4,16},{8,28},{12,24},{16,4},{20,0},{24,12},{28,8},{1,21},{... | collective-permute-start | bytes 196616 | tf_op jit(solution)/shard_map/ppermute | solution.py:448
  13.5 5.9 %collective-permute-start.8 = (bf16[2,16,1024]{2,1,0:T(8,128)(2,1)S(1)}, bf16[2,16,1024]{2,1,0:T(8,128)(2,1)S(1)}, u32[]{:S(2)}, u32[]{:S(2)}) collective-permute-start(bf16[2,16,1024]{2,1,0:T(8,128)(2,1)S(1)} %get-tuple-element.57), channel_id=1, source_target_pairs={{0,16},{4,20},{8,24},{12,28},{16,0},{20,4},{24,8},{28,12},{1,17},{... | collective-permute-start | bytes 196616 | tf_op jit(solution)/shard_map/ppermute | solution.py:448
  13.5 5.9 %collective-permute-start.7 = (bf16[2,16,1024]{2,1,0:T(8,128)(2,1)S(1)}, bf16[2,16,1024]{2,1,0:T(8,128)(2,1)S(1)}, u32[]{:S(2)}, u32[]{:S(2)}) collective-permute-start(bf16[2,16,1024]{2,1,0:T(8,128)(2,1)S(1)} %get-tuple-element.56), channel_id=1, source_target_pairs={{0,8},{4,12},{8,0},{12,4},{16,24},{20,28},{24,16},{28,20},{1,9},{5... | collective-permute-start | bytes 196616 | tf_op jit(solution)/shard_map/ppermute | solution.py:448
  15.6 6.8 %collective-permute-start.4 = (bf16[4,2,16,1024]{3,2,1,0:T(8,128)(2,1)S(1)}, bf16[4,2,16,1024]{3,2,1,0:T(8,128)(2,1)S(1)}, u32[]{:S(2)}, u32[]{:S(2)}) collective-permute-start(bf16[4,2,16,1024]{3,2,1,0:T(8,128)(2,1)S(1)} %pad_maximum_fusion.after.refs_0_), channel_id=1, source_target_pairs={{0,2},{1,3},{2,0},{3,1},{4,6},{5,7},{6,4},{7,5},{8,10},{9,11},{10,... | collective-permute-start | bytes 786440 | tf_op jit(solution)/shard_map/ppermute | solution.py:441
  19.4 6.8 %collective-permute-start.11 = (bf16[4,16,1024]{2,1,0:T(8,128)(2,1)S(1)}, bf16[4,16,1024]{2,1,0:T(8,128)(2,1)S(1)}, u32[]{:S(2)}, u32[]{:S(2)}) collective-permute-start(bf16[4,16,1024]{2,1,0:T(8,128)(2,1)S(1)} %pad_maximum_fusion.1.refs_4_), channel_id=1, source_target_pairs={{0,2},{1,3},{2,0},{3,1},{4,6},{5,7},{6,4},{7,5},{8,10},{9,11},{10,... | collective-permute-start | bytes 393224 | tf_op jit(solution)/shard_map/ppermute | solution.py:441
  21.0 6.6 %collective-permute-start.14 = (bf16[4,16,1024]{2,1,0:T(8,128)(2,1)S(1)}, bf16[4,16,1024]{2,1,0:T(8,128)(2,1)S(1)}, u32[]{:S(2)}, u32[]{:S(2)}) collective-permute-start(bf16[4,16,1024]{2,1,0:T(8,128)(2,1)S(1)} %pad_maximum_fusion.2.refs_4_), channel_id=1, source_target_pairs={{0,2},{1,3},{2,0},{3,1},{4,6},{5,7},{6,4},{7,5},{8,10},{9,11},{10,... | collective-permute-start | bytes 393224 | tf_op jit(solution)/shard_map/ppermute | solution.py:441
  21.6 6.7 %collective-permute-start.3 = (bf16[4,2,16,1024]{3,2,1,0:T(8,128)(2,1)S(1)}, bf16[4,2,16,1024]{3,2,1,0:T(8,128)(2,1)S(1)}, u32[]{:S(2)}, u32[]{:S(2)}) collective-permute-start(bf16[4,2,16,1024]{3,2,1,0:T(8,128)(2,1)S(1)} %pad_maximum_fusion.after.refs_0_), channel_id=1, source_target_pairs={{0,1},{1,0},{2,3},{3,2},{4,5},{5,4},{6,7},{7,6},{8,9},{9,8},{10,11... | collective-permute-start | bytes 786440 | tf_op jit(solution)/shard_map/ppermute | solution.py:441
  21.6 6.1 %collective-permute-start.10 = (bf16[4,16,1024]{2,1,0:T(8,128)(2,1)S(1)}, bf16[4,16,1024]{2,1,0:T(8,128)(2,1)S(1)}, u32[]{:S(2)}, u32[]{:S(2)}) collective-permute-start(bf16[4,16,1024]{2,1,0:T(8,128)(2,1)S(1)} %pad_maximum_fusion.1.refs_4_), channel_id=1, source_target_pairs={{0,1},{1,0},{2,3},{3,2},{4,5},{5,4},{6,7},{7,6},{8,9},{9,8},{10,11... | collective-permute-start | bytes 393224 | tf_op jit(solution)/shard_map/ppermute | solution.py:441
  22.4 6.9 %collective-permute-start.5 = (bf16[4,2,16,1024]{3,2,1,0:T(8,128)(2,1)S(1)}, bf16[4,2,16,1024]{3,2,1,0:T(8,128)(2,1)S(1)}, u32[]{:S(2)}, u32[]{:S(2)}) collective-permute-start(bf16[4,2,16,1024]{3,2,1,0:T(8,128)(2,1)S(1)} %collective-permute-done.4.refs_2_), channel_id=1, source_target_pairs={{0,1},{1,0},{2,3},{3,2},{4,5},{5,4},{6,7},{7,6},{8,9},{9,8},{10,11... | collective-permute-start | bytes 786440 | tf_op jit(solution)/shard_map/ppermute | solution.py:441
  31.2 4.5 %collective-permute-start.16 = (bf16[2,128,1024]{2,1,0:T(8,128)(2,1)S(1)}, bf16[2,128,1024]{2,1,0:T(8,128)(2,1)S(1)}, u32[]{:S(2)}, u32[]{:S(2)}) collective-permute-start(bf16[2,128,1024]{2,1,0:T(8,128)(2,1)S(1)} %get-tuple-element.71), channel_id=1, source_target_pairs={{0,1},{1,0},{2,3},{3,2},{4,5},{5,4},{6,7},{7,6},{8,9},{9,8},{10,11... | collective-permute-start | bytes 1572872 | tf_op jit(solution)/shard_map/ppermute | solution.py:441
  35.2 7.5 %collective-permute-start.18 = (bf16[128,1024]{1,0:T(8,128)(2,1)S(1)}, bf16[128,1024]{1,0:T(8,128)(2,1)S(1)}, u32[]{:S(2)}, u32[]{:S(2)}) collective-permute-start(bf16[128,1024]{1,0:T(8,128)(2,1)S(1)} %get-tuple-element.75), channel_id=1, source_target_pairs={{0,1},{1,0},{2,3},{3,2},{4,5},{5,4},{6,7},{7,6},{8,9},{9,8},{10,11... | collective-permute-start | bytes 786440 | tf_op jit(solution)/shard_map/ppermute | solution.py:441
  35.7 7.1 %collective-permute-start.19 = (bf16[80,1024]{1,0:T(8,128)(2,1)S(1)}, bf16[80,1024]{1,0:T(8,128)(2,1)S(1)}, u32[]{:S(2)}, u32[]{:S(2)}) collective-permute-start(bf16[80,1024]{1,0:T(8,128)(2,1)S(1)} %half.3.after), channel_id=1, source_target_pairs={{0,2},{1,3},{2,0},{3,1},{4,6},{5,7},{6,4},{7,5},{8,10},{9,11},{10,... | collective-permute-start | bytes 491528 | tf_op jit(solution)/shard_map/ppermute | solution.py:441
  37.3 11.0 %collective-permute-start.22 = (bf16[96,1024]{1,0:T(8,128)(2,1)S(1)}, bf16[96,1024]{1,0:T(8,128)(2,1)S(1)}, u32[]{:S(2)}, u32[]{:S(2)}) collective-permute-start(bf16[96,1024]{1,0:T(8,128)(2,1)S(1)} %half.4), channel_id=1, source_target_pairs={{0,2},{1,3},{2,0},{3,1},{4,6},{5,7},{6,4},{7,5},{8,10},{9,11},{10,... | collective-permute-start | bytes 589832 | tf_op jit(solution)/shard_map/ppermute | solution.py:441
  41.2 12.7 %collective-permute-start.26 = (bf16[96,1024]{1,0:T(8,128)(2,1)S(1)}, bf16[96,1024]{1,0:T(8,128)(2,1)S(1)}, u32[]{:S(2)}, u32[]{:S(2)}) collective-permute-start(bf16[96,1024]{1,0:T(8,128)(2,1)S(1)} %half.5), channel_id=1, source_target_pairs={{0,2},{1,3},{2,0},{3,1},{4,6},{5,7},{6,4},{7,5},{8,10},{9,11},{10,... | collective-permute-start | bytes 589832 | tf_op jit(solution)/shard_map/ppermute | solution.py:441
  42.9 11.1 %collective-permute-start.20 = (bf16[17,16,128]{2,1,0:T(8,128)(2,1)S(1)}, bf16[17,16,128]{2,1,0:T(8,128)(2,1)S(1)}, u32[]{:S(2)}, u32[]{:S(2)}) collective-permute-start(bf16[17,16,128]{2,1,0:T(8,128)(2,1)S(1)} %get-tuple-element.76.after), channel_id=1, source_target_pairs={{0,28},{4,24},{8,20},{12,16},{16,12},{20,8},{24,4},{28,0},{1,29},{... | collective-permute-start | bytes 208904 | tf_op jit(solution)/shard_map/ppermute | solution.py:448
  48.4 6.8 %collective-permute-start.21 = (bf16[17,16,128]{2,1,0:T(8,128)(2,1)S(1)}, bf16[17,16,128]{2,1,0:T(8,128)(2,1)S(1)}, u32[]{:S(2)}, u32[]{:S(2)}) collective-permute-start(bf16[17,16,128]{2,1,0:T(8,128)(2,1)S(1)} %get-tuple-element.77), channel_id=1, source_target_pairs={{0,24},{4,28},{8,16},{12,20},{16,8},{20,12},{24,0},{28,4},{1,25},{... | collective-permute-start | bytes 208904 | tf_op jit(solution)/shard_map/ppermute | solution.py:448
  48.5 10.8 %collective-permute-start.23 = (bf16[17,16,128]{2,1,0:T(8,128)(2,1)S(1)}, bf16[17,16,128]{2,1,0:T(8,128)(2,1)S(1)}, u32[]{:S(2)}, u32[]{:S(2)}) collective-permute-start(bf16[17,16,128]{2,1,0:T(8,128)(2,1)S(1)} %get-tuple-element.78.after), channel_id=1, source_target_pairs={{0,12},{4,8},{8,4},{12,0},{16,28},{20,24},{24,20},{28,16},{1,13},{... | collective-permute-start | bytes 208904 | tf_op jit(solution)/shard_map/ppermute | solution.py:448
  50.2 9.1 %collective-permute-start.24 = (bf16[17,16,128]{2,1,0:T(8,128)(2,1)S(1)}, bf16[17,16,128]{2,1,0:T(8,128)(2,1)S(1)}, u32[]{:S(2)}, u32[]{:S(2)}) collective-permute-start(bf16[17,16,128]{2,1,0:T(8,128)(2,1)S(1)} %get-tuple-element.79), channel_id=1, source_target_pairs={{0,20},{4,16},{8,28},{12,24},{16,4},{20,0},{24,12},{28,8},{1,21},{... | collective-permute-start | bytes 208904 | tf_op jit(solution)/shard_map/ppermute | solution.py:448
  53.8 5.5 %collective-permute-start.25 = (bf16[17,16,128]{2,1,0:T(8,128)(2,1)S(1)}, bf16[17,16,128]{2,1,0:T(8,128)(2,1)S(1)}, u32[]{:S(2)}, u32[]{:S(2)}) collective-permute-start(bf16[17,16,128]{2,1,0:T(8,128)(2,1)S(1)} %get-tuple-element.80), channel_id=1, source_target_pairs={{0,16},{4,20},{8,24},{12,28},{16,0},{20,4},{24,8},{28,12},{1,17},{... | collective-permute-start | bytes 208904 | tf_op jit(solution)/shard_map/ppermute | solution.py:448
  54.0 5.5 %collective-permute-start.27 = (bf16[17,16,128]{2,1,0:T(8,128)(2,1)S(1)}, bf16[17,16,128]{2,1,0:T(8,128)(2,1)S(1)}, u32[]{:S(2)}, u32[]{:S(2)}) collective-permute-start(bf16[17,16,128]{2,1,0:T(8,128)(2,1)S(1)} %get-tuple-element.82), channel_id=1, source_target_pairs={{0,8},{4,12},{8,0},{12,4},{16,24},{20,28},{24,16},{28,20},{1,9},{5... | collective-permute-start | bytes 208904 | tf_op jit(solution)/shard_map/ppermute | solution.py:448
  55.1 4.4 %collective-permute-start.28 = (bf16[17,16,128]{2,1,0:T(8,128)(2,1)S(1)}, bf16[17,16,128]{2,1,0:T(8,128)(2,1)S(1)}, u32[]{:S(2)}, u32[]{:S(2)}) collective-permute-start(bf16[17,16,128]{2,1,0:T(8,128)(2,1)S(1)} %get-tuple-element.83), channel_id=1, source_target_pairs={{0,4},{4,0},{8,12},{12,8},{16,20},{20,16},{24,28},{28,24},{1,5},{5... | collective-permute-start | bytes 208904 | tf_op jit(solution)/shard_map/ppermute | solution.py:448
  (7 other events, 22.5 us)

commit v5 on v4

--- a/solution.py
+++ b/solution.py
@@ -61,7 +61,7 @@
 
 
 def steps(count):
-    return [0] + sorted(range(1, count), key=lambda s: ([3,6,7,1,2,4,5].index(s) if count == 8 else -s))
+    return [0] + sorted(range(1, count), key=lambda s: ([2, 6, 7, 1, 3, 4, 5].index(s) if count == 8 else -s))
 
 
 def groups(count):
@@ -86,7 +86,7 @@
 def dispatch_kernel(experts, *refs):
     routes_in, gates_in, tokens_in, d_in = refs[:4]
     outs = refs[4 : 4 + experts]
-    sel, pick, w_hi, w_lo, routes, gates, tokens, d_out, sem = refs[4 + experts :]
+    sel, weights, routes, gates, tokens, d_out, sem = refs[4 + experts :]
     topk, tok = routes.shape
     slots = experts * CAP
     pairs = ((routes_in, routes), (gates_in, gates), (tokens_in, tokens), (d_in, d_out))
@@ -115,11 +115,7 @@
         out[0] = x[e * CAP : (e + 1) * CAP]
         out[1] = d[e * CAP : (e + 1) * CAP]
     sel[...] = select
-    pick[...] = chosen.T.astype(BF16)
-    back = weight.T
-    high = back.astype(BF16)
-    w_hi[...] = high
-    w_lo[...] = (back - high.astype(F32)).astype(BF16)
+    weights[...] = weight
 
 
 def dispatch(routes_t, gates_t, tokens, d_out, experts):
@@ -129,8 +125,7 @@
         functools.partial(dispatch_kernel, experts),
         "dispatch",
         (array((2, CAP, quarter)),) * experts
-        + (array((slots, tok)),)
-        + (array((tok, slots)),) * 3,
+        + (array((slots, tok)), array((slots, tok), F32)),
         [hspec()] * 4,
         vspec(),
         [
@@ -142,6 +137,26 @@
         ],
     )(*(fixed(v) for v in (routes_t, gates_t, tokens, d_out)))
     return results[:experts], results[experts:]
+
+
+def turn_kernel(after, sel, weights, pick, mix):
+    slots = sel.shape[0]
+    pick[...] = sel[...].astype(F32).T.astype(BF16)
+    back = weights[...].T
+    high = back.astype(BF16)
+    mix[:, :slots] = high
+    mix[:, slots:] = (back - high.astype(F32)).astype(BF16)
+
+
+def turn(after, sel, weights):
+    slots, tok = sel.shape
+    return call(
+        turn_kernel,
+        "turn",
+        (array((tok, slots)), array((tok, 2 * slots))),
+        [aspec()] + [vspec()] * 2,
+        vspec(),
+    )(after, sel, weights)
 
 
 def quarter_of(me, flip, size):
@@ -399,42 +414,59 @@
 
 
 def combine_kernel(places, *refs):
-    w_hi, w_lo, pick, sel, routes, gates = refs[:6]
-    back = [refs[6 + places.index(p)] for p in range(len(places))]
-    mixed, d_tokens, d_gates = refs[-3:]
+    mix, pick, sel, routes, gates = refs[:5]
+    back = [refs[5 + places.index(p)] for p in range(len(places))]
+    mixed, d_tokens, d_gates, held_mixed, held_tokens, held_gates, sem = refs[5 + len(places) :]
     tiles, cap, lanes = back[0].shape
     slots, tok = sel.shape
     topk = routes.shape[0]
     experts = len(back)
     middle = tiles // 2
-
-    def all_rows(first):
+    span = middle // 2
+
+    def columns(first):
         return jnp.concatenate(
-            [jnp.concatenate([b[first + j] for j in range(middle)], axis=1) for b in back], axis=0
+            [jnp.concatenate([b[first + j] for j in range(span)], axis=1) for b in back], axis=0
         )
 
-    o = all_rows(0)
-    mixed[...] = (dot(w_hi[...], o) + dot(w_lo[...], o)).astype(BF16)
-    d_tokens[...] = dot(pick[...], all_rows(middle)).astype(BF16)
-    both = jnp.concatenate([b[tiles - 1] for b in back], axis=0).astype(F32)
-    per_slot = both[:, :1] + both[:, lanes // 2 : lanes // 2 + 1]
-    spread = sel[...].astype(F32) * per_slot
-    per_expert = jnp.sum(spread.reshape(experts, cap, tok), axis=1)
-    match = routes[...][None] == relative(experts, topk, tok)
-    scaled = jnp.sum(jnp.where(match, per_expert[:, None, :], 0.0), axis=0)
-    d_gates[...] = scaled / gates[...]
-
-
-def combine(places, back, w_hi, w_lo, pick, sel, routes_t, gates_t):
+    copies = []
+    for c in range(2):
+        part = slice(c * span * lanes, (c + 1) * span * lanes)
+        o = columns(c * span)
+        both = jnp.concatenate([o, o], axis=0)
+        held_mixed[:, part] = dot(mix[...], both).astype(BF16)
+        copies.append(fetch(held_mixed.at[:, part], mixed.at[:, part], sem.at[0, c]))
+        held_tokens[:, part] = dot(pick[...], columns(middle + c * span)).astype(BF16)
+        copies.append(fetch(held_tokens.at[:, part], d_tokens.at[:, part], sem.at[1, c]))
+        if c == 0:
+            pair = jnp.concatenate([b[tiles - 1] for b in back], axis=0).astype(F32)
+            per_slot = pair[:, :1] + pair[:, lanes // 2 : lanes // 2 + 1]
+            spread = sel[...].astype(F32) * per_slot
+            per_expert = jnp.sum(spread.reshape(experts, cap, tok), axis=1)
+            match = routes[...][None] == relative(experts, topk, tok)
+            scaled = jnp.sum(jnp.where(match, per_expert[:, None, :], 0.0), axis=0)
+            held_gates[...] = scaled / gates[...]
+            copies.append(fetch(held_gates, d_gates, sem.at[2, 0]))
+    for copy in copies:
+        copy.wait()
+
+
+def combine(places, back, mix, pick, sel, routes_t, gates_t):
     quarter = back[0].shape[0] // 2 * LANES
     topk, tok = routes_t.shape
     return call(
         functools.partial(combine_kernel, places),
         "combine",
         (array((tok, quarter)), array((tok, quarter)), array((topk, tok), F32)),
-        [vspec()] * (6 + len(back)),
-        vspec(),
-    )(w_hi, w_lo, pick, sel, routes_t, gates_t, *back)
+        [vspec()] * (5 + len(back)),
+        hspec(),
+        [
+            pltpu.VMEM((tok, quarter), BF16),
+            pltpu.VMEM((tok, quarter), BF16),
+            pltpu.VMEM((topk, tok), F32),
+            pltpu.SemaphoreType.DMA((3, 2)),
+        ],
+    )(mix, pick, sel, routes_t, gates_t, *back)
 
 
 def swap(x, flip):
@@ -453,7 +485,7 @@
 def on_device(tokens, routes, gates, w_gate, w_up, w_down, d_out):
     sources = lax.axis_size("ctx")
     routes_t, gates_t = routes.T, gates.T
-    parts, (sel, pick, w_hi, w_lo) = dispatch(routes_t, gates_t, tokens, d_out, sources)
+    parts, (sel, weights) = dispatch(routes_t, gates_t, tokens, d_out, sources)
     got = exchange(parts, range(sources), sources)
     early = sources // 2
     cut = early * CAP
@@ -465,9 +497,8 @@
     far_x = swap(rest_x, 2)
     far_d = swap(rest_d, 2)
     vg, vu, vd = load(first, w_gate[0], w_up[0], w_down[0])
-    firsts = (first, swap(first, 1), far_first, swap(far_first, 1))
-    across = jnp.concatenate([swap(piece, 1) for piece in pass_on(vg, far_x, 1)])
-    xs = (rest_x, swap(rest_x, 1), far_x, across)
+    firsts = (first, swap(pass_on(vg, first, 1)[0], 1), far_first, swap(pass_on(vg, far_first, 1)[0], 1))
+    xs = (rest_x, swap(rest_x, 1), far_x, swap(pass_on(vg, far_x, 1)[0], 1))
     ds = (rest_d, swap(rest_d, 1), far_d, swap(far_d, 1))
 
     act, lin, hidden, send, keep_far, keep_own = forward(ds[3], ds[1], firsts, xs, vg, vu, vd)
@@ -476,13 +507,14 @@
     send_dx, keep_dx = input_grad((3, 2), dots, dots, dact, dlin, vg, vu, more=16)
     near_send = swap(send_dx, 1)
     send_dx_near, keep_dx_own = input_grad((1, 0), send_dx, dots, dact, dlin, vg, vu)
-    near_dx = swap(send_dx_near, 1)
     one, two, three = groups(sources)
     halves = (keep_far, near_out, keep_dx, near_send, dots)
     half_one = half(keep_dx_own, one, *halves, more=16)
     half_two = half(half_one, two, *halves)
+    near_dx = swap(send_dx_near, 1)
     grad_gate, grad_up = grads(half_one, 0, firsts, xs, (dact, dlin))
     half_three = half(fixed(grad_gate), three, *halves)
+    pick, mix = turn(vg, sel, weights)
     far_one, far_two, far_three = swap(half_one, 2), swap(half_two, 2), swap(half_three, 2)
     (grad_down,) = grads(half_one, 1, firsts, ds, (hidden,))
     keeps = (keep_own, near_out, keep_dx_own, near_dx)
@@ -492,7 +524,7 @@
     back_three = total(back_two[0], three, keeps, far_three, sums)
     places = [*one, *two, *three]
     back = exchange([*back_one, *back_two, *back_three], places, sources)
-    mixed, d_tokens, d_gates = combine(places, back, w_hi, w_lo, pick, sel, routes_t, gates_t)
+    mixed, d_tokens, d_gates = combine(places, back, mix, pick, sel, routes_t, gates_t)
     return (mixed, d_tokens, d_gates.T, grad_gate[None], grad_up[None], grad_down[None])
 
 

time: 60.8 us -> 60.3 us (level)
  starting transfers between devices: 36.7 us -> 34.3 us
  waiting for transfers between devices: 5.57 us -> 7.31 us
    ppermute x14, starting transfers between devices: 26.5 us -> 24.4 us  [exchange(): lax.ppermute(part, 'ctx', [(i, i ^ order[p]) for i in range(count)])]
    ppermute x14, waiting for transfers between devices: 3.36 us -> 4.3 us  [exchange(): lax.ppermute(part, 'ctx', [(i, i ^ order[p]) for i in range(count)])]
    ppermute x15, waiting for transfers between devices: 2.21 us -> 3.01 us  [swap(): return lax.ppermute(x, 'tp', [(i, i ^ flip) for i in range(4)])]
  transfers between devices with their start and end apart: 29 -> 29, of which waited for: 11 -> 9; matrix products, arithmetic and copies ran while one was open for 0% -> 0% of each run, Pallas kernels for 21% -> 22%
where the time goes in v5:
time: 60.3 us; the launch traced here: 60.1 us
  starting transfers between devices  34.3 us (57%)
  Pallas kernels  17.5 us (29%)
  waiting for transfers between devices  7.31 us (12%)
  between operations  0.87 us (1%)
    ppermute x14, starting transfers between devices, exchange(): lax.ppermute(part, 'ctx', [(i, i ^ order[p]) for i in range(count)])  24.4 us
    ppermute x15, starting transfers between devices, swap(): return lax.ppermute(x, 'tp', [(i, i ^ flip) for i in range(4)])  9.9 us
    pallas_call x2, Pallas kernels, grads(): call(functools.partial(grads_kernel, which, count), 'grads', (array(shape...  5.3 us
    ppermute x14, waiting for transfers between devices, exchange(): lax.ppermute(part, 'ctx', [(i, i ^ order[p]) for i in range(count)])  4.3 us
    pallas_call x1, Pallas kernels, load(): call(load_kernel, 'load', tuple((array(w.shape) for w in weights)), [aspe...  3.8 us
    ppermute x15, waiting for transfers between devices, swap(): return lax.ppermute(x, 'tp', [(i, i ^ flip) for i in range(4)])  3.01 us
    pallas_call x2, Pallas kernels, input_grad(): call(functools.partial(input_grad_kernel, flips), 'input_grad', (array((r...  2.22 us
    pallas_call x1, Pallas kernels, forward(): call(forward_kernel, 'forward', (array((rows, ff), F32),) * 2 + (array((r...  1.92 us
  transfers between devices with their start and end apart: 29, of which 9 were waited for; matrix products, arithmetic and copies ran while one was open for 0% of the time, Pallas kernels for 22%

profile of v5, /device:TPU:0, one launch (start us, length us, event | category | flops | bytes accessed | tf_op | source)
XLA Modules:
  0.0 60.1 jit_solution(489771972445156695)
XLA Ops:
  0.6 1.5 %dispatch.1 = (bf16[2,16,1024]{2,1,0:T(8,128)(2,1)S(1)}, bf16[2,16,1024]{2,1,0:T(8,128)(2,1)S(1)}, bf16[2,16,1024]{2,1,0:T(8,128)(2,1)S(1)}, bf16[2,16,1024]{2,1...) custom-call(s32[8,128]{1,0:T(8,128)} %bitcast.14, ...), custom_call_target="tpu_custom_call" | custom-call | tf_op jit(solution)/shard_map/dispatch/pallas_call | solution.py:124
  2.1 6.0 %collective-permute-start.2 = (bf16[2,16,1024]{2,1,0:T(8,128)(2,1)S(1)}, bf16[2,16,1024]{2,1,0:T(8,128)(2,1)S(1)}, u32[]{:S(2)}, u32[]{:S(2)}) collective-permute-start(bf16[2,16,1024]{2,1,0:T(8,128)(2,1)S(1)} %get-tuple-element.50), channel_id=1, source_target_pairs={{0,28},{4,24},{8,20},{12,16},{16,12},{20,8},{24,4},{28,0},{1,29},{... | collective-permute-start | bytes 196616 | tf_op jit(solution)/shard_map/ppermute | solution.py:480
  8.4 4.1 %collective-permute-start.9 = (bf16[2,16,1024]{2,1,0:T(8,128)(2,1)S(1)}, bf16[2,16,1024]{2,1,0:T(8,128)(2,1)S(1)}, u32[]{:S(2)}, u32[]{:S(2)}) collective-permute-start(bf16[2,16,1024]{2,1,0:T(8,128)(2,1)S(1)} %get-tuple-element.59), channel_id=1, source_target_pairs={{0,20},{4,16},{8,28},{12,24},{16,4},{20,0},{24,12},{28,8},{1,21},{... | collective-permute-start | bytes 196616 | tf_op jit(solution)/shard_map/ppermute | solution.py:480
  12.6 1.7 %collective-permute-start.7 = (bf16[2,16,1024]{2,1,0:T(8,128)(2,1)S(1)}, bf16[2,16,1024]{2,1,0:T(8,128)(2,1)S(1)}, u32[]{:S(2)}, u32[]{:S(2)}) collective-permute-start(bf16[2,16,1024]{2,1,0:T(8,128)(2,1)S(1)} %get-tuple-element.57), channel_id=1, source_target_pairs={{0,12},{4,8},{8,4},{12,0},{16,28},{20,24},{24,20},{28,16},{1,13},{... | collective-permute-start | bytes 196616 | tf_op jit(solution)/shard_map/ppermute | solution.py:480
  15.6 1.6 %collective-permute-start.4 = (bf16[4,2,16,1024]{3,2,1,0:T(8,128)(2,1)S(1)}, bf16[4,2,16,1024]{3,2,1,0:T(8,128)(2,1)S(1)}, u32[]{:S(2)}, u32[]{:S(2)}) collective-permute-start(bf16[4,2,16,1024]{3,2,1,0:T(8,128)(2,1)S(1)} %pad_maximum_fusion.after.x.refs_0_), channel_id=1, source_target_pairs={{0,2},{1,3},{2,0},{3,1},{4,6},{5,7},{6,4},{7,5},{8,10},{9,11},{10,... | collective-permute-start | bytes 786440 | tf_op jit(solution)/shard_map/ppermute | solution.py:473
  17.7 1.7 %collective-permute-done.8 = bf16[2,16,1024]{2,1,0:T(8,128)(2,1)S(1)} collective-permute-done((bf16[2,16,1024]{2,1,0:T(8,128)(2,1)S(1)}, bf16[2,16,1024]{2,1,0:T(8,128)(2,1)S(1)}, u32[]{:S(2)}, u32[]{:S(2)}) %collective-permute-start.8) | collective-permute-done | bytes 65568 | tf_op jit(solution)/shard_map/ppermute | solution.py:480
  19.5 1.6 %collective-permute-start.11 = (bf16[4,16,1024]{2,1,0:T(8,128)(2,1)S(1)}, bf16[4,16,1024]{2,1,0:T(8,128)(2,1)S(1)}, u32[]{:S(2)}, u32[]{:S(2)}) collective-permute-start(bf16[4,16,1024]{2,1,0:T(8,128)(2,1)S(1)} %pad_maximum_fusion.1.refs_4_), channel_id=1, source_target_pairs={{0,2},{1,3},{2,0},{3,1},{4,6},{5,7},{6,4},{7,5},{8,10},{9,11},{10,... | collective-permute-start | bytes 393224 | tf_op jit(solution)/shard_map/ppermute | solution.py:473
  21.7 3.8 %load.1 = (bf16[4096,384]{1,0:T(8,128)(2,1)S(1)}, bf16[4096,384]{1,0:T(8,128)(2,1)S(1)}, bf16[384,4096]{1,0:T(8,128)(2,1)S(1)}) custom-call(bf16[4,2,16,1024]{3,2,1,0:T(8,128)(2,1)S(1)} %pad_maximum_fusion.after.x.refs_0_, bf16[4096,384]{1,0:T(8,128)(2,1)} %bitcast.21, bf16[4096,384]{1,0:T(8,128)(2,1)} %bitcast.22, bf16[384,4096]{1,0:T(8,128)(2,1)} %bitcast.23), custom_call_target="tpu_custom_call" | custom-call | tf_op jit(solution)/shard_map/load/pallas_call | solution.py:180
  26.3 2.0 %collective-permute-done.14.x.refs_6_ = bf16[4,16,1024]{2,1,0:T(8,128)(2,1)S(1)} collective-permute-done((bf16[4,16,1024]{2,1,0:T(8,128)(2,1)S(1)}, bf16[4,16,1024]{2,1,0:T(8,128)(2,1)S(1)}, u32[]{:S(2)}, u32[]{:S(2)}) %collective-permute-start.14) | collective-permute-done | bytes 131104 | tf_op jit(solution)/shard_map/ppermute | solution.py:473
  29.8 1.9 %forward.1 = (f32[128,384]{1,0:T(8,128)S(1)}, f32[128,384]{1,0:T(8,128)S(1)}, bf16[128,384]{1,0:T(8,128)(2,1)S(1)}, bf16[2,128,1024]{2,1,0:T(8,128)(2,1)S(1)}, f...) custom-call(bf16[4,16,1024]{2,1,0:T(8,128)(2,1)S(1)} %collective-permute-done.12.after.refs_7_, ...), custom_call_target="tpu_custom_call" | custom-call | tf_op jit(solution)/shard_map/forward/pallas_call | solution.py:235
  32.2 1.2 %hidden_grad.1 = (bf16[128,384]{1,0:T(8,128)(2,1)S(1)}, bf16[128,384]{1,0:T(8,128)(2,1)S(1)}, f32[8,128]{1,0:T(8,128)S(1)}) custom-call(bf16[4,2,16,1024]{3,2,1,0:T(8,128)(2,1)S(1)} %pad_maximum_fusion.after.x.refs_0_, bf16[4,2,16,1024]{3,2,1,0:T(8,128)(2,1)S(1)} %collective-permute-done.3.refs_1_, ...), custom_call_target="tpu_custom_call" | custom-call | tf_op jit(solution)/shard_map/hidden_grad/pallas_call | solution.py:267
  33.4 1.1 %input_grad.2 = (bf16[144,1024]{1,0:T(8,128)(2,1)S(1)}, f32[128,1024]{1,0:T(8,128)S(1)}) custom-call(f32[8,128]{1,0:T(8,128)S(1)} %get-tuple-element.65.after.dots, f32[8,128]{1,0:T(8,128)S(1)} %get-tuple-element.65.after.dots, bf16[128,384]{1,0:T(8,128)(2,1)S(1)} %get-tuple-element.66.dact.refs_8_, bf16[128,384]{1,0:T(8,128)(2,1)S(1)} %get-tuple-element.67.dlin.refs_9_, ...), custom_call_target="tpu_custom_call" | custom-call | tf_op jit(solution)/shard_map/input_grad/pallas_call | solution.py:305
  34.7 1.1 %input_grad.3 = (bf16[128,1024]{1,0:T(8,128)(2,1)S(1)}, f32[128,1024]{1,0:T(8,128)S(1)}) custom-call(bf16[144,1024]{1,0:T(8,128)(2,1)S(1)} %get-tuple-element.68.after, f32[8,128]{1,0:T(8,128)S(1)} %get-tuple-element.65.after.dots, bf16[128,384]{1,0:T(8,128)(2,1)S(1)} %get-tuple-element.66.dact.refs_8_, bf16[128,384]{1,0:T(8,128)(2,1)S(1)} %get-tuple-element.67.dlin.refs_9_, ...), custom_call_target="tpu_custom_call" | custom-call | tf_op jit(solution)/shard_map/input_grad/pallas_call | solution.py:305
  36.3 1.6 %collective-permute-start.19 = (bf16[80,1024]{1,0:T(8,128)(2,1)S(1)}, bf16[80,1024]{1,0:T(8,128)(2,1)S(1)}, u32[]{:S(2)}, u32[]{:S(2)}) collective-permute-start(bf16[80,1024]{1,0:T(8,128)(2,1)S(1)} %half.3.after), channel_id=1, source_target_pairs={{0,2},{1,3},{2,0},{3,1},{4,6},{5,7},{6,4},{7,5},{8,10},{9,11},{10,... | collective-permute-start | bytes 491528 | tf_op jit(solution)/shard_map/ppermute | solution.py:473
  38.5 3.2 %grads.2 = (bf16[4096,384]{1,0:T(8,128)(2,1)}, bf16[4096,384]{1,0:T(8,128)(2,1)}) custom-call(bf16[80,1024]{1,0:T(8,128)(2,1)S(1)} %half.3.after, bf16[4,2,16,1024]{3,2,1,0:T(8,128)(2,1)S(1)} %pad_maximum_fusion.after.x.refs_0_, bf16[4,2,16,1024]{3,2,1,0:T(8,128)(2,1)S(1)} %collective-permute-done.3.refs_1_, ...), custom_call_target="tpu_custom_call" | custom-call | flops 805306368 | bytes 6291456 | tf_op jit(solution)/shard_map/grads/pallas_call | solution.py:368
  41.7 1.6 %collective-permute-start.26 = (bf16[96,1024]{1,0:T(8,128)(2,1)S(1)}, bf16[96,1024]{1,0:T(8,128)(2,1)S(1)}, u32[]{:S(2)}, u32[]{:S(2)}) collective-permute-start(bf16[96,1024]{1,0:T(8,128)(2,1)S(1)} %half.5), channel_id=1, source_target_pairs={{0,2},{1,3},{2,0},{3,1},{4,6},{5,7},{6,4},{7,5},{8,10},{9,11},{10,... | collective-permute-start | bytes 589832 | tf_op jit(solution)/shard_map/ppermute | solution.py:473
  43.5 3.3 %collective-permute-start.20 = (bf16[17,16,128]{2,1,0:T(8,128)(2,1)S(1)}, bf16[17,16,128]{2,1,0:T(8,128)(2,1)S(1)}, u32[]{:S(2)}, u32[]{:S(2)}) collective-permute-start(bf16[17,16,128]{2,1,0:T(8,128)(2,1)S(1)} %get-tuple-element.76.after), channel_id=1, source_target_pairs={{0,28},{4,24},{8,20},{12,16},{16,12},{20,8},{24,4},{28,0},{1,29},{... | collective-permute-start | bytes 208904 | tf_op jit(solution)/shard_map/ppermute | solution.py:480
  46.7 1.1 %collective-permute-start.21 = (bf16[17,16,128]{2,1,0:T(8,128)(2,1)S(1)}, bf16[17,16,128]{2,1,0:T(8,128)(2,1)S(1)}, u32[]{:S(2)}, u32[]{:S(2)}) collective-permute-start(bf16[17,16,128]{2,1,0:T(8,128)(2,1)S(1)} %get-tuple-element.77), channel_id=1, source_target_pairs={{0,24},{4,28},{8,16},{12,20},{16,8},{20,12},{24,0},{28,4},{1,25},{... | collective-permute-start | bytes 208904 | tf_op jit(solution)/shard_map/ppermute | solution.py:480
  48.0 0.9 %collective-permute-start.23 = (bf16[17,16,128]{2,1,0:T(8,128)(2,1)S(1)}, bf16[17,16,128]{2,1,0:T(8,128)(2,1)S(1)}, u32[]{:S(2)}, u32[]{:S(2)}) collective-permute-start(bf16[17,16,128]{2,1,0:T(8,128)(2,1)S(1)} %get-tuple-element.78.after), channel_id=1, source_target_pairs={{0,12},{4,8},{8,4},{12,0},{16,28},{20,24},{24,20},{28,16},{1,13},{... | collective-permute-start | bytes 208904 | tf_op jit(solution)/shard_map/ppermute | solution.py:480
  48.9 3.4 %collective-permute-start.24 = (bf16[17,16,128]{2,1,0:T(8,128)(2,1)S(1)}, bf16[17,16,128]{2,1,0:T(8,128)(2,1)S(1)}, u32[]{:S(2)}, u32[]{:S(2)}) collective-permute-start(bf16[17,16,128]{2,1,0:T(8,128)(2,1)S(1)} %get-tuple-element.79), channel_id=1, source_target_pairs={{0,20},{4,16},{8,28},{12,24},{16,4},{20,0},{24,12},{28,8},{1,21},{... | collective-permute-start | bytes 208904 | tf_op jit(solution)/shard_map/ppermute | solution.py:480
  53.1 1.4 %collective-permute-start.27 = (bf16[17,16,128]{2,1,0:T(8,128)(2,1)S(1)}, bf16[17,16,128]{2,1,0:T(8,128)(2,1)S(1)}, u32[]{:S(2)}, u32[]{:S(2)}) collective-permute-start(bf16[17,16,128]{2,1,0:T(8,128)(2,1)S(1)} %get-tuple-element.82), channel_id=1, source_target_pairs={{0,8},{4,12},{8,0},{12,4},{16,24},{20,28},{24,16},{28,20},{1,9},{5... | collective-permute-start | bytes 208904 | tf_op jit(solution)/shard_map/ppermute | solution.py:480
  54.5 1.0 %collective-permute-start.28 = (bf16[17,16,128]{2,1,0:T(8,128)(2,1)S(1)}, bf16[17,16,128]{2,1,0:T(8,128)(2,1)S(1)}, u32[]{:S(2)}, u32[]{:S(2)}) collective-permute-start(bf16[17,16,128]{2,1,0:T(8,128)(2,1)S(1)} %get-tuple-element.83), channel_id=1, source_target_pairs={{0,4},{4,0},{8,12},{12,8},{16,20},{20,16},{24,28},{28,24},{1,5},{5... | collective-permute-start | bytes 208904 | tf_op jit(solution)/shard_map/ppermute | solution.py:480
  55.6 2.1 %grads.3 = bf16[384,4096]{1,0:T(8,128)(2,1)} custom-call(bf16[80,1024]{1,0:T(8,128)(2,1)S(1)} %half.3.after, bf16[4,2,16,1024]{3,2,1,0:T(8,128)(2,1)S(1)} %pad_maximum_fusion.after.x.refs_0_, bf16[4,2,16,1024]{3,2,1,0:T(8,128)(2,1)S(1)} %collective-permute-done.3.refs_1_, bf16[4,2,16,1024]{3,2,1,0:T(8,128)(2,1)S(1)} %collective-permute-done.4.x.refs_2_, ...), custom_call_target="tpu_custom_call" | custom-call | flops 402653184 | bytes 3145728 | tf_op jit(solution)/shard_map/grads/pallas_call | solution.py:368
  59.1 1.1 %combine.1 = (bf16[128,1024]{1,0:T(8,128)(2,1)}, bf16[128,1024]{1,0:T(8,128)(2,1)}, f32[8,128]{1,0:T(8,128)}) custom-call(bf16[128,256]{1,0:T(8,128)(2,1)S(1)} %get-tuple-element.54.refs_0_, bf16[128,128]{1,0:T(8,128)(2,1)S(1)} %get-tuple-element.55.refs_1_, bf16[128,128]{1,0:T(8,128)(2,1)S(1)} %get-tuple-element.52.sel.refs_2_, s32[8,128]{1,0:T(8,128)S(1)} %bitcast.15, ...), custom_call_target="tpu_custom_call" | custom-call | tf_op jit(solution)/shard_map/combine/pallas_call | solution.py:457
  (64 shorter events, 9.4 us)
Async XLA Ops:
  2.1 10.4 %collective-permute-start.2 = (bf16[2,16,1024]{2,1,0:T(8,128)(2,1)S(1)}, bf16[2,16,1024]{2,1,0:T(8,128)(2,1)S(1)}, u32[]{:S(2)}, u32[]{:S(2)}) collective-permute-start(bf16[2,16,1024]{2,1,0:T(8,128)(2,1)S(1)} %get-tuple-element.50), channel_id=1, source_target_pairs={{0,28},{4,24},{8,20},{12,16},{16,12},{20,8},{24,4},{28,0},{1,29},{... | collective-permute-start | bytes 196616 | tf_op jit(solution)/shard_map/ppermute | solution.py:480
  8.2 6.9 %collective-permute-start.1 = (bf16[2,16,1024]{2,1,0:T(8,128)(2,1)S(1)}, bf16[2,16,1024]{2,1,0:T(8,128)(2,1)S(1)}, u32[]{:S(2)}, u32[]{:S(2)}) collective-permute-start(bf16[2,16,1024]{2,1,0:T(8,128)(2,1)S(1)} %get-tuple-element.49), channel_id=1, source_target_pairs={{0,24},{4,28},{8,16},{12,20},{16,8},{20,12},{24,0},{28,4},{1,25},{... | collective-permute-start | bytes 196616 | tf_op jit(solution)/shard_map/ppermute | solution.py:480
  8.4 7.2 %collective-permute-start = (bf16[2,16,1024]{2,1,0:T(8,128)(2,1)S(1)}, bf16[2,16,1024]{2,1,0:T(8,128)(2,1)S(1)}, u32[]{:S(2)}, u32[]{:S(2)}) collective-permute-start(bf16[2,16,1024]{2,1,0:T(8,128)(2,1)S(1)} %get-tuple-element.48), channel_id=1, source_target_pairs={{0,8},{4,12},{8,0},{12,4},{16,24},{20,28},{24,16},{28,20},{1,9},{5... | collective-permute-start | bytes 196616 | tf_op jit(solution)/shard_map/ppermute | solution.py:480
  8.4 9.3 %collective-permute-start.9 = (bf16[2,16,1024]{2,1,0:T(8,128)(2,1)S(1)}, bf16[2,16,1024]{2,1,0:T(8,128)(2,1)S(1)}, u32[]{:S(2)}, u32[]{:S(2)}) collective-permute-start(bf16[2,16,1024]{2,1,0:T(8,128)(2,1)S(1)} %get-tuple-element.59), channel_id=1, source_target_pairs={{0,20},{4,16},{8,28},{12,24},{16,4},{20,0},{24,12},{28,8},{1,21},{... | collective-permute-start | bytes 196616 | tf_op jit(solution)/shard_map/ppermute | solution.py:480
  12.5 6.8 %collective-permute-start.8 = (bf16[2,16,1024]{2,1,0:T(8,128)(2,1)S(1)}, bf16[2,16,1024]{2,1,0:T(8,128)(2,1)S(1)}, u32[]{:S(2)}, u32[]{:S(2)}) collective-permute-start(bf16[2,16,1024]{2,1,0:T(8,128)(2,1)S(1)} %get-tuple-element.58), channel_id=1, source_target_pairs={{0,16},{4,20},{8,24},{12,28},{16,0},{20,4},{24,8},{28,12},{1,17},{... | collective-permute-start | bytes 196616 | tf_op jit(solution)/shard_map/ppermute | solution.py:480
  12.6 6.8 %collective-permute-start.7 = (bf16[2,16,1024]{2,1,0:T(8,128)(2,1)S(1)}, bf16[2,16,1024]{2,1,0:T(8,128)(2,1)S(1)}, u32[]{:S(2)}, u32[]{:S(2)}) collective-permute-start(bf16[2,16,1024]{2,1,0:T(8,128)(2,1)S(1)} %get-tuple-element.57), channel_id=1, source_target_pairs={{0,12},{4,8},{8,4},{12,0},{16,28},{20,24},{24,20},{28,16},{1,13},{... | collective-permute-start | bytes 196616 | tf_op jit(solution)/shard_map/ppermute | solution.py:480
  15.1 4.3 %collective-permute-start.6 = (bf16[2,16,1024]{2,1,0:T(8,128)(2,1)S(1)}, bf16[2,16,1024]{2,1,0:T(8,128)(2,1)S(1)}, u32[]{:S(2)}, u32[]{:S(2)}) collective-permute-start(bf16[2,16,1024]{2,1,0:T(8,128)(2,1)S(1)} %get-tuple-element.56), channel_id=1, source_target_pairs={{0,4},{4,0},{8,12},{12,8},{16,20},{20,16},{24,28},{28,24},{1,5},{5... | collective-permute-start | bytes 196616 | tf_op jit(solution)/shard_map/ppermute | solution.py:480
  15.6 10.0 %collective-permute-start.4 = (bf16[4,2,16,1024]{3,2,1,0:T(8,128)(2,1)S(1)}, bf16[4,2,16,1024]{3,2,1,0:T(8,128)(2,1)S(1)}, u32[]{:S(2)}, u32[]{:S(2)}) collective-permute-start(bf16[4,2,16,1024]{3,2,1,0:T(8,128)(2,1)S(1)} %pad_maximum_fusion.after.x.refs_0_), channel_id=1, source_target_pairs={{0,2},{1,3},{2,0},{3,1},{4,6},{5,7},{6,4},{7,5},{8,10},{9,11},{10,... | collective-permute-start | bytes 786440 | tf_op jit(solution)/shard_map/ppermute | solution.py:473
  19.4 8.8 %collective-permute-start.10 = (bf16[4,16,1024]{2,1,0:T(8,128)(2,1)S(1)}, bf16[4,16,1024]{2,1,0:T(8,128)(2,1)S(1)}, u32[]{:S(2)}, u32[]{:S(2)}) collective-permute-start(bf16[4,16,1024]{2,1,0:T(8,128)(2,1)S(1)} %pad_maximum_fusion.1.refs_4_), channel_id=1, source_target_pairs={{0,1},{1,0},{2,3},{3,2},{4,5},{5,4},{6,7},{7,6},{8,9},{9,8},{10,11... | collective-permute-start | bytes 393224 | tf_op jit(solution)/shard_map/ppermute | solution.py:473
  19.5 6.7 %collective-permute-start.11 = (bf16[4,16,1024]{2,1,0:T(8,128)(2,1)S(1)}, bf16[4,16,1024]{2,1,0:T(8,128)(2,1)S(1)}, u32[]{:S(2)}, u32[]{:S(2)}) collective-permute-start(bf16[4,16,1024]{2,1,0:T(8,128)(2,1)S(1)} %pad_maximum_fusion.1.refs_4_), channel_id=1, source_target_pairs={{0,2},{1,3},{2,0},{3,1},{4,6},{5,7},{6,4},{7,5},{8,10},{9,11},{10,... | collective-permute-start | bytes 393224 | tf_op jit(solution)/shard_map/ppermute | solution.py:473
  21.1 7.1 %collective-permute-start.14 = (bf16[4,16,1024]{2,1,0:T(8,128)(2,1)S(1)}, bf16[4,16,1024]{2,1,0:T(8,128)(2,1)S(1)}, u32[]{:S(2)}, u32[]{:S(2)}) collective-permute-start(bf16[4,16,1024]{2,1,0:T(8,128)(2,1)S(1)} %pad_maximum_fusion.2.refs_4_), channel_id=1, source_target_pairs={{0,2},{1,3},{2,0},{3,1},{4,6},{5,7},{6,4},{7,5},{8,10},{9,11},{10,... | collective-permute-start | bytes 393224 | tf_op jit(solution)/shard_map/ppermute | solution.py:473
  25.6 4.2 %collective-permute-start.5 = (bf16[4,2,16,1024]{3,2,1,0:T(8,128)(2,1)S(1)}, bf16[4,2,16,1024]{3,2,1,0:T(8,128)(2,1)S(1)}, u32[]{:S(2)}, u32[]{:S(2)}) collective-permute-start(bf16[4,2,16,1024]{3,2,1,0:T(8,128)(2,1)S(1)} %pass_on.4), channel_id=1, source_target_pairs={{0,1},{1,0},{2,3},{3,2},{4,5},{5,4},{6,7},{7,6},{8,9},{9,8},{10,11... | collective-permute-start | bytes 786440 | tf_op jit(solution)/shard_map/ppermute | solution.py:473
  31.7 4.5 %collective-permute-start.16 = (bf16[2,128,1024]{2,1,0:T(8,128)(2,1)S(1)}, bf16[2,128,1024]{2,1,0:T(8,128)(2,1)S(1)}, u32[]{:S(2)}, u32[]{:S(2)}) collective-permute-start(bf16[2,128,1024]{2,1,0:T(8,128)(2,1)S(1)} %get-tuple-element.71), channel_id=1, source_target_pairs={{0,1},{1,0},{2,3},{3,2},{4,5},{5,4},{6,7},{7,6},{8,9},{9,8},{10,11... | collective-permute-start | bytes 1572872 | tf_op jit(solution)/shard_map/ppermute | solution.py:473
  35.8 7.5 %collective-permute-start.18 = (bf16[128,1024]{1,0:T(8,128)(2,1)S(1)}, bf16[128,1024]{1,0:T(8,128)(2,1)S(1)}, u32[]{:S(2)}, u32[]{:S(2)}) collective-permute-start(bf16[128,1024]{1,0:T(8,128)(2,1)S(1)} %get-tuple-element.75), channel_id=1, source_target_pairs={{0,1},{1,0},{2,3},{3,2},{4,5},{5,4},{6,7},{7,6},{8,9},{9,8},{10,11... | collective-permute-start | bytes 786440 | tf_op jit(solution)/shard_map/ppermute | solution.py:473
  36.3 7.1 %collective-permute-start.19 = (bf16[80,1024]{1,0:T(8,128)(2,1)S(1)}, bf16[80,1024]{1,0:T(8,128)(2,1)S(1)}, u32[]{:S(2)}, u32[]{:S(2)}) collective-permute-start(bf16[80,1024]{1,0:T(8,128)(2,1)S(1)} %half.3.after), channel_id=1, source_target_pairs={{0,2},{1,3},{2,0},{3,1},{4,6},{5,7},{6,4},{7,5},{8,10},{9,11},{10,... | collective-permute-start | bytes 491528 | tf_op jit(solution)/shard_map/ppermute | solution.py:473
  37.9 10.0 %collective-permute-start.22 = (bf16[96,1024]{1,0:T(8,128)(2,1)S(1)}, bf16[96,1024]{1,0:T(8,128)(2,1)S(1)}, u32[]{:S(2)}, u32[]{:S(2)}) collective-permute-start(bf16[96,1024]{1,0:T(8,128)(2,1)S(1)} %half.4), channel_id=1, source_target_pairs={{0,2},{1,3},{2,0},{3,1},{4,6},{5,7},{6,4},{7,5},{8,10},{9,11},{10,... | collective-permute-start | bytes 589832 | tf_op jit(solution)/shard_map/ppermute | solution.py:473
  41.7 10.5 %collective-permute-start.26 = (bf16[96,1024]{1,0:T(8,128)(2,1)S(1)}, bf16[96,1024]{1,0:T(8,128)(2,1)S(1)}, u32[]{:S(2)}, u32[]{:S(2)}) collective-permute-start(bf16[96,1024]{1,0:T(8,128)(2,1)S(1)} %half.5), channel_id=1, source_target_pairs={{0,2},{1,3},{2,0},{3,1},{4,6},{5,7},{6,4},{7,5},{8,10},{9,11},{10,... | collective-permute-start | bytes 589832 | tf_op jit(solution)/shard_map/ppermute | solution.py:473
  43.5 9.6 %collective-permute-start.20 = (bf16[17,16,128]{2,1,0:T(8,128)(2,1)S(1)}, bf16[17,16,128]{2,1,0:T(8,128)(2,1)S(1)}, u32[]{:S(2)}, u32[]{:S(2)}) collective-permute-start(bf16[17,16,128]{2,1,0:T(8,128)(2,1)S(1)} %get-tuple-element.76.after), channel_id=1, source_target_pairs={{0,28},{4,24},{8,20},{12,16},{16,12},{20,8},{24,4},{28,0},{1,29},{... | collective-permute-start | bytes 208904 | tf_op jit(solution)/shard_map/ppermute | solution.py:480
  46.7 7.8 %collective-permute-start.21 = (bf16[17,16,128]{2,1,0:T(8,128)(2,1)S(1)}, bf16[17,16,128]{2,1,0:T(8,128)(2,1)S(1)}, u32[]{:S(2)}, u32[]{:S(2)}) collective-permute-start(bf16[17,16,128]{2,1,0:T(8,128)(2,1)S(1)} %get-tuple-element.77), channel_id=1, source_target_pairs={{0,24},{4,28},{8,16},{12,20},{16,8},{20,12},{24,0},{28,4},{1,25},{... | collective-permute-start | bytes 208904 | tf_op jit(solution)/shard_map/ppermute | solution.py:480
  48.0 9.8 %collective-permute-start.23 = (bf16[17,16,128]{2,1,0:T(8,128)(2,1)S(1)}, bf16[17,16,128]{2,1,0:T(8,128)(2,1)S(1)}, u32[]{:S(2)}, u32[]{:S(2)}) collective-permute-start(bf16[17,16,128]{2,1,0:T(8,128)(2,1)S(1)} %get-tuple-element.78.after), channel_id=1, source_target_pairs={{0,12},{4,8},{8,4},{12,0},{16,28},{20,24},{24,20},{28,16},{1,13},{... | collective-permute-start | bytes 208904 | tf_op jit(solution)/shard_map/ppermute | solution.py:480
  48.9 9.7 %collective-permute-start.24 = (bf16[17,16,128]{2,1,0:T(8,128)(2,1)S(1)}, bf16[17,16,128]{2,1,0:T(8,128)(2,1)S(1)}, u32[]{:S(2)}, u32[]{:S(2)}) collective-permute-start(bf16[17,16,128]{2,1,0:T(8,128)(2,1)S(1)} %get-tuple-element.79), channel_id=1, source_target_pairs={{0,20},{4,16},{8,28},{12,24},{16,4},{20,0},{24,12},{28,8},{1,21},{... | collective-permute-start | bytes 208904 | tf_op jit(solution)/shard_map/ppermute | solution.py:480
  52.2 6.3 %collective-permute-start.25 = (bf16[17,16,128]{2,1,0:T(8,128)(2,1)S(1)}, bf16[17,16,128]{2,1,0:T(8,128)(2,1)S(1)}, u32[]{:S(2)}, u32[]{:S(2)}) collective-permute-start(bf16[17,16,128]{2,1,0:T(8,128)(2,1)S(1)} %get-tuple-element.80), channel_id=1, source_target_pairs={{0,16},{4,20},{8,24},{12,28},{16,0},{20,4},{24,8},{28,12},{1,17},{... | collective-permute-start | bytes 208904 | tf_op jit(solution)/shard_map/ppermute | solution.py:480
  53.1 5.5 %collective-permute-start.27 = (bf16[17,16,128]{2,1,0:T(8,128)(2,1)S(1)}, bf16[17,16,128]{2,1,0:T(8,128)(2,1)S(1)}, u32[]{:S(2)}, u32[]{:S(2)}) collective-permute-start(bf16[17,16,128]{2,1,0:T(8,128)(2,1)S(1)} %get-tuple-element.82), channel_id=1, source_target_pairs={{0,8},{4,12},{8,0},{12,4},{16,24},{20,28},{24,16},{28,20},{1,9},{5... | collective-permute-start | bytes 208904 | tf_op jit(solution)/shard_map/ppermute | solution.py:480
  54.5 4.6 %collective-permute-start.28 = (bf16[17,16,128]{2,1,0:T(8,128)(2,1)S(1)}, bf16[17,16,128]{2,1,0:T(8,128)(2,1)S(1)}, u32[]{:S(2)}, u32[]{:S(2)}) collective-permute-start(bf16[17,16,128]{2,1,0:T(8,128)(2,1)S(1)} %get-tuple-element.83), channel_id=1, source_target_pairs={{0,4},{4,0},{8,12},{12,8},{16,20},{20,16},{24,28},{28,24},{1,5},{5... | collective-permute-start | bytes 208904 | tf_op jit(solution)/shard_map/ppermute | solution.py:480
  (7 other events, 17.5 us)

commit v6 on v5

--- a/solution.py
+++ b/solution.py
@@ -497,7 +497,7 @@
     far_x = swap(rest_x, 2)
     far_d = swap(rest_d, 2)
     vg, vu, vd = load(first, w_gate[0], w_up[0], w_down[0])
-    firsts = (first, swap(pass_on(vg, first, 1)[0], 1), far_first, swap(pass_on(vg, far_first, 1)[0], 1))
+    firsts = (first, swap(pass_on(vg, first, 1)[0], 1), far_first, swap(far_first, 1))
     xs = (rest_x, swap(rest_x, 1), far_x, swap(pass_on(vg, far_x, 1)[0], 1))
     ds = (rest_d, swap(rest_d, 1), far_d, swap(far_d, 1))
 

time: 60.3 us -> 59.6 us (0.988)
  waiting for transfers between devices: 7.31 us -> 5.81 us
  starting transfers between devices: 34.3 us -> 35.2 us
    ppermute x15, waiting for transfers between devices: 3.01 us -> 2.19 us  [swap(): return lax.ppermute(x, 'tp', [(i, i ^ flip) for i in range(4)])]
    ppermute x14, waiting for transfers between devices: 4.3 us -> 3.62 us  [exchange(): lax.ppermute(part, 'ctx', [(i, i ^ order[p]) for i in range(count)])]
  transfers between devices with their start and end apart: 29 -> 29, of which waited for: 9 -> 8; matrix products, arithmetic and copies ran while one was open for 0% -> 0% of each run, Pallas kernels for 22% -> 22%
where the time goes in v6:
time: 59.6 us; the launch traced here: 59.4 us
  starting transfers between devices  35.2 us (59%)
  Pallas kernels  17.5 us (29%)
  waiting for transfers between devices  5.81 us (10%)
  between operations  0.85 us (1%)
    ppermute x14, starting transfers between devices, exchange(): lax.ppermute(part, 'ctx', [(i, i ^ order[p]) for i in range(count)])  24.9 us
    ppermute x15, starting transfers between devices, swap(): return lax.ppermute(x, 'tp', [(i, i ^ flip) for i in range(4)])  10.2 us
    pallas_call x2, Pallas kernels, grads(): call(functools.partial(grads_kernel, which, count), 'grads', (array(shape...  5.29 us
    pallas_call x1, Pallas kernels, load(): call(load_kernel, 'load', tuple((array(w.shape) for w in weights)), [aspe...  3.8 us
    ppermute x14, waiting for transfers between devices, exchange(): lax.ppermute(part, 'ctx', [(i, i ^ order[p]) for i in range(count)])  3.62 us
    pallas_call x2, Pallas kernels, input_grad(): call(functools.partial(input_grad_kernel, flips), 'input_grad', (array((r...  2.2 us
    ppermute x15, waiting for transfers between devices, swap(): return lax.ppermute(x, 'tp', [(i, i ^ flip) for i in range(4)])  2.19 us
    pallas_call x1, Pallas kernels, forward(): call(forward_kernel, 'forward', (array((rows, ff), F32),) * 2 + (array((r...  1.91 us
  transfers between devices with their start and end apart: 29, of which 8 were waited for; matrix products, arithmetic and copies ran while one was open for 0% of the time, Pallas kernels for 22%

profile of v6, /device:TPU:0, one launch (start us, length us, event | category | flops | bytes accessed | tf_op | source)
XLA Modules:
  0.0 59.4 jit_solution(10954586395959963109)
XLA Ops:
  0.6 1.5 %dispatch.1 = (bf16[2,16,1024]{2,1,0:T(8,128)(2,1)S(1)}, bf16[2,16,1024]{2,1,0:T(8,128)(2,1)S(1)}, bf16[2,16,1024]{2,1,0:T(8,128)(2,1)S(1)}, bf16[2,16,1024]{2,1...) custom-call(s32[8,128]{1,0:T(8,128)} %bitcast.14, ...), custom_call_target="tpu_custom_call" | custom-call | tf_op jit(solution)/shard_map/dispatch/pallas_call | solution.py:124
  2.1 6.0 %collective-permute-start.2 = (bf16[2,16,1024]{2,1,0:T(8,128)(2,1)S(1)}, bf16[2,16,1024]{2,1,0:T(8,128)(2,1)S(1)}, u32[]{:S(2)}, u32[]{:S(2)}) collective-permute-start(bf16[2,16,1024]{2,1,0:T(8,128)(2,1)S(1)} %get-tuple-element.50), channel_id=1, source_target_pairs={{0,28},{4,24},{8,20},{12,16},{16,12},{20,8},{24,4},{28,0},{1,29},{... | collective-permute-start | bytes 196616 | tf_op jit(solution)/shard_map/ppermute | solution.py:480
  8.4 4.1 %collective-permute-start.9 = (bf16[2,16,1024]{2,1,0:T(8,128)(2,1)S(1)}, bf16[2,16,1024]{2,1,0:T(8,128)(2,1)S(1)}, u32[]{:S(2)}, u32[]{:S(2)}) collective-permute-start(bf16[2,16,1024]{2,1,0:T(8,128)(2,1)S(1)} %get-tuple-element.59), channel_id=1, source_target_pairs={{0,20},{4,16},{8,28},{12,24},{16,4},{20,0},{24,12},{28,8},{1,21},{... | collective-permute-start | bytes 196616 | tf_op jit(solution)/shard_map/ppermute | solution.py:480
  12.6 1.7 %collective-permute-start.7 = (bf16[2,16,1024]{2,1,0:T(8,128)(2,1)S(1)}, bf16[2,16,1024]{2,1,0:T(8,128)(2,1)S(1)}, u32[]{:S(2)}, u32[]{:S(2)}) collective-permute-start(bf16[2,16,1024]{2,1,0:T(8,128)(2,1)S(1)} %get-tuple-element.57), channel_id=1, source_target_pairs={{0,12},{4,8},{8,4},{12,0},{16,28},{20,24},{24,20},{28,16},{1,13},{... | collective-permute-start | bytes 196616 | tf_op jit(solution)/shard_map/ppermute | solution.py:480
  14.2 0.8 %collective-permute-done.1 = bf16[2,16,1024]{2,1,0:T(8,128)(2,1)S(1)} collective-permute-done((bf16[2,16,1024]{2,1,0:T(8,128)(2,1)S(1)}, bf16[2,16,1024]{2,1,0:T(8,128)(2,1)S(1)}, u32[]{:S(2)}, u32[]{:S(2)}) %collective-permute-start.1) | collective-permute-done | bytes 65568 | tf_op jit(solution)/shard_map/ppermute | solution.py:480
  15.6 1.6 %collective-permute-start.4 = (bf16[4,2,16,1024]{3,2,1,0:T(8,128)(2,1)S(1)}, bf16[4,2,16,1024]{3,2,1,0:T(8,128)(2,1)S(1)}, u32[]{:S(2)}, u32[]{:S(2)}) collective-permute-start(bf16[4,2,16,1024]{3,2,1,0:T(8,128)(2,1)S(1)} %pad_maximum_fusion.after.x.refs_0_), channel_id=1, source_target_pairs={{0,2},{1,3},{2,0},{3,1},{4,6},{5,7},{6,4},{7,5},{8,10},{9,11},{10,... | collective-permute-start | bytes 786440 | tf_op jit(solution)/shard_map/ppermute | solution.py:473
  17.7 1.7 %collective-permute-done.8 = bf16[2,16,1024]{2,1,0:T(8,128)(2,1)S(1)} collective-permute-done((bf16[2,16,1024]{2,1,0:T(8,128)(2,1)S(1)}, bf16[2,16,1024]{2,1,0:T(8,128)(2,1)S(1)}, u32[]{:S(2)}, u32[]{:S(2)}) %collective-permute-start.8) | collective-permute-done | bytes 65568 | tf_op jit(solution)/shard_map/ppermute | solution.py:480
  19.4 1.6 %collective-permute-start.11 = (bf16[4,16,1024]{2,1,0:T(8,128)(2,1)S(1)}, bf16[4,16,1024]{2,1,0:T(8,128)(2,1)S(1)}, u32[]{:S(2)}, u32[]{:S(2)}) collective-permute-start(bf16[4,16,1024]{2,1,0:T(8,128)(2,1)S(1)} %pad_maximum_fusion.1.refs_4_), channel_id=1, source_target_pairs={{0,2},{1,3},{2,0},{3,1},{4,6},{5,7},{6,4},{7,5},{8,10},{9,11},{10,... | collective-permute-start | bytes 393224 | tf_op jit(solution)/shard_map/ppermute | solution.py:473
  21.6 3.8 %load.1 = (bf16[4096,384]{1,0:T(8,128)(2,1)S(1)}, bf16[4096,384]{1,0:T(8,128)(2,1)S(1)}, bf16[384,4096]{1,0:T(8,128)(2,1)S(1)}) custom-call(bf16[4,2,16,1024]{3,2,1,0:T(8,128)(2,1)S(1)} %pad_maximum_fusion.after.x.refs_0_, bf16[4096,384]{1,0:T(8,128)(2,1)} %bitcast.21, bf16[4096,384]{1,0:T(8,128)(2,1)} %bitcast.22, bf16[384,4096]{1,0:T(8,128)(2,1)} %bitcast.23), custom_call_target="tpu_custom_call" | custom-call | tf_op jit(solution)/shard_map/load/pallas_call | solution.py:180
  26.5 1.1 %collective-permute-done.14.x.refs_6_ = bf16[4,16,1024]{2,1,0:T(8,128)(2,1)S(1)} collective-permute-done((bf16[4,16,1024]{2,1,0:T(8,128)(2,1)S(1)}, bf16[4,16,1024]{2,1,0:T(8,128)(2,1)S(1)}, u32[]{:S(2)}, u32[]{:S(2)}) %collective-permute-start.14) | collective-permute-done | bytes 131104 | tf_op jit(solution)/shard_map/ppermute | solution.py:473
  29.3 1.9 %forward.1 = (f32[128,384]{1,0:T(8,128)S(1)}, f32[128,384]{1,0:T(8,128)S(1)}, bf16[128,384]{1,0:T(8,128)(2,1)S(1)}, bf16[2,128,1024]{2,1,0:T(8,128)(2,1)S(1)}, f...) custom-call(bf16[4,16,1024]{2,1,0:T(8,128)(2,1)S(1)} %collective-permute-done.12.after.refs_7_, ...), custom_call_target="tpu_custom_call" | custom-call | tf_op jit(solution)/shard_map/forward/pallas_call | solution.py:235
  31.6 1.2 %hidden_grad.1 = (bf16[128,384]{1,0:T(8,128)(2,1)S(1)}, bf16[128,384]{1,0:T(8,128)(2,1)S(1)}, f32[8,128]{1,0:T(8,128)S(1)}) custom-call(bf16[4,2,16,1024]{3,2,1,0:T(8,128)(2,1)S(1)} %pad_maximum_fusion.after.x.refs_0_, bf16[4,2,16,1024]{3,2,1,0:T(8,128)(2,1)S(1)} %collective-permute-done.3.refs_1_, ...), custom_call_target="tpu_custom_call" | custom-call | tf_op jit(solution)/shard_map/hidden_grad/pallas_call | solution.py:267
  32.8 1.1 %input_grad.2 = (bf16[144,1024]{1,0:T(8,128)(2,1)S(1)}, f32[128,1024]{1,0:T(8,128)S(1)}) custom-call(f32[8,128]{1,0:T(8,128)S(1)} %get-tuple-element.65.after.dots, f32[8,128]{1,0:T(8,128)S(1)} %get-tuple-element.65.after.dots, bf16[128,384]{1,0:T(8,128)(2,1)S(1)} %get-tuple-element.66.dact.refs_8_, bf16[128,384]{1,0:T(8,128)(2,1)S(1)} %get-tuple-element.67.dlin.refs_9_, ...), custom_call_target="tpu_custom_call" | custom-call | tf_op jit(solution)/shard_map/input_grad/pallas_call | solution.py:305
  34.1 1.1 %input_grad.3 = (bf16[128,1024]{1,0:T(8,128)(2,1)S(1)}, f32[128,1024]{1,0:T(8,128)S(1)}) custom-call(bf16[144,1024]{1,0:T(8,128)(2,1)S(1)} %get-tuple-element.68.after, f32[8,128]{1,0:T(8,128)S(1)} %get-tuple-element.65.after.dots, bf16[128,384]{1,0:T(8,128)(2,1)S(1)} %get-tuple-element.66.dact.refs_8_, bf16[128,384]{1,0:T(8,128)(2,1)S(1)} %get-tuple-element.67.dlin.refs_9_, ...), custom_call_target="tpu_custom_call" | custom-call | tf_op jit(solution)/shard_map/input_grad/pallas_call | solution.py:305
  35.7 1.6 %collective-permute-start.19 = (bf16[80,1024]{1,0:T(8,128)(2,1)S(1)}, bf16[80,1024]{1,0:T(8,128)(2,1)S(1)}, u32[]{:S(2)}, u32[]{:S(2)}) collective-permute-start(bf16[80,1024]{1,0:T(8,128)(2,1)S(1)} %half.3.after), channel_id=1, source_target_pairs={{0,2},{1,3},{2,0},{3,1},{4,6},{5,7},{6,4},{7,5},{8,10},{9,11},{10,... | collective-permute-start | bytes 491528 | tf_op jit(solution)/shard_map/ppermute | solution.py:473
  37.9 3.2 %grads.2 = (bf16[4096,384]{1,0:T(8,128)(2,1)}, bf16[4096,384]{1,0:T(8,128)(2,1)}) custom-call(bf16[80,1024]{1,0:T(8,128)(2,1)S(1)} %half.3.after, bf16[4,2,16,1024]{3,2,1,0:T(8,128)(2,1)S(1)} %pad_maximum_fusion.after.x.refs_0_, bf16[4,2,16,1024]{3,2,1,0:T(8,128)(2,1)S(1)} %collective-permute-done.3.refs_1_, ...), custom_call_target="tpu_custom_call" | custom-call | flops 805306368 | bytes 6291456 | tf_op jit(solution)/shard_map/grads/pallas_call | solution.py:368
  41.2 1.6 %collective-permute-start.26 = (bf16[96,1024]{1,0:T(8,128)(2,1)S(1)}, bf16[96,1024]{1,0:T(8,128)(2,1)S(1)}, u32[]{:S(2)}, u32[]{:S(2)}) collective-permute-start(bf16[96,1024]{1,0:T(8,128)(2,1)S(1)} %half.5), channel_id=1, source_target_pairs={{0,2},{1,3},{2,0},{3,1},{4,6},{5,7},{6,4},{7,5},{8,10},{9,11},{10,... | collective-permute-start | bytes 589832 | tf_op jit(solution)/shard_map/ppermute | solution.py:473
  42.9 3.8 %collective-permute-start.20 = (bf16[17,16,128]{2,1,0:T(8,128)(2,1)S(1)}, bf16[17,16,128]{2,1,0:T(8,128)(2,1)S(1)}, u32[]{:S(2)}, u32[]{:S(2)}) collective-permute-start(bf16[17,16,128]{2,1,0:T(8,128)(2,1)S(1)} %get-tuple-element.76.after), channel_id=1, source_target_pairs={{0,28},{4,24},{8,20},{12,16},{16,12},{20,8},{24,4},{28,0},{1,29},{... | collective-permute-start | bytes 208904 | tf_op jit(solution)/shard_map/ppermute | solution.py:480
  46.7 1.1 %collective-permute-start.21 = (bf16[17,16,128]{2,1,0:T(8,128)(2,1)S(1)}, bf16[17,16,128]{2,1,0:T(8,128)(2,1)S(1)}, u32[]{:S(2)}, u32[]{:S(2)}) collective-permute-start(bf16[17,16,128]{2,1,0:T(8,128)(2,1)S(1)} %get-tuple-element.77), channel_id=1, source_target_pairs={{0,24},{4,28},{8,16},{12,20},{16,8},{20,12},{24,0},{28,4},{1,25},{... | collective-permute-start | bytes 208904 | tf_op jit(solution)/shard_map/ppermute | solution.py:480
  48.6 3.6 %collective-permute-start.24 = (bf16[17,16,128]{2,1,0:T(8,128)(2,1)S(1)}, bf16[17,16,128]{2,1,0:T(8,128)(2,1)S(1)}, u32[]{:S(2)}, u32[]{:S(2)}) collective-permute-start(bf16[17,16,128]{2,1,0:T(8,128)(2,1)S(1)} %get-tuple-element.79), channel_id=1, source_target_pairs={{0,20},{4,16},{8,28},{12,24},{16,4},{20,0},{24,12},{28,8},{1,21},{... | collective-permute-start | bytes 208904 | tf_op jit(solution)/shard_map/ppermute | solution.py:480
  52.3 1.7 %collective-permute-start.27 = (bf16[17,16,128]{2,1,0:T(8,128)(2,1)S(1)}, bf16[17,16,128]{2,1,0:T(8,128)(2,1)S(1)}, u32[]{:S(2)}, u32[]{:S(2)}) collective-permute-start(bf16[17,16,128]{2,1,0:T(8,128)(2,1)S(1)} %get-tuple-element.82), channel_id=1, source_target_pairs={{0,8},{4,12},{8,0},{12,4},{16,24},{20,28},{24,16},{28,20},{1,9},{5... | collective-permute-start | bytes 208904 | tf_op jit(solution)/shard_map/ppermute | solution.py:480
  54.1 1.4 %collective-permute-start.28 = (bf16[17,16,128]{2,1,0:T(8,128)(2,1)S(1)}, bf16[17,16,128]{2,1,0:T(8,128)(2,1)S(1)}, u32[]{:S(2)}, u32[]{:S(2)}) collective-permute-start(bf16[17,16,128]{2,1,0:T(8,128)(2,1)S(1)} %get-tuple-element.83), channel_id=1, source_target_pairs={{0,4},{4,0},{8,12},{12,8},{16,20},{20,16},{24,28},{28,24},{1,5},{5... | collective-permute-start | bytes 208904 | tf_op jit(solution)/shard_map/ppermute | solution.py:480
  55.6 2.1 %grads.3 = bf16[384,4096]{1,0:T(8,128)(2,1)} custom-call(bf16[80,1024]{1,0:T(8,128)(2,1)S(1)} %half.3.after, bf16[4,2,16,1024]{3,2,1,0:T(8,128)(2,1)S(1)} %pad_maximum_fusion.after.x.refs_0_, bf16[4,2,16,1024]{3,2,1,0:T(8,128)(2,1)S(1)} %collective-permute-done.3.refs_1_, bf16[4,2,16,1024]{3,2,1,0:T(8,128)(2,1)S(1)} %collective-permute-done.4.refs_2_, ...), custom_call_target="tpu_custom_call" | custom-call | flops 402653184 | bytes 3145728 | tf_op jit(solution)/shard_map/grads/pallas_call | solution.py:368
  58.4 1.0 %combine.1 = (bf16[128,1024]{1,0:T(8,128)(2,1)}, bf16[128,1024]{1,0:T(8,128)(2,1)}, f32[8,128]{1,0:T(8,128)}) custom-call(bf16[128,256]{1,0:T(8,128)(2,1)S(1)} %get-tuple-element.54.refs_0_, bf16[128,128]{1,0:T(8,128)(2,1)S(1)} %get-tuple-element.55.refs_1_, bf16[128,128]{1,0:T(8,128)(2,1)S(1)} %get-tuple-element.52.sel.refs_2_, s32[8,128]{1,0:T(8,128)S(1)} %bitcast.15, ...), custom_call_target="tpu_custom_call" | custom-call | tf_op jit(solution)/shard_map/combine/pallas_call | solution.py:457
  (63 shorter events, 8.1 us)
Async XLA Ops:
  2.1 10.4 %collective-permute-start.2 = (bf16[2,16,1024]{2,1,0:T(8,128)(2,1)S(1)}, bf16[2,16,1024]{2,1,0:T(8,128)(2,1)S(1)}, u32[]{:S(2)}, u32[]{:S(2)}) collective-permute-start(bf16[2,16,1024]{2,1,0:T(8,128)(2,1)S(1)} %get-tuple-element.50), channel_id=1, source_target_pairs={{0,28},{4,24},{8,20},{12,16},{16,12},{20,8},{24,4},{28,0},{1,29},{... | collective-permute-start | bytes 196616 | tf_op jit(solution)/shard_map/ppermute | solution.py:480
  8.2 6.9 %collective-permute-start.1 = (bf16[2,16,1024]{2,1,0:T(8,128)(2,1)S(1)}, bf16[2,16,1024]{2,1,0:T(8,128)(2,1)S(1)}, u32[]{:S(2)}, u32[]{:S(2)}) collective-permute-start(bf16[2,16,1024]{2,1,0:T(8,128)(2,1)S(1)} %get-tuple-element.49), channel_id=1, source_target_pairs={{0,24},{4,28},{8,16},{12,20},{16,8},{20,12},{24,0},{28,4},{1,25},{... | collective-permute-start | bytes 196616 | tf_op jit(solution)/shard_map/ppermute | solution.py:480
  8.4 7.2 %collective-permute-start = (bf16[2,16,1024]{2,1,0:T(8,128)(2,1)S(1)}, bf16[2,16,1024]{2,1,0:T(8,128)(2,1)S(1)}, u32[]{:S(2)}, u32[]{:S(2)}) collective-permute-start(bf16[2,16,1024]{2,1,0:T(8,128)(2,1)S(1)} %get-tuple-element.48), channel_id=1, source_target_pairs={{0,8},{4,12},{8,0},{12,4},{16,24},{20,28},{24,16},{28,20},{1,9},{5... | collective-permute-start | bytes 196616 | tf_op jit(solution)/shard_map/ppermute | solution.py:480
  8.4 9.3 %collective-permute-start.9 = (bf16[2,16,1024]{2,1,0:T(8,128)(2,1)S(1)}, bf16[2,16,1024]{2,1,0:T(8,128)(2,1)S(1)}, u32[]{:S(2)}, u32[]{:S(2)}) collective-permute-start(bf16[2,16,1024]{2,1,0:T(8,128)(2,1)S(1)} %get-tuple-element.59), channel_id=1, source_target_pairs={{0,20},{4,16},{8,28},{12,24},{16,4},{20,0},{24,12},{28,8},{1,21},{... | collective-permute-start | bytes 196616 | tf_op jit(solution)/shard_map/ppermute | solution.py:480
  12.5 6.8 %collective-permute-start.8 = (bf16[2,16,1024]{2,1,0:T(8,128)(2,1)S(1)}, bf16[2,16,1024]{2,1,0:T(8,128)(2,1)S(1)}, u32[]{:S(2)}, u32[]{:S(2)}) collective-permute-start(bf16[2,16,1024]{2,1,0:T(8,128)(2,1)S(1)} %get-tuple-element.58), channel_id=1, source_target_pairs={{0,16},{4,20},{8,24},{12,28},{16,0},{20,4},{24,8},{28,12},{1,17},{... | collective-permute-start | bytes 196616 | tf_op jit(solution)/shard_map/ppermute | solution.py:480
  12.6 6.8 %collective-permute-start.7 = (bf16[2,16,1024]{2,1,0:T(8,128)(2,1)S(1)}, bf16[2,16,1024]{2,1,0:T(8,128)(2,1)S(1)}, u32[]{:S(2)}, u32[]{:S(2)}) collective-permute-start(bf16[2,16,1024]{2,1,0:T(8,128)(2,1)S(1)} %get-tuple-element.57), channel_id=1, source_target_pairs={{0,12},{4,8},{8,4},{12,0},{16,28},{20,24},{24,20},{28,16},{1,13},{... | collective-permute-start | bytes 196616 | tf_op jit(solution)/shard_map/ppermute | solution.py:480
  15.1 4.3 %collective-permute-start.6 = (bf16[2,16,1024]{2,1,0:T(8,128)(2,1)S(1)}, bf16[2,16,1024]{2,1,0:T(8,128)(2,1)S(1)}, u32[]{:S(2)}, u32[]{:S(2)}) collective-permute-start(bf16[2,16,1024]{2,1,0:T(8,128)(2,1)S(1)} %get-tuple-element.56), channel_id=1, source_target_pairs={{0,4},{4,0},{8,12},{12,8},{16,20},{20,16},{24,28},{28,24},{1,5},{5... | collective-permute-start | bytes 196616 | tf_op jit(solution)/shard_map/ppermute | solution.py:480
  15.6 10.4 %collective-permute-start.4 = (bf16[4,2,16,1024]{3,2,1,0:T(8,128)(2,1)S(1)}, bf16[4,2,16,1024]{3,2,1,0:T(8,128)(2,1)S(1)}, u32[]{:S(2)}, u32[]{:S(2)}) collective-permute-start(bf16[4,2,16,1024]{3,2,1,0:T(8,128)(2,1)S(1)} %pad_maximum_fusion.after.x.refs_0_), channel_id=1, source_target_pairs={{0,2},{1,3},{2,0},{3,1},{4,6},{5,7},{6,4},{7,5},{8,10},{9,11},{10,... | collective-permute-start | bytes 786440 | tf_op jit(solution)/shard_map/ppermute | solution.py:473
  19.4 6.7 %collective-permute-start.11 = (bf16[4,16,1024]{2,1,0:T(8,128)(2,1)S(1)}, bf16[4,16,1024]{2,1,0:T(8,128)(2,1)S(1)}, u32[]{:S(2)}, u32[]{:S(2)}) collective-permute-start(bf16[4,16,1024]{2,1,0:T(8,128)(2,1)S(1)} %pad_maximum_fusion.1.refs_4_), channel_id=1, source_target_pairs={{0,2},{1,3},{2,0},{3,1},{4,6},{5,7},{6,4},{7,5},{8,10},{9,11},{10,... | collective-permute-start | bytes 393224 | tf_op jit(solution)/shard_map/ppermute | solution.py:473
  21.0 6.6 %collective-permute-start.14 = (bf16[4,16,1024]{2,1,0:T(8,128)(2,1)S(1)}, bf16[4,16,1024]{2,1,0:T(8,128)(2,1)S(1)}, u32[]{:S(2)}, u32[]{:S(2)}) collective-permute-start(bf16[4,16,1024]{2,1,0:T(8,128)(2,1)S(1)} %pad_maximum_fusion.2.refs_4_), channel_id=1, source_target_pairs={{0,2},{1,3},{2,0},{3,1},{4,6},{5,7},{6,4},{7,5},{8,10},{9,11},{10,... | collective-permute-start | bytes 393224 | tf_op jit(solution)/shard_map/ppermute | solution.py:473
  25.4 2.8 %collective-permute-start.3 = (bf16[4,2,16,1024]{3,2,1,0:T(8,128)(2,1)S(1)}, bf16[4,2,16,1024]{3,2,1,0:T(8,128)(2,1)S(1)}, u32[]{:S(2)}, u32[]{:S(2)}) collective-permute-start(bf16[4,2,16,1024]{3,2,1,0:T(8,128)(2,1)S(1)} %pass_on.2), channel_id=1, source_target_pairs={{0,1},{1,0},{2,3},{3,2},{4,5},{5,4},{6,7},{7,6},{8,9},{9,8},{10,11... | collective-permute-start | bytes 786440 | tf_op jit(solution)/shard_map/ppermute | solution.py:473
  26.0 3.2 %collective-permute-start.5 = (bf16[4,2,16,1024]{3,2,1,0:T(8,128)(2,1)S(1)}, bf16[4,2,16,1024]{3,2,1,0:T(8,128)(2,1)S(1)}, u32[]{:S(2)}, u32[]{:S(2)}) collective-permute-start(bf16[4,2,16,1024]{3,2,1,0:T(8,128)(2,1)S(1)} %collective-permute-done.4.refs_2_), channel_id=1, source_target_pairs={{0,1},{1,0},{2,3},{3,2},{4,5},{5,4},{6,7},{7,6},{8,9},{9,8},{10,11... | collective-permute-start | bytes 786440 | tf_op jit(solution)/shard_map/ppermute | solution.py:473
  31.2 4.5 %collective-permute-start.16 = (bf16[2,128,1024]{2,1,0:T(8,128)(2,1)S(1)}, bf16[2,128,1024]{2,1,0:T(8,128)(2,1)S(1)}, u32[]{:S(2)}, u32[]{:S(2)}) collective-permute-start(bf16[2,128,1024]{2,1,0:T(8,128)(2,1)S(1)} %get-tuple-element.71), channel_id=1, source_target_pairs={{0,1},{1,0},{2,3},{3,2},{4,5},{5,4},{6,7},{7,6},{8,9},{9,8},{10,11... | collective-permute-start | bytes 1572872 | tf_op jit(solution)/shard_map/ppermute | solution.py:473
  35.2 7.5 %collective-permute-start.18 = (bf16[128,1024]{1,0:T(8,128)(2,1)S(1)}, bf16[128,1024]{1,0:T(8,128)(2,1)S(1)}, u32[]{:S(2)}, u32[]{:S(2)}) collective-permute-start(bf16[128,1024]{1,0:T(8,128)(2,1)S(1)} %get-tuple-element.75), channel_id=1, source_target_pairs={{0,1},{1,0},{2,3},{3,2},{4,5},{5,4},{6,7},{7,6},{8,9},{9,8},{10,11... | collective-permute-start | bytes 786440 | tf_op jit(solution)/shard_map/ppermute | solution.py:473
  35.7 7.1 %collective-permute-start.19 = (bf16[80,1024]{1,0:T(8,128)(2,1)S(1)}, bf16[80,1024]{1,0:T(8,128)(2,1)S(1)}, u32[]{:S(2)}, u32[]{:S(2)}) collective-permute-start(bf16[80,1024]{1,0:T(8,128)(2,1)S(1)} %half.3.after), channel_id=1, source_target_pairs={{0,2},{1,3},{2,0},{3,1},{4,6},{5,7},{6,4},{7,5},{8,10},{9,11},{10,... | collective-permute-start | bytes 491528 | tf_op jit(solution)/shard_map/ppermute | solution.py:473
  37.3 10.5 %collective-permute-start.22 = (bf16[96,1024]{1,0:T(8,128)(2,1)S(1)}, bf16[96,1024]{1,0:T(8,128)(2,1)S(1)}, u32[]{:S(2)}, u32[]{:S(2)}) collective-permute-start(bf16[96,1024]{1,0:T(8,128)(2,1)S(1)} %half.4), channel_id=1, source_target_pairs={{0,2},{1,3},{2,0},{3,1},{4,6},{5,7},{6,4},{7,5},{8,10},{9,11},{10,... | collective-permute-start | bytes 589832 | tf_op jit(solution)/shard_map/ppermute | solution.py:473
  41.2 11.1 %collective-permute-start.26 = (bf16[96,1024]{1,0:T(8,128)(2,1)S(1)}, bf16[96,1024]{1,0:T(8,128)(2,1)S(1)}, u32[]{:S(2)}, u32[]{:S(2)}) collective-permute-start(bf16[96,1024]{1,0:T(8,128)(2,1)S(1)} %half.5), channel_id=1, source_target_pairs={{0,2},{1,3},{2,0},{3,1},{4,6},{5,7},{6,4},{7,5},{8,10},{9,11},{10,... | collective-permute-start | bytes 589832 | tf_op jit(solution)/shard_map/ppermute | solution.py:473
  42.9 9.4 %collective-permute-start.20 = (bf16[17,16,128]{2,1,0:T(8,128)(2,1)S(1)}, bf16[17,16,128]{2,1,0:T(8,128)(2,1)S(1)}, u32[]{:S(2)}, u32[]{:S(2)}) collective-permute-start(bf16[17,16,128]{2,1,0:T(8,128)(2,1)S(1)} %get-tuple-element.76.after), channel_id=1, source_target_pairs={{0,28},{4,24},{8,20},{12,16},{16,12},{20,8},{24,4},{28,0},{1,29},{... | collective-permute-start | bytes 208904 | tf_op jit(solution)/shard_map/ppermute | solution.py:480
  46.7 7.3 %collective-permute-start.21 = (bf16[17,16,128]{2,1,0:T(8,128)(2,1)S(1)}, bf16[17,16,128]{2,1,0:T(8,128)(2,1)S(1)}, u32[]{:S(2)}, u32[]{:S(2)}) collective-permute-start(bf16[17,16,128]{2,1,0:T(8,128)(2,1)S(1)} %get-tuple-element.77), channel_id=1, source_target_pairs={{0,24},{4,28},{8,16},{12,20},{16,8},{20,12},{24,0},{28,4},{1,25},{... | collective-permute-start | bytes 208904 | tf_op jit(solution)/shard_map/ppermute | solution.py:480
  47.9 9.8 %collective-permute-start.23 = (bf16[17,16,128]{2,1,0:T(8,128)(2,1)S(1)}, bf16[17,16,128]{2,1,0:T(8,128)(2,1)S(1)}, u32[]{:S(2)}, u32[]{:S(2)}) collective-permute-start(bf16[17,16,128]{2,1,0:T(8,128)(2,1)S(1)} %get-tuple-element.78.after), channel_id=1, source_target_pairs={{0,12},{4,8},{8,4},{12,0},{16,28},{20,24},{24,20},{28,16},{1,13},{... | collective-permute-start | bytes 208904 | tf_op jit(solution)/shard_map/ppermute | solution.py:480
  48.6 9.1 %collective-permute-start.24 = (bf16[17,16,128]{2,1,0:T(8,128)(2,1)S(1)}, bf16[17,16,128]{2,1,0:T(8,128)(2,1)S(1)}, u32[]{:S(2)}, u32[]{:S(2)}) collective-permute-start(bf16[17,16,128]{2,1,0:T(8,128)(2,1)S(1)} %get-tuple-element.79), channel_id=1, source_target_pairs={{0,20},{4,16},{8,28},{12,24},{16,4},{20,0},{24,12},{28,8},{1,21},{... | collective-permute-start | bytes 208904 | tf_op jit(solution)/shard_map/ppermute | solution.py:480
  52.2 5.9 %collective-permute-start.25 = (bf16[17,16,128]{2,1,0:T(8,128)(2,1)S(1)}, bf16[17,16,128]{2,1,0:T(8,128)(2,1)S(1)}, u32[]{:S(2)}, u32[]{:S(2)}) collective-permute-start(bf16[17,16,128]{2,1,0:T(8,128)(2,1)S(1)} %get-tuple-element.80), channel_id=1, source_target_pairs={{0,16},{4,20},{8,24},{12,28},{16,0},{20,4},{24,8},{28,12},{1,17},{... | collective-permute-start | bytes 208904 | tf_op jit(solution)/shard_map/ppermute | solution.py:480
  52.3 5.7 %collective-permute-start.27 = (bf16[17,16,128]{2,1,0:T(8,128)(2,1)S(1)}, bf16[17,16,128]{2,1,0:T(8,128)(2,1)S(1)}, u32[]{:S(2)}, u32[]{:S(2)}) collective-permute-start(bf16[17,16,128]{2,1,0:T(8,128)(2,1)S(1)} %get-tuple-element.82), channel_id=1, source_target_pairs={{0,8},{4,12},{8,0},{12,4},{16,24},{20,28},{24,16},{28,20},{1,9},{5... | collective-permute-start | bytes 208904 | tf_op jit(solution)/shard_map/ppermute | solution.py:480
  54.1 4.3 %collective-permute-start.28 = (bf16[17,16,128]{2,1,0:T(8,128)(2,1)S(1)}, bf16[17,16,128]{2,1,0:T(8,128)(2,1)S(1)}, u32[]{:S(2)}, u32[]{:S(2)}) collective-permute-start(bf16[17,16,128]{2,1,0:T(8,128)(2,1)S(1)} %get-tuple-element.83), channel_id=1, source_target_pairs={{0,4},{4,0},{8,12},{12,8},{16,20},{20,16},{24,28},{28,24},{1,5},{5... | collective-permute-start | bytes 208904 | tf_op jit(solution)/shard_map/ppermute | solution.py:480
  (7 other events, 14.5 us)

commit v7 on v6

--- a/solution.py
+++ b/solution.py
@@ -343,19 +343,22 @@
     sem = refs[8 + 3 * count]
     me = lax.axis_index("tp")
     size = firsts[0].shape[3]
-    values = [g[...] for g in given]
+    values = [g[...].T if which else g[...] for g in given]
+    piece = size // 2
     stores = []
     for i in range(4):
-        part = quarter_of(me, i, size)
         rows = rows_of(firsts[i], rests[i], which)
-        for n in range(count):
-            if which == 0:
-                at = (part, slice(None))
-                made[n][at] = dot(rows, values[n], TN).astype(BF16)
-            else:
-                at = (slice(None), part)
-                made[n][at] = dot(values[n], rows, TN).astype(BF16)
-            stores.append(fetch(made[n].at[at], outs[n].at[at], sem.at[n, i]))
+        for j in range(2):
+            part = pl.ds(pl.multiple_of((me ^ i) * size + j * piece, piece), piece)
+            some = rows[:, j * piece : (j + 1) * piece]
+            for n in range(count):
+                if which == 0:
+                    at = (part, slice(None))
+                    made[n][at] = dot(some, values[n], TN).astype(BF16)
+                else:
+                    at = (slice(None), part)
+                    made[n][at] = dot(values[n], some).astype(BF16)
+                stores.append(fetch(made[n].at[at], outs[n].at[at], sem.at[n, 2 * i + j]))
     for copy in stores:
         copy.wait()
 
@@ -371,7 +374,7 @@
         (array(shape),) * count,
         [aspec()] + [vspec()] * (8 + count),
         hspec(),
-        [pltpu.VMEM(shape, BF16)] * count + [pltpu.SemaphoreType.DMA((count, 4))],
+        [pltpu.VMEM(shape, BF16)] * count + [pltpu.SemaphoreType.DMA((count, 8))],
         mib=20,
         flops=2 * count * rows * ff * 4 * size,
         nbytes=2 * count * ff * 4 * size,

time: 59.6 us -> 59.6 us (level)
  transfers between devices with their start and end apart: 29 -> 29, of which waited for: 8 -> 9; matrix products, arithmetic and copies ran while one was open for 0% -> 0% of each run, Pallas kernels for 22% -> 22%
where the time goes in v7:
time: 59.6 us; the launch traced here: 59.4 us
  starting transfers between devices  35.2 us (59%)
  Pallas kernels  17.3 us (29%)
  waiting for transfers between devices  5.99 us (10%)
  between operations  0.85 us (1%)
    ppermute x14, starting transfers between devices, exchange(): lax.ppermute(part, 'ctx', [(i, i ^ order[p]) for i in range(count)])  24.9 us
    ppermute x15, starting transfers between devices, swap(): return lax.ppermute(x, 'tp', [(i, i ^ flip) for i in range(4)])  10.2 us
    pallas_call x2, Pallas kernels, grads(): call(functools.partial(grads_kernel, which, count), 'grads', (array(shape...  5.12 us
    pallas_call x1, Pallas kernels, load(): call(load_kernel, 'load', tuple((array(w.shape) for w in weights)), [aspe...  3.8 us
    ppermute x14, waiting for transfers between devices, exchange(): lax.ppermute(part, 'ctx', [(i, i ^ order[p]) for i in range(count)])  3.69 us
    ppermute x15, waiting for transfers between devices, swap(): return lax.ppermute(x, 'tp', [(i, i ^ flip) for i in range(4)])  2.29 us
    pallas_call x2, Pallas kernels, input_grad(): call(functools.partial(input_grad_kernel, flips), 'input_grad', (array((r...  2.2 us
    pallas_call x1, Pallas kernels, forward(): call(forward_kernel, 'forward', (array((rows, ff), F32),) * 2 + (array((r...  1.91 us
  transfers between devices with their start and end apart: 29, of which 9 were waited for; matrix products, arithmetic and copies ran while one was open for 0% of the time, Pallas kernels for 22%

profile of v7, /device:TPU:0, one launch (start us, length us, event | category | flops | bytes accessed | tf_op | source)
XLA Modules:
  0.0 59.4 jit_solution(2620550059015494561)
XLA Ops:
  0.6 1.5 %dispatch.1 = (bf16[2,16,1024]{2,1,0:T(8,128)(2,1)S(1)}, bf16[2,16,1024]{2,1,0:T(8,128)(2,1)S(1)}, bf16[2,16,1024]{2,1,0:T(8,128)(2,1)S(1)}, bf16[2,16,1024]{2,1...) custom-call(s32[8,128]{1,0:T(8,128)} %bitcast.14, ...), custom_call_target="tpu_custom_call" | custom-call | tf_op jit(solution)/shard_map/dispatch/pallas_call | solution.py:124
  2.1 6.0 %collective-permute-start.2 = (bf16[2,16,1024]{2,1,0:T(8,128)(2,1)S(1)}, bf16[2,16,1024]{2,1,0:T(8,128)(2,1)S(1)}, u32[]{:S(2)}, u32[]{:S(2)}) collective-permute-start(bf16[2,16,1024]{2,1,0:T(8,128)(2,1)S(1)} %get-tuple-element.50), channel_id=1, source_target_pairs={{0,28},{4,24},{8,20},{12,16},{16,12},{20,8},{24,4},{28,0},{1,29},{... | collective-permute-start | bytes 196616 | tf_op jit(solution)/shard_map/ppermute | solution.py:483
  8.4 4.1 %collective-permute-start.9 = (bf16[2,16,1024]{2,1,0:T(8,128)(2,1)S(1)}, bf16[2,16,1024]{2,1,0:T(8,128)(2,1)S(1)}, u32[]{:S(2)}, u32[]{:S(2)}) collective-permute-start(bf16[2,16,1024]{2,1,0:T(8,128)(2,1)S(1)} %get-tuple-element.59), channel_id=1, source_target_pairs={{0,20},{4,16},{8,28},{12,24},{16,4},{20,0},{24,12},{28,8},{1,21},{... | collective-permute-start | bytes 196616 | tf_op jit(solution)/shard_map/ppermute | solution.py:483
  12.6 1.7 %collective-permute-start.7 = (bf16[2,16,1024]{2,1,0:T(8,128)(2,1)S(1)}, bf16[2,16,1024]{2,1,0:T(8,128)(2,1)S(1)}, u32[]{:S(2)}, u32[]{:S(2)}) collective-permute-start(bf16[2,16,1024]{2,1,0:T(8,128)(2,1)S(1)} %get-tuple-element.57), channel_id=1, source_target_pairs={{0,12},{4,8},{8,4},{12,0},{16,28},{20,24},{24,20},{28,16},{1,13},{... | collective-permute-start | bytes 196616 | tf_op jit(solution)/shard_map/ppermute | solution.py:483
  14.2 0.8 %collective-permute-done.1 = bf16[2,16,1024]{2,1,0:T(8,128)(2,1)S(1)} collective-permute-done((bf16[2,16,1024]{2,1,0:T(8,128)(2,1)S(1)}, bf16[2,16,1024]{2,1,0:T(8,128)(2,1)S(1)}, u32[]{:S(2)}, u32[]{:S(2)}) %collective-permute-start.1) | collective-permute-done | bytes 65568 | tf_op jit(solution)/shard_map/ppermute | solution.py:483
  15.6 1.6 %collective-permute-start.4 = (bf16[4,2,16,1024]{3,2,1,0:T(8,128)(2,1)S(1)}, bf16[4,2,16,1024]{3,2,1,0:T(8,128)(2,1)S(1)}, u32[]{:S(2)}, u32[]{:S(2)}) collective-permute-start(bf16[4,2,16,1024]{3,2,1,0:T(8,128)(2,1)S(1)} %pad_maximum_fusion.after.x.refs_0_), channel_id=1, source_target_pairs={{0,2},{1,3},{2,0},{3,1},{4,6},{5,7},{6,4},{7,5},{8,10},{9,11},{10,... | collective-permute-start | bytes 786440 | tf_op jit(solution)/shard_map/ppermute | solution.py:476
  17.7 1.7 %collective-permute-done.8 = bf16[2,16,1024]{2,1,0:T(8,128)(2,1)S(1)} collective-permute-done((bf16[2,16,1024]{2,1,0:T(8,128)(2,1)S(1)}, bf16[2,16,1024]{2,1,0:T(8,128)(2,1)S(1)}, u32[]{:S(2)}, u32[]{:S(2)}) %collective-permute-start.8) | collective-permute-done | bytes 65568 | tf_op jit(solution)/shard_map/ppermute | solution.py:483
  19.4 1.6 %collective-permute-start.11 = (bf16[4,16,1024]{2,1,0:T(8,128)(2,1)S(1)}, bf16[4,16,1024]{2,1,0:T(8,128)(2,1)S(1)}, u32[]{:S(2)}, u32[]{:S(2)}) collective-permute-start(bf16[4,16,1024]{2,1,0:T(8,128)(2,1)S(1)} %pad_maximum_fusion.1.refs_4_), channel_id=1, source_target_pairs={{0,2},{1,3},{2,0},{3,1},{4,6},{5,7},{6,4},{7,5},{8,10},{9,11},{10,... | collective-permute-start | bytes 393224 | tf_op jit(solution)/shard_map/ppermute | solution.py:476
  21.6 3.8 %load.1 = (bf16[4096,384]{1,0:T(8,128)(2,1)S(1)}, bf16[4096,384]{1,0:T(8,128)(2,1)S(1)}, bf16[384,4096]{1,0:T(8,128)(2,1)S(1)}) custom-call(bf16[4,2,16,1024]{3,2,1,0:T(8,128)(2,1)S(1)} %pad_maximum_fusion.after.x.refs_0_, bf16[4096,384]{1,0:T(8,128)(2,1)} %bitcast.21, bf16[4096,384]{1,0:T(8,128)(2,1)} %bitcast.22, bf16[384,4096]{1,0:T(8,128)(2,1)} %bitcast.23), custom_call_target="tpu_custom_call" | custom-call | tf_op jit(solution)/shard_map/load/pallas_call | solution.py:180
  26.5 1.1 %collective-permute-done.14.x.refs_6_ = bf16[4,16,1024]{2,1,0:T(8,128)(2,1)S(1)} collective-permute-done((bf16[4,16,1024]{2,1,0:T(8,128)(2,1)S(1)}, bf16[4,16,1024]{2,1,0:T(8,128)(2,1)S(1)}, u32[]{:S(2)}, u32[]{:S(2)}) %collective-permute-start.14) | collective-permute-done | bytes 131104 | tf_op jit(solution)/shard_map/ppermute | solution.py:476
  29.3 1.9 %forward.1 = (f32[128,384]{1,0:T(8,128)S(1)}, f32[128,384]{1,0:T(8,128)S(1)}, bf16[128,384]{1,0:T(8,128)(2,1)S(1)}, bf16[2,128,1024]{2,1,0:T(8,128)(2,1)S(1)}, f...) custom-call(bf16[4,16,1024]{2,1,0:T(8,128)(2,1)S(1)} %collective-permute-done.12.after.refs_7_, ...), custom_call_target="tpu_custom_call" | custom-call | tf_op jit(solution)/shard_map/forward/pallas_call | solution.py:235
  31.6 1.2 %hidden_grad.1 = (bf16[128,384]{1,0:T(8,128)(2,1)S(1)}, bf16[128,384]{1,0:T(8,128)(2,1)S(1)}, f32[8,128]{1,0:T(8,128)S(1)}) custom-call(bf16[4,2,16,1024]{3,2,1,0:T(8,128)(2,1)S(1)} %pad_maximum_fusion.after.x.refs_0_, bf16[4,2,16,1024]{3,2,1,0:T(8,128)(2,1)S(1)} %collective-permute-done.3.refs_1_, ...), custom_call_target="tpu_custom_call" | custom-call | tf_op jit(solution)/shard_map/hidden_grad/pallas_call | solution.py:267
  32.8 1.1 %input_grad.2 = (bf16[144,1024]{1,0:T(8,128)(2,1)S(1)}, f32[128,1024]{1,0:T(8,128)S(1)}) custom-call(f32[8,128]{1,0:T(8,128)S(1)} %get-tuple-element.65.after.dots, f32[8,128]{1,0:T(8,128)S(1)} %get-tuple-element.65.after.dots, bf16[128,384]{1,0:T(8,128)(2,1)S(1)} %get-tuple-element.66.dact.refs_8_, bf16[128,384]{1,0:T(8,128)(2,1)S(1)} %get-tuple-element.67.dlin.refs_9_, ...), custom_call_target="tpu_custom_call" | custom-call | tf_op jit(solution)/shard_map/input_grad/pallas_call | solution.py:305
  34.1 1.1 %input_grad.3 = (bf16[128,1024]{1,0:T(8,128)(2,1)S(1)}, f32[128,1024]{1,0:T(8,128)S(1)}) custom-call(bf16[144,1024]{1,0:T(8,128)(2,1)S(1)} %get-tuple-element.68.after, f32[8,128]{1,0:T(8,128)S(1)} %get-tuple-element.65.after.dots, bf16[128,384]{1,0:T(8,128)(2,1)S(1)} %get-tuple-element.66.dact.refs_8_, bf16[128,384]{1,0:T(8,128)(2,1)S(1)} %get-tuple-element.67.dlin.refs_9_, ...), custom_call_target="tpu_custom_call" | custom-call | tf_op jit(solution)/shard_map/input_grad/pallas_call | solution.py:305
  35.7 1.6 %collective-permute-start.19 = (bf16[80,1024]{1,0:T(8,128)(2,1)S(1)}, bf16[80,1024]{1,0:T(8,128)(2,1)S(1)}, u32[]{:S(2)}, u32[]{:S(2)}) collective-permute-start(bf16[80,1024]{1,0:T(8,128)(2,1)S(1)} %half.3.after), channel_id=1, source_target_pairs={{0,2},{1,3},{2,0},{3,1},{4,6},{5,7},{6,4},{7,5},{8,10},{9,11},{10,... | collective-permute-start | bytes 491528 | tf_op jit(solution)/shard_map/ppermute | solution.py:476
  37.9 3.1 %grads.2 = (bf16[4096,384]{1,0:T(8,128)(2,1)}, bf16[4096,384]{1,0:T(8,128)(2,1)}) custom-call(bf16[80,1024]{1,0:T(8,128)(2,1)S(1)} %half.3.after, bf16[4,2,16,1024]{3,2,1,0:T(8,128)(2,1)S(1)} %pad_maximum_fusion.after.x.refs_0_, bf16[4,2,16,1024]{3,2,1,0:T(8,128)(2,1)S(1)} %collective-permute-done.3.refs_1_, ...), custom_call_target="tpu_custom_call" | custom-call | flops 805306368 | bytes 6291456 | tf_op jit(solution)/shard_map/grads/pallas_call | solution.py:371
  41.0 1.6 %collective-permute-start.26 = (bf16[96,1024]{1,0:T(8,128)(2,1)S(1)}, bf16[96,1024]{1,0:T(8,128)(2,1)S(1)}, u32[]{:S(2)}, u32[]{:S(2)}) collective-permute-start(bf16[96,1024]{1,0:T(8,128)(2,1)S(1)} %half.5), channel_id=1, source_target_pairs={{0,2},{1,3},{2,0},{3,1},{4,6},{5,7},{6,4},{7,5},{8,10},{9,11},{10,... | collective-permute-start | bytes 589832 | tf_op jit(solution)/shard_map/ppermute | solution.py:476
  42.9 3.8 %collective-permute-start.20 = (bf16[17,16,128]{2,1,0:T(8,128)(2,1)S(1)}, bf16[17,16,128]{2,1,0:T(8,128)(2,1)S(1)}, u32[]{:S(2)}, u32[]{:S(2)}) collective-permute-start(bf16[17,16,128]{2,1,0:T(8,128)(2,1)S(1)} %get-tuple-element.76.after), channel_id=1, source_target_pairs={{0,28},{4,24},{8,20},{12,16},{16,12},{20,8},{24,4},{28,0},{1,29},{... | collective-permute-start | bytes 208904 | tf_op jit(solution)/shard_map/ppermute | solution.py:483
  46.7 1.1 %collective-permute-start.21 = (bf16[17,16,128]{2,1,0:T(8,128)(2,1)S(1)}, bf16[17,16,128]{2,1,0:T(8,128)(2,1)S(1)}, u32[]{:S(2)}, u32[]{:S(2)}) collective-permute-start(bf16[17,16,128]{2,1,0:T(8,128)(2,1)S(1)} %get-tuple-element.77), channel_id=1, source_target_pairs={{0,24},{4,28},{8,16},{12,20},{16,8},{20,12},{24,0},{28,4},{1,25},{... | collective-permute-start | bytes 208904 | tf_op jit(solution)/shard_map/ppermute | solution.py:483
  48.6 3.6 %collective-permute-start.24 = (bf16[17,16,128]{2,1,0:T(8,128)(2,1)S(1)}, bf16[17,16,128]{2,1,0:T(8,128)(2,1)S(1)}, u32[]{:S(2)}, u32[]{:S(2)}) collective-permute-start(bf16[17,16,128]{2,1,0:T(8,128)(2,1)S(1)} %get-tuple-element.79), channel_id=1, source_target_pairs={{0,20},{4,16},{8,28},{12,24},{16,4},{20,0},{24,12},{28,8},{1,21},{... | collective-permute-start | bytes 208904 | tf_op jit(solution)/shard_map/ppermute | solution.py:483
  52.3 1.7 %collective-permute-start.27 = (bf16[17,16,128]{2,1,0:T(8,128)(2,1)S(1)}, bf16[17,16,128]{2,1,0:T(8,128)(2,1)S(1)}, u32[]{:S(2)}, u32[]{:S(2)}) collective-permute-start(bf16[17,16,128]{2,1,0:T(8,128)(2,1)S(1)} %get-tuple-element.82), channel_id=1, source_target_pairs={{0,8},{4,12},{8,0},{12,4},{16,24},{20,28},{24,16},{28,20},{1,9},{5... | collective-permute-start | bytes 208904 | tf_op jit(solution)/shard_map/ppermute | solution.py:483
  54.1 1.4 %collective-permute-start.28 = (bf16[17,16,128]{2,1,0:T(8,128)(2,1)S(1)}, bf16[17,16,128]{2,1,0:T(8,128)(2,1)S(1)}, u32[]{:S(2)}, u32[]{:S(2)}) collective-permute-start(bf16[17,16,128]{2,1,0:T(8,128)(2,1)S(1)} %get-tuple-element.83), channel_id=1, source_target_pairs={{0,4},{4,0},{8,12},{12,8},{16,20},{20,16},{24,28},{28,24},{1,5},{5... | collective-permute-start | bytes 208904 | tf_op jit(solution)/shard_map/ppermute | solution.py:483
  55.6 2.0 %grads.3 = bf16[384,4096]{1,0:T(8,128)(2,1)} custom-call(bf16[80,1024]{1,0:T(8,128)(2,1)S(1)} %half.3.after, bf16[4,2,16,1024]{3,2,1,0:T(8,128)(2,1)S(1)} %pad_maximum_fusion.after.x.refs_0_, bf16[4,2,16,1024]{3,2,1,0:T(8,128)(2,1)S(1)} %collective-permute-done.3.refs_1_, bf16[4,2,16,1024]{3,2,1,0:T(8,128)(2,1)S(1)} %collective-permute-done.4.refs_2_, ...), custom_call_target="tpu_custom_call" | custom-call | flops 402653184 | bytes 3145728 | tf_op jit(solution)/shard_map/grads/pallas_call | solution.py:371
  58.4 1.0 %combine.1 = (bf16[128,1024]{1,0:T(8,128)(2,1)}, bf16[128,1024]{1,0:T(8,128)(2,1)}, f32[8,128]{1,0:T(8,128)}) custom-call(bf16[128,256]{1,0:T(8,128)(2,1)S(1)} %get-tuple-element.54.refs_0_, bf16[128,128]{1,0:T(8,128)(2,1)S(1)} %get-tuple-element.55.refs_1_, bf16[128,128]{1,0:T(8,128)(2,1)S(1)} %get-tuple-element.52.sel.refs_2_, s32[8,128]{1,0:T(8,128)S(1)} %bitcast.15, ...), custom_call_target="tpu_custom_call" | custom-call | tf_op jit(solution)/shard_map/combine/pallas_call | solution.py:460
  (63 shorter events, 8.3 us)
Async XLA Ops:
  2.1 10.4 %collective-permute-start.2 = (bf16[2,16,1024]{2,1,0:T(8,128)(2,1)S(1)}, bf16[2,16,1024]{2,1,0:T(8,128)(2,1)S(1)}, u32[]{:S(2)}, u32[]{:S(2)}) collective-permute-start(bf16[2,16,1024]{2,1,0:T(8,128)(2,1)S(1)} %get-tuple-element.50), channel_id=1, source_target_pairs={{0,28},{4,24},{8,20},{12,16},{16,12},{20,8},{24,4},{28,0},{1,29},{... | collective-permute-start | bytes 196616 | tf_op jit(solution)/shard_map/ppermute | solution.py:483
  8.2 6.9 %collective-permute-start.1 = (bf16[2,16,1024]{2,1,0:T(8,128)(2,1)S(1)}, bf16[2,16,1024]{2,1,0:T(8,128)(2,1)S(1)}, u32[]{:S(2)}, u32[]{:S(2)}) collective-permute-start(bf16[2,16,1024]{2,1,0:T(8,128)(2,1)S(1)} %get-tuple-element.49), channel_id=1, source_target_pairs={{0,24},{4,28},{8,16},{12,20},{16,8},{20,12},{24,0},{28,4},{1,25},{... | collective-permute-start | bytes 196616 | tf_op jit(solution)/shard_map/ppermute | solution.py:483
  8.4 7.2 %collective-permute-start = (bf16[2,16,1024]{2,1,0:T(8,128)(2,1)S(1)}, bf16[2,16,1024]{2,1,0:T(8,128)(2,1)S(1)}, u32[]{:S(2)}, u32[]{:S(2)}) collective-permute-start(bf16[2,16,1024]{2,1,0:T(8,128)(2,1)S(1)} %get-tuple-element.48), channel_id=1, source_target_pairs={{0,8},{4,12},{8,0},{12,4},{16,24},{20,28},{24,16},{28,20},{1,9},{5... | collective-permute-start | bytes 196616 | tf_op jit(solution)/shard_map/ppermute | solution.py:483
  8.4 9.3 %collective-permute-start.9 = (bf16[2,16,1024]{2,1,0:T(8,128)(2,1)S(1)}, bf16[2,16,1024]{2,1,0:T(8,128)(2,1)S(1)}, u32[]{:S(2)}, u32[]{:S(2)}) collective-permute-start(bf16[2,16,1024]{2,1,0:T(8,128)(2,1)S(1)} %get-tuple-element.59), channel_id=1, source_target_pairs={{0,20},{4,16},{8,28},{12,24},{16,4},{20,0},{24,12},{28,8},{1,21},{... | collective-permute-start | bytes 196616 | tf_op jit(solution)/shard_map/ppermute | solution.py:483
  12.5 6.8 %collective-permute-start.8 = (bf16[2,16,1024]{2,1,0:T(8,128)(2,1)S(1)}, bf16[2,16,1024]{2,1,0:T(8,128)(2,1)S(1)}, u32[]{:S(2)}, u32[]{:S(2)}) collective-permute-start(bf16[2,16,1024]{2,1,0:T(8,128)(2,1)S(1)} %get-tuple-element.58), channel_id=1, source_target_pairs={{0,16},{4,20},{8,24},{12,28},{16,0},{20,4},{24,8},{28,12},{1,17},{... | collective-permute-start | bytes 196616 | tf_op jit(solution)/shard_map/ppermute | solution.py:483
  12.6 6.8 %collective-permute-start.7 = (bf16[2,16,1024]{2,1,0:T(8,128)(2,1)S(1)}, bf16[2,16,1024]{2,1,0:T(8,128)(2,1)S(1)}, u32[]{:S(2)}, u32[]{:S(2)}) collective-permute-start(bf16[2,16,1024]{2,1,0:T(8,128)(2,1)S(1)} %get-tuple-element.57), channel_id=1, source_target_pairs={{0,12},{4,8},{8,4},{12,0},{16,28},{20,24},{24,20},{28,16},{1,13},{... | collective-permute-start | bytes 196616 | tf_op jit(solution)/shard_map/ppermute | solution.py:483
  15.1 4.3 %collective-permute-start.6 = (bf16[2,16,1024]{2,1,0:T(8,128)(2,1)S(1)}, bf16[2,16,1024]{2,1,0:T(8,128)(2,1)S(1)}, u32[]{:S(2)}, u32[]{:S(2)}) collective-permute-start(bf16[2,16,1024]{2,1,0:T(8,128)(2,1)S(1)} %get-tuple-element.56), channel_id=1, source_target_pairs={{0,4},{4,0},{8,12},{12,8},{16,20},{20,16},{24,28},{28,24},{1,5},{5... | collective-permute-start | bytes 196616 | tf_op jit(solution)/shard_map/ppermute | solution.py:483
  15.6 10.4 %collective-permute-start.4 = (bf16[4,2,16,1024]{3,2,1,0:T(8,128)(2,1)S(1)}, bf16[4,2,16,1024]{3,2,1,0:T(8,128)(2,1)S(1)}, u32[]{:S(2)}, u32[]{:S(2)}) collective-permute-start(bf16[4,2,16,1024]{3,2,1,0:T(8,128)(2,1)S(1)} %pad_maximum_fusion.after.x.refs_0_), channel_id=1, source_target_pairs={{0,2},{1,3},{2,0},{3,1},{4,6},{5,7},{6,4},{7,5},{8,10},{9,11},{10,... | collective-permute-start | bytes 786440 | tf_op jit(solution)/shard_map/ppermute | solution.py:476
  19.4 6.7 %collective-permute-start.11 = (bf16[4,16,1024]{2,1,0:T(8,128)(2,1)S(1)}, bf16[4,16,1024]{2,1,0:T(8,128)(2,1)S(1)}, u32[]{:S(2)}, u32[]{:S(2)}) collective-permute-start(bf16[4,16,1024]{2,1,0:T(8,128)(2,1)S(1)} %pad_maximum_fusion.1.refs_4_), channel_id=1, source_target_pairs={{0,2},{1,3},{2,0},{3,1},{4,6},{5,7},{6,4},{7,5},{8,10},{9,11},{10,... | collective-permute-start | bytes 393224 | tf_op jit(solution)/shard_map/ppermute | solution.py:476
  21.0 6.6 %collective-permute-start.14 = (bf16[4,16,1024]{2,1,0:T(8,128)(2,1)S(1)}, bf16[4,16,1024]{2,1,0:T(8,128)(2,1)S(1)}, u32[]{:S(2)}, u32[]{:S(2)}) collective-permute-start(bf16[4,16,1024]{2,1,0:T(8,128)(2,1)S(1)} %pad_maximum_fusion.2.refs_4_), channel_id=1, source_target_pairs={{0,2},{1,3},{2,0},{3,1},{4,6},{5,7},{6,4},{7,5},{8,10},{9,11},{10,... | collective-permute-start | bytes 393224 | tf_op jit(solution)/shard_map/ppermute | solution.py:476
  25.4 2.8 %collective-permute-start.3 = (bf16[4,2,16,1024]{3,2,1,0:T(8,128)(2,1)S(1)}, bf16[4,2,16,1024]{3,2,1,0:T(8,128)(2,1)S(1)}, u32[]{:S(2)}, u32[]{:S(2)}) collective-permute-start(bf16[4,2,16,1024]{3,2,1,0:T(8,128)(2,1)S(1)} %pass_on.2), channel_id=1, source_target_pairs={{0,1},{1,0},{2,3},{3,2},{4,5},{5,4},{6,7},{7,6},{8,9},{9,8},{10,11... | collective-permute-start | bytes 786440 | tf_op jit(solution)/shard_map/ppermute | solution.py:476
  26.0 3.2 %collective-permute-start.5 = (bf16[4,2,16,1024]{3,2,1,0:T(8,128)(2,1)S(1)}, bf16[4,2,16,1024]{3,2,1,0:T(8,128)(2,1)S(1)}, u32[]{:S(2)}, u32[]{:S(2)}) collective-permute-start(bf16[4,2,16,1024]{3,2,1,0:T(8,128)(2,1)S(1)} %collective-permute-done.4.refs_2_), channel_id=1, source_target_pairs={{0,1},{1,0},{2,3},{3,2},{4,5},{5,4},{6,7},{7,6},{8,9},{9,8},{10,11... | collective-permute-start | bytes 786440 | tf_op jit(solution)/shard_map/ppermute | solution.py:476
  31.2 4.5 %collective-permute-start.16 = (bf16[2,128,1024]{2,1,0:T(8,128)(2,1)S(1)}, bf16[2,128,1024]{2,1,0:T(8,128)(2,1)S(1)}, u32[]{:S(2)}, u32[]{:S(2)}) collective-permute-start(bf16[2,128,1024]{2,1,0:T(8,128)(2,1)S(1)} %get-tuple-element.71), channel_id=1, source_target_pairs={{0,1},{1,0},{2,3},{3,2},{4,5},{5,4},{6,7},{7,6},{8,9},{9,8},{10,11... | collective-permute-start | bytes 1572872 | tf_op jit(solution)/shard_map/ppermute | solution.py:476
  35.2 7.4 %collective-permute-start.18 = (bf16[128,1024]{1,0:T(8,128)(2,1)S(1)}, bf16[128,1024]{1,0:T(8,128)(2,1)S(1)}, u32[]{:S(2)}, u32[]{:S(2)}) collective-permute-start(bf16[128,1024]{1,0:T(8,128)(2,1)S(1)} %get-tuple-element.75), channel_id=1, source_target_pairs={{0,1},{1,0},{2,3},{3,2},{4,5},{5,4},{6,7},{7,6},{8,9},{9,8},{10,11... | collective-permute-start | bytes 786440 | tf_op jit(solution)/shard_map/ppermute | solution.py:476
  35.7 7.1 %collective-permute-start.19 = (bf16[80,1024]{1,0:T(8,128)(2,1)S(1)}, bf16[80,1024]{1,0:T(8,128)(2,1)S(1)}, u32[]{:S(2)}, u32[]{:S(2)}) collective-permute-start(bf16[80,1024]{1,0:T(8,128)(2,1)S(1)} %half.3.after), channel_id=1, source_target_pairs={{0,2},{1,3},{2,0},{3,1},{4,6},{5,7},{6,4},{7,5},{8,10},{9,11},{10,... | collective-permute-start | bytes 491528 | tf_op jit(solution)/shard_map/ppermute | solution.py:476
  37.3 10.5 %collective-permute-start.22 = (bf16[96,1024]{1,0:T(8,128)(2,1)S(1)}, bf16[96,1024]{1,0:T(8,128)(2,1)S(1)}, u32[]{:S(2)}, u32[]{:S(2)}) collective-permute-start(bf16[96,1024]{1,0:T(8,128)(2,1)S(1)} %half.4), channel_id=1, source_target_pairs={{0,2},{1,3},{2,0},{3,1},{4,6},{5,7},{6,4},{7,5},{8,10},{9,11},{10,... | collective-permute-start | bytes 589832 | tf_op jit(solution)/shard_map/ppermute | solution.py:476
  41.0 11.2 %collective-permute-start.26 = (bf16[96,1024]{1,0:T(8,128)(2,1)S(1)}, bf16[96,1024]{1,0:T(8,128)(2,1)S(1)}, u32[]{:S(2)}, u32[]{:S(2)}) collective-permute-start(bf16[96,1024]{1,0:T(8,128)(2,1)S(1)} %half.5), channel_id=1, source_target_pairs={{0,2},{1,3},{2,0},{3,1},{4,6},{5,7},{6,4},{7,5},{8,10},{9,11},{10,... | collective-permute-start | bytes 589832 | tf_op jit(solution)/shard_map/ppermute | solution.py:476
  42.9 9.4 %collective-permute-start.20 = (bf16[17,16,128]{2,1,0:T(8,128)(2,1)S(1)}, bf16[17,16,128]{2,1,0:T(8,128)(2,1)S(1)}, u32[]{:S(2)}, u32[]{:S(2)}) collective-permute-start(bf16[17,16,128]{2,1,0:T(8,128)(2,1)S(1)} %get-tuple-element.76.after), channel_id=1, source_target_pairs={{0,28},{4,24},{8,20},{12,16},{16,12},{20,8},{24,4},{28,0},{1,29},{... | collective-permute-start | bytes 208904 | tf_op jit(solution)/shard_map/ppermute | solution.py:483
  46.7 7.3 %collective-permute-start.21 = (bf16[17,16,128]{2,1,0:T(8,128)(2,1)S(1)}, bf16[17,16,128]{2,1,0:T(8,128)(2,1)S(1)}, u32[]{:S(2)}, u32[]{:S(2)}) collective-permute-start(bf16[17,16,128]{2,1,0:T(8,128)(2,1)S(1)} %get-tuple-element.77), channel_id=1, source_target_pairs={{0,24},{4,28},{8,16},{12,20},{16,8},{20,12},{24,0},{28,4},{1,25},{... | collective-permute-start | bytes 208904 | tf_op jit(solution)/shard_map/ppermute | solution.py:483
  47.9 9.7 %collective-permute-start.23 = (bf16[17,16,128]{2,1,0:T(8,128)(2,1)S(1)}, bf16[17,16,128]{2,1,0:T(8,128)(2,1)S(1)}, u32[]{:S(2)}, u32[]{:S(2)}) collective-permute-start(bf16[17,16,128]{2,1,0:T(8,128)(2,1)S(1)} %get-tuple-element.78.after), channel_id=1, source_target_pairs={{0,12},{4,8},{8,4},{12,0},{16,28},{20,24},{24,20},{28,16},{1,13},{... | collective-permute-start | bytes 208904 | tf_op jit(solution)/shard_map/ppermute | solution.py:483
  48.6 9.1 %collective-permute-start.24 = (bf16[17,16,128]{2,1,0:T(8,128)(2,1)S(1)}, bf16[17,16,128]{2,1,0:T(8,128)(2,1)S(1)}, u32[]{:S(2)}, u32[]{:S(2)}) collective-permute-start(bf16[17,16,128]{2,1,0:T(8,128)(2,1)S(1)} %get-tuple-element.79), channel_id=1, source_target_pairs={{0,20},{4,16},{8,28},{12,24},{16,4},{20,0},{24,12},{28,8},{1,21},{... | collective-permute-start | bytes 208904 | tf_op jit(solution)/shard_map/ppermute | solution.py:483
  52.2 5.8 %collective-permute-start.25 = (bf16[17,16,128]{2,1,0:T(8,128)(2,1)S(1)}, bf16[17,16,128]{2,1,0:T(8,128)(2,1)S(1)}, u32[]{:S(2)}, u32[]{:S(2)}) collective-permute-start(bf16[17,16,128]{2,1,0:T(8,128)(2,1)S(1)} %get-tuple-element.80), channel_id=1, source_target_pairs={{0,16},{4,20},{8,24},{12,28},{16,0},{20,4},{24,8},{28,12},{1,17},{... | collective-permute-start | bytes 208904 | tf_op jit(solution)/shard_map/ppermute | solution.py:483
  52.3 5.7 %collective-permute-start.27 = (bf16[17,16,128]{2,1,0:T(8,128)(2,1)S(1)}, bf16[17,16,128]{2,1,0:T(8,128)(2,1)S(1)}, u32[]{:S(2)}, u32[]{:S(2)}) collective-permute-start(bf16[17,16,128]{2,1,0:T(8,128)(2,1)S(1)} %get-tuple-element.82), channel_id=1, source_target_pairs={{0,8},{4,12},{8,0},{12,4},{16,24},{20,28},{24,16},{28,20},{1,9},{5... | collective-permute-start | bytes 208904 | tf_op jit(solution)/shard_map/ppermute | solution.py:483
  54.1 4.3 %collective-permute-start.28 = (bf16[17,16,128]{2,1,0:T(8,128)(2,1)S(1)}, bf16[17,16,128]{2,1,0:T(8,128)(2,1)S(1)}, u32[]{:S(2)}, u32[]{:S(2)}) collective-permute-start(bf16[17,16,128]{2,1,0:T(8,128)(2,1)S(1)} %get-tuple-element.83), channel_id=1, source_target_pairs={{0,4},{4,0},{8,12},{12,8},{16,20},{20,16},{24,28},{28,24},{1,5},{5... | collective-permute-start | bytes 208904 | tf_op jit(solution)/shard_map/ppermute | solution.py:483
  (7 other events, 14.5 us)
